TPU v7x, 512 devices: a whole 4x8x8 slice. The times are simulated.
512 devices in a mesh: dp: 8 (over z), dap: 64 (over y, x, core).
Axes of the slice: x: 4, y: 8, z: 8, core: 2. Of those that a mesh axis runs over, the one named last changes fastest.
Arguments:
- pair_map: bfloat16 [4096, 512, 128], P(('dp', 'dap')), parts along dimension 0, may hold values from -3 to 3
- atom_feats: bfloat16 [49152, 128], P(('dp', 'dap')), parts along dimension 0, may hold values from -6 to 6
- atom_token: int32 [49152], P(('dp', 'dap')), parts along dimension 0, may hold values from 0 to 511, as said below
- atom_weight: bfloat16 [128, 384], replicated, may hold values from -0.5 to 0.5
- left_weight: bfloat16 [384, 128], replicated, may hold values from -0.109375 to 0.109375
- right_weight: bfloat16 [384, 128], replicated, may hold values from -0.109375 to 0.109375
- tri_proj: bfloat16 [2, 128, 512], replicated, may hold values from -0.5 to 0.5
- tri_gate: bfloat16 [2, 128, 128], replicated, may hold values from -1 to 1
- tri_out: bfloat16 [2, 128, 128], replicated, may hold values from -0.5 to 0.5
- tri_gains: float32 [2, 2, 128], replicated, may hold values from 0.1 to 1.9
Outputs:
- token_single: bfloat16 [4096, 384], P(('dp', 'dap')), parts along dimension 0
- pair_out: bfloat16 [4096, 512, 128], P(('dp', 'dap')), parts along dimension 0
There are 8 independent parts, one for each index of `dp`. A program takes and returns all parts, laid end to end along the dimension named above; an argument that names none is the same for every part. Nothing has to cross between parts.
Inputs may be any that keep to these rules, and one draw needn't show every extreme that they name: Within each aligned block of 32 atoms atom_token never falls; the blocks are pieces of one crop's token list in order, stored on devices in a drawn order; every token of the crop has at least one atom; the atoms of one device belong to at most min(96, 512) distinct tokens, and in every draw the atoms of some device belong to exactly that many.
All inputs are finite; a program needn't handle non-finite values.
Results may differ from a plain program's by a relative error of at most 0.02.
Values may be sent and summed in bfloat16 or wider, within the bound.
No kernel may reach another device: no remote copies, remote signals or barrier semaphores. Data moves between devices by JAX's collectives and lax.ppermute only.
A program may use at most 64 MiB of HBM per device.

v0:
```python
import jax
import jax.numpy as jnp
from jax import lax
from jax.sharding import PartitionSpec as P

EPS = 1e-05


def layer_norm(values, gain_vec, norm_axis):
    average = jnp.mean(values, axis=norm_axis, keepdims=True)
    centred = values - average
    variance = jnp.mean(centred * centred, axis=norm_axis, keepdims=True)
    return centred * lax.rsqrt(variance + EPS) * gain_vec


def contract(left_part, right_part, incoming):
    if incoming:
        result = jnp.einsum(
            "gcki,gckj->gcij", left_part, right_part, preferred_element_type=jnp.float32
        )
    else:
        result = jnp.einsum(
            "gcik,gcjk->gcij", left_part, right_part, preferred_element_type=jnp.float32
        )
    return result.astype(jnp.bfloat16)


def triangle(pair_rows, proj, gate, out, gains, incoming):
    row_count, length, channels = pair_rows.shape
    groups = lax.axis_size("dap")
    normed = layer_norm(pair_rows.astype(jnp.float32), gains[0], 2).astype(jnp.bfloat16)
    stacked = jnp.einsum(
        "ijc,cqd->qdij",
        normed,
        proj.reshape(channels, 4, channels),
        preferred_element_type=jnp.float32,
    )
    left_ops = (jax.nn.sigmoid(stacked[0]) * stacked[1]).astype(jnp.bfloat16)
    right_ops = (jax.nn.sigmoid(stacked[2]) * stacked[3]).astype(jnp.bfloat16)
    left_ops = left_ops.reshape(groups, channels // groups, row_count, length)
    right_ops = right_ops.reshape(groups, channels // groups, row_count, length)
    exchanged = (
        lax.all_to_all(left_ops, "dap", split_axis=0, concat_axis=2, tiled=True),
        lax.all_to_all(right_ops, "dap", split_axis=0, concat_axis=2, tiled=True),
    )
    product = lax.all_to_all(
        contract(exchanged[0], exchanged[1], incoming),
        "dap",
        split_axis=2,
        concat_axis=0,
        tiled=True,
    )
    product = product.reshape(channels, row_count, length)
    normed_out = layer_norm(product.astype(jnp.float32), gains[1][:, None, None], 0).astype(
        jnp.bfloat16
    )
    update = jnp.einsum("cij,cd->ijd", normed_out, out, preferred_element_type=jnp.float32)
    gating = jax.nn.sigmoid(
        jnp.einsum("ijc,cd->ijd", normed, gate, preferred_element_type=jnp.float32)
    )
    return (pair_rows.astype(jnp.float32) + gating * update).astype(jnp.bfloat16)


def local(
    pair_map,
    atom_feats,
    atom_token,
    atom_weight,
    left_weight,
    right_weight,
    tri_proj,
    tri_gate,
    tri_out,
    tri_gains,
):
    total_tokens = pair_map.shape[1]
    hidden = jax.nn.relu(
        jnp.dot(atom_feats, atom_weight, preferred_element_type=jnp.float32)
    ).astype(jnp.bfloat16)
    selector = jnp.arange(total_tokens, dtype=jnp.int32)[:, None] == atom_token[None, :]
    partial_sums = jnp.dot(
        selector.astype(jnp.bfloat16), hidden, preferred_element_type=jnp.float32
    )
    partial_counts = jnp.sum(selector.astype(jnp.float32), axis=1)
    sums, counts = (
        lax.psum_scatter(partial_sums, "dap", scatter_dimension=0, tiled=True),
        lax.psum_scatter(partial_counts, "dap", scatter_dimension=0, tiled=True),
    )
    token_single = (sums / counts[:, None]).astype(jnp.bfloat16)
    left = jnp.dot(token_single, left_weight, preferred_element_type=jnp.float32).astype(
        jnp.bfloat16
    )
    right = jnp.dot(token_single, right_weight, preferred_element_type=jnp.float32).astype(
        jnp.bfloat16
    )
    right_all = lax.all_gather(right, "dap", axis=0, tiled=True)
    current = (
        pair_map.astype(jnp.float32)
        + left.astype(jnp.float32)[:, None, :]
        + right_all.astype(jnp.float32)[None, :, :]
    ).astype(jnp.bfloat16)
    for layer_index in range(2):
        current = triangle(
            current,
            tri_proj[layer_index],
            tri_gate[layer_index],
            tri_out[layer_index],
            tri_gains[layer_index],
            layer_index == 1,
        )
    return (token_single, current)


def solution(mesh):
    placed = (
        P(("dp", "dap"), None, None),
        P(("dp", "dap"), None),
        P(("dp", "dap")),
        P(),
        P(),
        P(),
        P(),
        P(),
        P(),
        P(),
    )
    return jax.shard_map(
        local,
        mesh=mesh,
        in_specs=placed,
        out_specs=(P(("dp", "dap"), None), P(("dp", "dap"), None, None)),
        check_vma=False,
    )
```

profile of v0, /device:TPU:1, one launch (start us, length us, event | category | flops | bytes accessed | tf_op | source)
XLA Modules:
  0.0 513.1 jit_solution(4341841822597679252)
XLA Ops:
  8.1 2.0 fusion.45
  14.5 130.4 %all-reduce.1 = f32[512]{0:T(512)S(1)} all-reduce(f32[512]{0:T(512)S(1)} %convert_reduce_fusion.2), channel_id=3, replica_groups=mesh['dp'=8,'dap'=64] {'dap'}, use_global_device_ids=true, to_apply=%region_2.3.clone | all-reduce | flops 512 | bytes 4096
  146.2 64.9 %all-reduce.4.cloned.1.call-done = f32[512,384]{1,0:T(8,128)} async-done(((f32[512,384]{1,0:T(8,128)}), f32[512,384]{1,0:T(8,128)}) %all-reduce.4.cloned.1.call-update) | async-done | bytes 786448
  212.0 49.9 %all_gather.3 = bf16[512,128]{1,0:T(8,128)(2,1)S(1)} all-gather(bf16[8,128]{1,0:T(8,128)(2,1)S(1)} %convolution_convert_fusion.2), channel_id=1, replica_groups=mesh['dp'=8,'dap'=64] {'dap'}, dimensions={0}, use_global_device_ids=true | all-gather | bytes 133120 | tf_op jit(solution)/shard_map/all_gather | solution.py:96
  263.2 1.8 convolution_bitcast_fusion.1
  267.4 3.4 copy.118
  270.8 7.7 %all-to-all-start.1 = ((bf16[64,2,8,512]{3,1,2,0:T(2,128)(2,1)}), bf16[64,2,8,512]{3,1,2,0:T(2,128)(2,1)}, u32[]{:S(2)}, u32[]{:S(2)}) async-start(bf16[64,2,8,512]{3,1,2,0:T(2,128)(2,1)} %copy.118), calls=%async_computation.1 | async-start | bytes 2097152 | tf_op jit(solution)/shard_map/all_to_all | solution.py:44
  280.1 26.3 %all-to-all-done.1 = bf16[64,2,8,512]{3,1,2,0:T(2,128)(2,1)} async-done(((bf16[64,2,8,512]{3,1,2,0:T(2,128)(2,1)}), bf16[64,2,8,512]{3,1,2,0:T(2,128)(2,1)}, u32[]{:S(2)}, u32[]{:S(2)}) %all-to-all-start.1) | async-done | bytes 1048608 | tf_op jit(solution)/shard_map/all_to_all | solution.py:44
  306.4 34.2 %all_to_all.78 = bf16[64,2,8,512]{3,1,2,0:T(2,128)(2,1)S(1)} all-to-all(bf16[64,2,8,512]{3,1,2,0:T(2,128)(2,1)S(1)} %copy.116), channel_id=1, replica_groups=mesh['dp'=8,'dap'=64] {'dap'}, dimensions={0} | all-to-all | bytes 2097152 | tf_op jit(solution)/shard_map/all_to_all | solution.py:43
  340.7 2.0 fusion.42
  342.7 2.0 copy.120
  344.7 6.5 %all-to-all-start.2 = ((bf16[1,2,512,512]{3,1,0,2:T(2,128)(2,1)}), bf16[1,2,512,512]{3,1,0,2:T(2,128)(2,1)S(1)}, u32[]{:S(2)}, u32[]{:S(2)}) async-start(bf16[1,2,512,512]{3,1,0,2:T(2,128)(2,1)} %copy.120), calls=%async_computation.2 | async-start | bytes 2097152 | tf_op jit(solution)/shard_map/all_to_all | solution.py:46
  352.1 2.2 fusion.59
  354.3 24.9 %all-to-all-done.2 = bf16[1,2,512,512]{3,1,0,2:T(2,128)(2,1)S(1)} async-done(((bf16[1,2,512,512]{3,1,0,2:T(2,128)(2,1)}), bf16[1,2,512,512]{3,1,0,2:T(2,128)(2,1)S(1)}, u32[]{:S(2)}, u32[]{:S(2)}) %all-to-all-start.2) | async-done | bytes 1048608 | tf_op jit(solution)/shard_map/all_to_all | solution.py:46
  384.2 2.6 convert_reduce_fusion
  391.1 3.4 copy.129
  394.6 6.6 %all-to-all-start.4 = ((bf16[64,2,8,512]{3,1,2,0:T(2,128)(2,1)}), bf16[64,2,8,512]{3,1,2,0:T(2,128)(2,1)}, u32[]{:S(2)}, u32[]{:S(2)}) async-start(bf16[64,2,8,512]{3,1,2,0:T(2,128)(2,1)} %copy.129), calls=%async_computation.4 | async-start | bytes 2097152 | tf_op jit(solution)/shard_map/all_to_all | solution.py:44
  401.8 27.3 %all-to-all-done.4 = bf16[64,2,8,512]{3,1,2,0:T(2,128)(2,1)} async-done(((bf16[64,2,8,512]{3,1,2,0:T(2,128)(2,1)}), bf16[64,2,8,512]{3,1,2,0:T(2,128)(2,1)}, u32[]{:S(2)}, u32[]{:S(2)}) %all-to-all-start.4) | async-done | bytes 1048608 | tf_op jit(solution)/shard_map/all_to_all | solution.py:44
  429.1 34.2 %all_to_all.79 = bf16[64,2,8,512]{3,2,1,0:T(8,128)(2,1)S(1)} all-to-all(bf16[64,2,8,512]{3,2,1,0:T(8,128)(2,1)S(1)} %bitcast.141), channel_id=1, replica_groups=mesh['dp'=8,'dap'=64] {'dap'}, dimensions={0} | all-to-all | bytes 2097152 | tf_op jit(solution)/shard_map/all_to_all | solution.py:43
  463.3 2.0 fusion.43
  465.4 2.0 copy.132
  467.4 6.5 %all-to-all-start.5 = ((bf16[1,2,512,512]{3,1,0,2:T(2,128)(2,1)}), bf16[1,2,512,512]{3,1,0,2:T(2,128)(2,1)S(1)}, u32[]{:S(2)}, u32[]{:S(2)}) async-start(bf16[1,2,512,512]{3,1,0,2:T(2,128)(2,1)} %copy.132), calls=%async_computation.5 | async-start | bytes 2097152 | tf_op jit(solution)/shard_map/all_to_all | solution.py:46
  474.1 1.9 fusion.62
  476.0 25.8 %all-to-all-done.5 = bf16[1,2,512,512]{3,1,0,2:T(2,128)(2,1)S(1)} async-done(((bf16[1,2,512,512]{3,1,0,2:T(2,128)(2,1)}), bf16[1,2,512,512]{3,1,0,2:T(2,128)(2,1)S(1)}, u32[]{:S(2)}, u32[]{:S(2)}) %all-to-all-start.5) | async-done | bytes 1048608 | tf_op jit(solution)/shard_map/all_to_all | solution.py:46
  (79 shorter events, 27.3 us)
Async XLA Ops:
  7.2 0.9 copy-start
  7.2 7.2 %copy-start.11 = (s32[96]{0:T(128)S(1)}, s32[96]{0:T(128)}, u32[]{:S(2)}) copy-start(s32[96]{0:T(128)} %param.12) | copy-start | bytes 1156
  7.2 4.6 copy-start.2
  7.2 137.8 %copy-start.14 = (f32[2,2,128]{2,1,0:T(2,128)S(1)}, f32[2,2,128]{2,1,0:T(2,128)}, u32[]{:S(2)}) copy-start(f32[2,2,128]{2,1,0:T(2,128)} %param.19) | copy-start | bytes 6148
  7.2 204.7 %copy-start.5 = (bf16[384,128]{1,0:T(8,128)(2,1)S(1)}, bf16[384,128]{1,0:T(8,128)(2,1)}, u32[]{:S(2)}) copy-start(bf16[384,128]{1,0:T(8,128)(2,1)} %param.15) | copy-start | bytes 294916
  7.2 203.9 %all-reduce.4.cloned.1.call-start = ((), (), s32[]{:S(2)}) async-start(), calls=%async_computation.6 | async-start | bytes 1572864
  10.1 252.0 %copy-start.6 = (bf16[384,128]{1,0:T(8,128)(2,1)S(1)}, bf16[384,128]{1,0:T(8,128)(2,1)}, u32[]{:S(2)}) copy-start(bf16[384,128]{1,0:T(8,128)(2,1)} %param.14) | copy-start | bytes 294916
  211.9 53.1 %copy-start.9 = (bf16[8,384]{1,0:T(8,128)(2,1)}, bf16[8,384]{1,0:T(8,128)(2,1)S(1)}, u32[]{:S(2)}) copy-start(bf16[8,384]{1,0:T(8,128)(2,1)S(1)} %fusion.74) | copy-start | bytes 18436
  270.8 35.6 %all-to-all-start.1 = ((bf16[64,2,8,512]{3,1,2,0:T(2,128)(2,1)}), bf16[64,2,8,512]{3,1,2,0:T(2,128)(2,1)}, u32[]{:S(2)}, u32[]{:S(2)}) async-start(bf16[64,2,8,512]{3,1,2,0:T(2,128)(2,1)} %copy.118), calls=%async_computation.1 | async-start | bytes 2097152 | tf_op jit(solution)/shard_map/all_to_all | solution.py:44
  342.7 8.5 %copy-start.13 = (f32[128]{0:T(128)S(1)}, f32[128]{0:T(128)}, u32[]{:S(2)}) copy-start(f32[128]{0:T(128)} %get-tuple-element.22) | copy-start | bytes 1540
  342.7 8.7 %copy-start.4 = (bf16[1,128,512]{2,1,0:T(8,128)(2,1)S(1)}, bf16[1,128,512]{2,1,0:T(8,128)(2,1)}, u32[]{:S(2)}) copy-start(bf16[1,128,512]{2,1,0:T(8,128)(2,1)} %get-tuple-element.18) | copy-start | bytes 393220
  342.7 9.4 %copy-start.7 = (bf16[2,128,128]{2,1,0:T(8,128)(2,1)S(1)}, bf16[2,128,128]{2,1,0:T(8,128)(2,1)}, u32[]{:S(2)}) copy-start(bf16[2,128,128]{2,1,0:T(8,128)(2,1)} %param.17) | copy-start | bytes 196612
  344.7 34.4 %all-to-all-start.2 = ((bf16[1,2,512,512]{3,1,0,2:T(2,128)(2,1)}), bf16[1,2,512,512]{3,1,0,2:T(2,128)(2,1)S(1)}, u32[]{:S(2)}, u32[]{:S(2)}) async-start(bf16[1,2,512,512]{3,1,0,2:T(2,128)(2,1)} %copy.120), calls=%async_computation.2 | async-start | bytes 2097152 | tf_op jit(solution)/shard_map/all_to_all | solution.py:46
  384.2 3.0 copy-start.3
  384.2 3.0 copy-start.10
  394.6 34.6 %all-to-all-start.4 = ((bf16[64,2,8,512]{3,1,2,0:T(2,128)(2,1)}), bf16[64,2,8,512]{3,1,2,0:T(2,128)(2,1)}, u32[]{:S(2)}, u32[]{:S(2)}) async-start(bf16[64,2,8,512]{3,1,2,0:T(2,128)(2,1)} %copy.129), calls=%async_computation.4 | async-start | bytes 2097152 | tf_op jit(solution)/shard_map/all_to_all | solution.py:44
  465.3 8.5 %copy-start.12 = (f32[128]{0:T(128)S(1)}, f32[128]{0:T(128)}, u32[]{:S(2)}) copy-start(f32[128]{0:T(128)} %get-tuple-element.23) | copy-start | bytes 1540
  465.3 8.8 %copy-start.8 = (bf16[2,128,128]{2,1,0:T(8,128)(2,1)S(1)}, bf16[2,128,128]{2,1,0:T(8,128)(2,1)}, u32[]{:S(2)}) copy-start(bf16[2,128,128]{2,1,0:T(8,128)(2,1)} %param.17) | copy-start | bytes 196612
  467.4 34.5 %all-to-all-start.5 = ((bf16[1,2,512,512]{3,1,0,2:T(2,128)(2,1)}), bf16[1,2,512,512]{3,1,0,2:T(2,128)(2,1)S(1)}, u32[]{:S(2)}, u32[]{:S(2)}) async-start(bf16[1,2,512,512]{3,1,0,2:T(2,128)(2,1)} %copy.132), calls=%async_computation.5 | async-start | bytes 2097152 | tf_op jit(solution)/shard_map/all_to_all | solution.py:46
  502.4 1.6 copy-start.1
  502.4 1.6 copy-start.15
Sparse Core Ops, SparseCore 0:
  12.1 198.9 all-reduce.3
where the time goes:
time: 514 us; the launch traced here: 513 us
  blocking collectives  249 us (48%)
  waiting for transfers between devices  169 us (33%)
  starting transfers between devices  27.3 us (5%)
  local copies, waits for them, and re-layouts  26.1 us (5%)
  matrix products  17.2 us (3%)
  between operations  15.1 us (3%)
  other arithmetic  9.24 us (2%)
    unnamed x1, blocking collectives  130 us
    all_to_all x2, blocking collectives, triangle(): lax.all_to_all(left_ops, 'dap', split_axis=0, concat_axis=2, tiled=True)  68.5 us
    unnamed x2, waiting for transfers between devices  65 us
    all_to_all x2, waiting for transfers between devices, triangle(): lax.all_to_all(right_ops, 'dap', split_axis=0, concat_axis=2, tiled=True)  53.6 us
    all_to_all x2, waiting for transfers between devices, triangle(): lax.all_to_all(contract(exchanged[0], exchanged[1], incoming), 'dap', spl...  50.7 us
    all_gather x1, blocking collectives, local(): right_all = lax.all_gather(right, 'dap', axis=0, tiled=True)  49.9 us
    all_to_all x2, starting transfers between devices, triangle(): lax.all_to_all(right_ops, 'dap', split_axis=0, concat_axis=2, tiled=True)  14.3 us
    all_to_all x2, starting transfers between devices, triangle(): lax.all_to_all(contract(exchanged[0], exchanged[1], incoming), 'dap', spl...  12.9 us
  transfers between devices with their start and end apart: 5, of which 5 were waited for; matrix products, arithmetic and copies ran while one was open for 2% of the time, Pallas kernels for 0%

commit v1 on v0

v1 whole, which is shorter than its diff:
```python
import jax
import jax.numpy as jnp
from jax import lax
from jax.experimental import pallas as pl
from jax.experimental.pallas import tpu as pltpu
from jax.sharding import PartitionSpec as P

EPS = 1e-05
F32, BF16 = jnp.float32, jnp.bfloat16
NT = (((1,), (1,)), ((), ()))
TN = (((0,), (0,)), ((), ()))
VMEM_LIMIT = 44 * 2**20


def mm(a, b, dims=(((1,), (0,)), ((), ()))):
    return lax.dot_general(a, b, dims, preferred_element_type=F32)


def sigmoid(x):
    return 0.5 * jnp.tanh(0.5 * x) + 0.5


def column(row, width):
    n = row.shape[1]
    tile = jnp.broadcast_to(row, (128, n)).T
    return jnp.concatenate([tile] * (width // 128), axis=1)


def norm_rows(x, gain):
    n = x.shape[0]
    centred = x - jnp.sum(x, axis=0, keepdims=True) * (1.0 / n)
    variance = jnp.sum(centred * centred, axis=0, keepdims=True) * (1.0 / n)
    return centred * lax.rsqrt(variance + EPS) * gain


def pool(feats_ref, tok_ref, weight_ref, tokens):
    atoms = feats_ref.shape[0]
    chunk = 512
    total = None
    for at in range(0, atoms, chunk):
        hidden = mm(feats_ref[at : at + chunk, :], weight_ref[...])
        hidden = jnp.maximum(hidden, 0.0).astype(BF16)
        hidden = jnp.concatenate([hidden, jnp.ones((chunk, 128), BF16)], axis=1)
        own = lax.broadcasted_iota(jnp.int32, (tokens, chunk), 0)
        picked = jnp.where(own == tok_ref[:, at : at + chunk], 1.0, 0.0).astype(BF16)
        part = mm(picked, hidden)
        total = part if total is None else total + part
    return total


def pool_kernel(feats_ref, tok_ref, weight_ref, out_ref):
    out_ref[...] = pool(feats_ref, tok_ref, weight_ref, out_ref.shape[0])


def put_row(s_ref, r, value):
    for t in range(s_ref.shape[0]):
        s_ref[t, pl.ds(r, value.shape[0], stride=8), :] = value[:, t * 128 : t * 128 + 128]


def get_row(s_ref, r, c):
    return jnp.concatenate(
        [s_ref[t, pl.ds(r, c, stride=8), :] for t in range(s_ref.shape[0])], axis=1
    )


def fill(s_ref, x_ref):
    for t in range(s_ref.shape[0]):
        s_ref[t] = x_ref[:, :, t * 128 : t * 128 + 128].reshape(-1, 128).astype(F32)


def operands(normed, proj_t, r, sa_ref, sb_ref):
    c = normed.shape[0]
    p = mm(proj_t, normed)
    put_row(sa_ref, r, sigmoid(p[:c]) * p[c : 2 * c])
    put_row(sb_ref, r, sigmoid(p[2 * c : 3 * c]) * p[3 * c :])


def pack(sa_ref, sb_ref, u_ref):
    n = u_ref.shape[0]
    for s_ref, at in ((sa_ref, 0), (sb_ref, 16)):
        for t in range(s_ref.shape[0]):
            u_ref[:, at : at + 16, t * 128 : t * 128 + 128] = (
                s_ref[t].reshape(n, 16, 128).astype(BF16)
            )


def first_kernel(
    idx_ref, psum_ref, feats_ref, tok_ref, weight_ref, wl_ref, wr_ref, pair_ref, proj_ref, gain_ref,
    single_ref, z_ref, n_ref, u_ref, ts_ref, sa_ref, sb_ref,
):
    rows, tokens, c = pair_ref.shape
    cs = wl_ref.shape[0]
    total = psum_ref[...] + pool(feats_ref, tok_ref, weight_ref, tokens)
    counts = total[:, cs:]
    single = jnp.concatenate(
        [total[:, at : at + 128] / counts for at in range(0, cs, 128)], axis=1
    )
    ts_ref[...] = single
    right = mm(single.astype(BF16), wr_ref[...]).astype(BF16).astype(F32)
    start = pl.multiple_of(idx_ref[0] * 8, 8)
    own = ts_ref[pl.ds(start, 8), :].astype(BF16)
    single_ref[...] = own
    left = mm(own, wl_ref[...]).astype(BF16).astype(F32)
    gain = column(gain_ref[...], tokens)
    proj_t = proj_ref[...].T
    for r in range(rows):
        z = (pair_ref[r].astype(F32) + left[r : r + 1, :] + right).astype(BF16)
        z = z.T
        z_ref[r] = z
        normed = norm_rows(z.astype(F32), gain).astype(BF16)
        n_ref[r] = normed
        operands(normed, proj_t, r, sa_ref, sb_ref)
    pack(sa_ref, sb_ref, u_ref)


def gate_kernel(n_ref, gate_ref, out_ref):
    gate_t = gate_ref[...].T
    for r in range(n_ref.shape[0]):
        out_ref[r] = sigmoid(mm(gate_t, n_ref[r]))


def product_kernel(dims, v_ref, r_ref):
    n, _, length = v_ref.shape
    a = v_ref[:, 0:16, :].astype(F32)
    b = v_ref[:, 16:32, :].astype(F32)
    out = []
    for ch in range(2):
        ac = a[:, ch * 8 : ch * 8 + 8, :].reshape(n * 8, length).astype(BF16)
        bc = b[:, ch * 8 : ch * 8 + 8, :].reshape(n * 8, length).astype(BF16)
        out.append(mm(ac, bc, dims).reshape(n, 8, length))
    r_ref[...] = jnp.concatenate(out, axis=1).astype(BF16)


def update_row(r, s_ref, out_t, gain, gating_ref, z_ref):
    c = out_t.shape[0]
    x = get_row(s_ref, r, c)
    normed = norm_rows(x, gain).astype(BF16)
    return z_ref[r].astype(F32) + gating_ref[r] * mm(out_t, normed)


def middle_kernel(
    x_ref, gating_ref, z_ref, out_ref, gain_out_ref, proj_ref, gain_in_ref,
    znew_ref, n_ref, u_ref, s_ref, sa_ref, sb_ref,
):
    rows, c, tokens = z_ref.shape
    fill(s_ref, x_ref)
    gain_out = column(gain_out_ref[...], tokens)
    gain_in = column(gain_in_ref[...], tokens)
    out_t = out_ref[...].T
    proj_t = proj_ref[...].T
    for r in range(rows):
        z = update_row(r, s_ref, out_t, gain_out, gating_ref, z_ref).astype(BF16)
        znew_ref[r] = z
        normed = norm_rows(z.astype(F32), gain_in).astype(BF16)
        n_ref[r] = normed
        operands(normed, proj_t, r, sa_ref, sb_ref)
    pack(sa_ref, sb_ref, u_ref)


def last_kernel(x_ref, gating_ref, z_ref, out_ref, gain_out_ref, pair_ref, s_ref):
    rows, c, tokens = z_ref.shape
    fill(s_ref, x_ref)
    gain_out = column(gain_out_ref[...], tokens)
    out_t = out_ref[...].T
    for r in range(rows):
        z = update_row(r, s_ref, out_t, gain_out, gating_ref, z_ref).astype(BF16)
        pair_ref[r] = z.T


def call(body, outs, args, scratch=(), name=None, flops=0, bytes_=0):
    specs = [
        pl.BlockSpec(memory_space=pltpu.SMEM if a.ndim == 1 else pltpu.VMEM) for a in args
    ]
    return pl.pallas_call(
        body,
        out_shape=outs,
        in_specs=specs,
        out_specs=jax.tree.map(lambda _: pl.BlockSpec(memory_space=pltpu.VMEM), outs),
        scratch_shapes=list(scratch),
        compiler_params=pltpu.CompilerParams(vmem_limit_bytes=VMEM_LIMIT),
        cost_estimate=pl.CostEstimate(flops=flops, bytes_accessed=bytes_, transcendentals=0),
        name=name,
    )(*args)


def local(
    pair_map, atom_feats, atom_token, atom_weight, left_weight, right_weight,
    tri_proj, tri_gate, tri_out, tri_gains,
):
    rows, tokens, c = pair_map.shape
    atoms = atom_feats.shape[0]
    cs = atom_weight.shape[1]
    n = lax.axis_size("dap")
    shape = jax.ShapeDtypeStruct
    me = lax.axis_index("dap").astype(jnp.int32).reshape(1)

    ny, nx = 8, 4
    groups_y = [[(y * nx + x) * 2 + k for y in range(ny)] for x in range(nx) for k in range(2)]
    groups_x = [[(y * nx + x) * 2 + k for x in range(nx)] for y in range(ny) for k in range(2)]
    tok = atom_token.reshape(1, atoms)
    tok = jnp.concatenate([tok // 32, tok % 32], axis=0).astype(BF16)
    tok = jnp.pad(tok, ((0, 14), (0, c - atoms)))
    packed = jnp.concatenate([atom_feats, tok], axis=0)

    def spread(v, count, groups):
        v = jnp.broadcast_to(v[None], (count,) + v.shape)
        return lax.all_to_all(
            v, "dap", split_axis=0, concat_axis=0, tiled=True, axis_index_groups=groups
        )

    got = spread(packed, ny, groups_y)
    got = spread(got.reshape(-1, c), nx, groups_x).reshape(ny * nx, atoms + 16, c)
    feats = got[:, :atoms, :].reshape(ny * nx * atoms, c)
    codes = got[:, atoms : atoms + 2, :atoms].astype(jnp.int32)
    toks = (codes[:, 0, :] * 32 + codes[:, 1, :]).reshape(1, ny * nx * atoms)
    swap = [(d, d ^ 1) for d in range(n)]
    feats_other = lax.ppermute(feats, "dap", swap)
    toks_other = lax.ppermute(toks, "dap", swap)
    psum = call(
        pool_kernel, shape((tokens, cs + 128), F32), (feats, toks, atom_weight),
        name="pool_half", flops=3_000_000_000, bytes_=2_000_000,
    )
    big = pltpu.VMEM((tokens // 128, rows * c, 128), F32)
    token_single, z, normed, sent = call(
        first_kernel,
        (
            shape((rows, cs), BF16),
            shape((rows, c, tokens), BF16),
            shape((rows, c, tokens), BF16),
            shape((n, 32, tokens), BF16),
        ),
        (me, psum, feats_other, toks_other, atom_weight, left_weight, right_weight, pair_map,
         tri_proj[0], tri_gains[0, 0:1]),
        [pltpu.VMEM((tokens, cs), F32), big, big],
        name="first", flops=4_000_000_000, bytes_=8_000_000,
    )

    def exchange(v):
        return lax.all_to_all(v, "dap", split_axis=0, concat_axis=0, tiled=True)

    for layer in range(2):
        got = exchange(sent)
        gating = call(
            gate_kernel, shape((rows, c, tokens), F32), (normed, tri_gate[layer]),
            name=f"gating{layer}", flops=200_000_000, bytes_=3_000_000,
        )
        dims = NT if layer == 0 else TN
        prod = call(
            lambda v, r, dims=dims: product_kernel(dims, v, r),
            shape((n, 16, tokens), BF16), (got,),
            name=f"product{layer}", flops=1_000_000_000, bytes_=3_000_000,
        )
        prod = exchange(prod)
        if layer == 0:
            z, normed, sent = call(
                middle_kernel,
                (
                    shape((rows, c, tokens), BF16),
                    shape((rows, c, tokens), BF16),
                    shape((n, 32, tokens), BF16),
                ),
                (prod, gating, z, tri_out[0], tri_gains[0, 1:2], tri_proj[1], tri_gains[1, 0:1]),
                [big, big, big],
                name="middle", flops=1_000_000_000, bytes_=8_000_000,
            )
        else:
            pair = call(
                last_kernel, shape((rows, tokens, c), BF16),
                (prod, gating, z, tri_out[1], tri_gains[1, 1:2]),
                [big],
                name="last", flops=200_000_000, bytes_=5_000_000,
            )
    return token_single, pair


def solution(mesh):
    placed = (
        P(("dp", "dap"), None, None),
        P(("dp", "dap"), None),
        P(("dp", "dap")),
        P(),
        P(),
        P(),
        P(),
        P(),
        P(),
        P(),
    )
    return jax.shard_map(
        local,
        mesh=mesh,
        in_specs=placed,
        out_specs=(P(("dp", "dap"), None), P(("dp", "dap"), None, None)),
        check_vma=False,
    )
```

time: 514 us -> 248 us (0.48)
  blocking collectives: 249 us -> 126 us
  waiting for transfers between devices: 169 us -> 63.2 us
  Pallas kernels: 0 us -> 20.3 us
  local copies, waits for them, and re-layouts: 26.1 us -> 8.14 us
  matrix products: 17.2 us -> 0 us
  between operations: 15.1 us -> 0.89 us
  other arithmetic: 9.24 us -> 1.54 us
    unnamed x1 -> x0, blocking collectives: 130 us -> none
    unnamed x2 -> x0, waiting for transfers between devices: 65 us -> none
    all_to_all x2 -> x3, blocking collectives: 68.5 us -> 126 us  [the longest x2 110 us: exchange(): return lax.all_to_all(v, 'dap', split_axis=0, concat_axis=0, tiled=True)]
    all_gather x1 -> x0, blocking collectives: 49.9 us -> none  [local(): right_all = lax.all_gather(right, 'dap', axis=0, tiled=True)]
    all_to_all x4 -> x3, waiting for transfers between devices: 104 us -> 63.2 us  [the longest x2 52.5 us: exchange(): return lax.all_to_all(v, 'dap', split_axis=0, concat_axis=0, tiled=True)]
    pallas_call x0 -> x8, Pallas kernels: none -> 20.3 us  [call(): pl.pallas_call(body, out_shape=outs, in_specs=specs, out_specs=jax.tree.m...]
    dot_general x11 -> x0, matrix products: 17.2 us -> none  [the longest x2 4.12 us: triangle(): jnp.einsum('ijc,cd->ijd', normed, gate, preferred_element_type=jnp.float32)]
    convert_element_type x13 -> x0, local copies, waits for them, and re-layouts: 16.9 us -> none  [the longest x4 9.26 us: triangle(): right_ops = (jax.nn.sigmoid(stacked[2]) * stacked[3]).astype(jnp.bfloat16)]
  transfers between devices with their start and end apart: 5 -> 5, of which waited for: 5 -> 3; matrix products, arithmetic and copies ran while one was open for 2% -> 0% of each run, Pallas kernels for 0% -> 2%
where the time goes in v1:
time: 248 us; the launch traced here: 247 us
  blocking collectives  126 us (51%)
  waiting for transfers between devices  63.2 us (25%)
  starting transfers between devices  26.9 us (11%)
  Pallas kernels  20.3 us (8%)
  local copies, waits for them, and re-layouts  8.14 us (3%)
    all_to_all x2, blocking collectives, exchange(): return lax.all_to_all(v, 'dap', split_axis=0, concat_axis=0, tiled=True)  110 us
    all_to_all x2, waiting for transfers between devices, exchange(): return lax.all_to_all(v, 'dap', split_axis=0, concat_axis=0, tiled=True)  52.5 us
    pallas_call x8, Pallas kernels, call(): pl.pallas_call(body, out_shape=outs, in_specs=specs, out_specs=jax.tree.m...  20.3 us
    all_to_all x1, blocking collectives, spread(): lax.all_to_all(v, 'dap', split_axis=0, concat_axis=0, tiled=True, axis_in...  16.3 us
    all_to_all x2, starting transfers between devices, exchange(): return lax.all_to_all(v, 'dap', split_axis=0, concat_axis=0, tiled=True)  14 us
    all_to_all x1, waiting for transfers between devices, spread(): lax.all_to_all(v, 'dap', split_axis=0, concat_axis=0, tiled=True, axis_in...  10.7 us
    unnamed x32, local copies, waits for them, and re-layouts  6.89 us
    ppermute x1, starting transfers between devices, local(): feats_other = lax.ppermute(feats, 'dap', swap)  5.79 us
  transfers between devices with their start and end apart: 5, of which 3 were waited for; matrix products, arithmetic and copies ran while one was open for 0% of the time, Pallas kernels for 2%

profile of v1, /device:TPU:1, one launch (start us, length us, event | category | flops | bytes accessed | tf_op | source)
XLA Modules:
  0.0 247.4 jit_solution(11203780196425627131)
XLA Ops:
  2.1 16.3 %all_to_all.30 = bf16[8,112,128]{2,1,0:T(8,128)(2,1)S(1)} all-to-all(bf16[8,112,128]{2,1,0:T(8,128)(2,1)S(1)} %broadcast_in_dim.6), channel_id=1, replica_groups={{0,8,16,24,32,40,48,56},{1,9,17,25,33,41,49,57},{2,10,18,26,34,42,50,58..., dimensions={0} | all-to-all | bytes 458752 | tf_op jit(solution)/shard_map/all_to_all | solution.py:207
  18.5 1.0 broadcast_in_dim.15
  19.5 5.0 %all-to-all-start.1 = ((bf16[4,896,128]{2,1,0:T(8,128)(2,1)}), bf16[4,896,128]{2,1,0:T(8,128)(2,1)S(1)}, u32[]{:S(2)}, u32[]{:S(2)}) async-start(bf16[4,896,128]{2,1,0:T(8,128)(2,1)} %broadcast_in_dim.15), calls=%async_computation.1 | async-start | bytes 1835008 | tf_op jit(solution)/shard_map/all_to_all | solution.py:207
  24.6 10.7 %all-to-all-done.1 = bf16[4,896,128]{2,1,0:T(8,128)(2,1)S(1)} async-done(((bf16[4,896,128]{2,1,0:T(8,128)(2,1)}), bf16[4,896,128]{2,1,0:T(8,128)(2,1)S(1)}, u32[]{:S(2)}, u32[]{:S(2)}) %all-to-all-start.1) | async-done | bytes 917536 | tf_op jit(solution)/shard_map/all_to_all | solution.py:207
  35.4 5.8 %collective-permute-start = (bf16[3072,128]{1,0:T(8,128)(2,1)S(1)}, bf16[3072,128]{1,0:T(8,128)(2,1)S(1)}, u32[]{:S(2)}, u32[]{:S(2)}) collective-permute-start(bf16[3072,128]{1,0:T(8,128)(2,1)S(1)} %bitcast.28), channel_id=1, source_target_pairs={{0,1},{1,0},{2,3},{3,2},{4,5},{5,4},{6,7},{7,6},{8,9},{9,8},{10,11... | collective-permute-start | bytes 2359304 | tf_op jit(solution)/shard_map/ppermute | solution.py:217
  41.4 2.1 collective-permute-start.1
  43.5 2.8 %pool_half.1.psum_ref = f32[512,512]{1,0:T(8,128)S(1)} custom-call(bf16[3072,128]{1,0:T(8,128)(2,1)S(1)} %bitcast.29, s32[1,3072]{1,0:T(1,128)S(1)} %add.26.tok_ref, bf16[128,384]{1,0:T(8,128)(2,1)S(1)} %copy-done.9), custom_call_target="tpu_custom_call" | custom-call | flops 3000000000 | bytes 2000000 | tf_op jit(solution)/shard_map/pool_half/pallas_call | solution.py:174
  46.3 6.2 %first.1 = (bf16[8,384]{1,0:T(8,128)(2,1)}, bf16[8,128,512]{2,1,0:T(8,128)(2,1)S(1)}, bf16[8,128,512]{2,1,0:T(8,128)(2,1)S(1)}, bf16[64,32,512]{2,1,0:T(8,128)(2,1)S(1)}) custom-call(s32[1]{0:T(128)} %bitcast.idx_ref, f32[512,512]{1,0:T(8,128)S(1)} %pool_half.1.psum_ref, bf16[3072,128]{1,0:T(8,128)(2,1)S(1)} %collective-permute-done.feats_ref, ...), custom_call_target="tpu_custom_call" | custom-call | flops 4000000000 | bytes 8000000 | tf_op jit(solution)/shard_map/first/pallas_call | solution.py:174
  52.5 54.1 %all_to_all.31.v = bf16[64,32,512]{2,1,0:T(8,128)(2,1)S(1)} all-to-all(bf16[64,32,512]{2,1,0:T(8,128)(2,1)S(1)} %get-tuple-element.10), channel_id=1, replica_groups=mesh['dp'=8,'dap'=64] {'dap'}, dimensions={0} | all-to-all | bytes 4194304 | tf_op jit(solution)/shard_map/all_to_all | solution.py:239
  106.6 1.7 product0.1
  108.3 7.0 %all-to-all-start.3 = ((bf16[64,16,512]{2,1,0:T(8,128)(2,1)}), bf16[64,16,512]{2,1,0:T(8,128)(2,1)S(1)}, u32[]{:S(2)}, u32[]{:S(2)}) async-start(bf16[64,16,512]{2,1,0:T(8,128)(2,1)} %product0.1), calls=%async_computation.3 | async-start | bytes 2097152 | tf_op jit(solution)/shard_map/all_to_all | solution.py:239
  115.4 1.2 copy-done.3
  117.1 26.2 %all-to-all-done.3.x_ref = bf16[64,16,512]{2,1,0:T(8,128)(2,1)S(1)} async-done(((bf16[64,16,512]{2,1,0:T(8,128)(2,1)}), bf16[64,16,512]{2,1,0:T(8,128)(2,1)S(1)}, u32[]{:S(2)}, u32[]{:S(2)}) %all-to-all-start.3) | async-done | bytes 1048608 | tf_op jit(solution)/shard_map/all_to_all | solution.py:239
  143.3 1.2 copy-done.1
  144.5 4.5 %middle.1 = (bf16[8,128,512]{2,1,0:T(8,128)(2,1)S(1)}, bf16[8,128,512]{2,1,0:T(8,128)(2,1)S(1)}, bf16[64,32,512]{2,1,0:T(8,128)(2,1)S(1)}) custom-call(bf16[64,16,512]{2,1,0:T(8,128)(2,1)S(1)} %all-to-all-done.3.x_ref, f32[8,128,512]{2,1,0:T(8,128)S(1)} %gating0.1.gating_ref, bf16[8,128,512]{2,1,0:T(8,128)(2,1)S(1)} %copy-done.1, ...), custom_call_target="tpu_custom_call" | custom-call | flops 1000000000 | bytes 8000000 | tf_op jit(solution)/shard_map/middle/pallas_call | solution.py:174
  149.0 1.0 copy-done.4
  150.0 1.0 copy-done.6
  151.0 55.9 %all_to_all.32.v = bf16[64,32,512]{2,1,0:T(8,128)(2,1)S(1)} all-to-all(bf16[64,32,512]{2,1,0:T(8,128)(2,1)S(1)} %get-tuple-element.13), channel_id=1, replica_groups=mesh['dp'=8,'dap'=64] {'dap'}, dimensions={0} | all-to-all | bytes 4194304 | tf_op jit(solution)/shard_map/all_to_all | solution.py:239
  206.9 1.7 product1.1
  208.6 7.0 %all-to-all-start.5 = ((bf16[64,16,512]{2,1,0:T(8,128)(2,1)}), bf16[64,16,512]{2,1,0:T(8,128)(2,1)S(1)}, u32[]{:S(2)}, u32[]{:S(2)}) async-start(bf16[64,16,512]{2,1,0:T(8,128)(2,1)} %product1.1), calls=%async_computation.5 | async-start | bytes 2097152 | tf_op jit(solution)/shard_map/all_to_all | solution.py:239
  215.6 1.2 copy-done.5
  217.3 26.3 %all-to-all-done.5.x_ref = bf16[64,16,512]{2,1,0:T(8,128)(2,1)S(1)} async-done(((bf16[64,16,512]{2,1,0:T(8,128)(2,1)}), bf16[64,16,512]{2,1,0:T(8,128)(2,1)S(1)}, u32[]{:S(2)}, u32[]{:S(2)}) %all-to-all-start.5) | async-done | bytes 1048608 | tf_op jit(solution)/shard_map/all_to_all | solution.py:239
  243.6 1.2 copy-done.7
  244.8 2.5 %last.1 = bf16[8,512,128]{2,1,0:T(8,128)(2,1)} custom-call(bf16[64,16,512]{2,1,0:T(8,128)(2,1)S(1)} %all-to-all-done.5.x_ref, f32[8,128,512]{2,1,0:T(8,128)S(1)} %gating1.1.gating_ref, bf16[8,128,512]{2,1,0:T(8,128)(2,1)S(1)} %copy-done.7, bf16[128,128]{1,0:T(8,128)(2,1)S(1)} %get-tuple-element.18.out_ref, f32[1,128]{1,0:T(1,128)S(1)} %get-tuple-element.22.gain_out_ref), custom_call_target="tpu_custom_call" | custom-call | flops 200000000 | bytes 5000000 | tf_op jit(solution)/shard_map/last/pallas_call | solution.py:174
  (42 shorter events, 2.8 us)
Async XLA Ops:
  0.6 23.9 %copy-start.12 = (bf16[2,128,512]{2,1,0:T(8,128)(2,1)S(1)}, bf16[2,128,512]{2,1,0:T(8,128)(2,1)}, u32[]{:S(2)}) copy-start(bf16[2,128,512]{2,1,0:T(8,128)(2,1)} %param.16) | copy-start | bytes 786436
  19.5 21.6 %copy-start.15 = (f32[2,2,128]{2,1,0:T(2,128)S(1)}, f32[2,2,128]{2,1,0:T(2,128)}, u32[]{:S(2)}) copy-start(f32[2,2,128]{2,1,0:T(2,128)} %param.19) | copy-start | bytes 6148
  19.5 23.9 %copy-start.9 = (bf16[128,384]{1,0:T(8,128)(2,1)S(1)}, bf16[128,384]{1,0:T(8,128)(2,1)}, u32[]{:S(2)}) copy-start(bf16[128,384]{1,0:T(8,128)(2,1)} %weight_ref.3) | copy-start | bytes 294916
  19.5 15.8 %all-to-all-start.1 = ((bf16[4,896,128]{2,1,0:T(8,128)(2,1)}), bf16[4,896,128]{2,1,0:T(8,128)(2,1)S(1)}, u32[]{:S(2)}, u32[]{:S(2)}) async-start(bf16[4,896,128]{2,1,0:T(8,128)(2,1)} %broadcast_in_dim.15), calls=%async_computation.1 | async-start | bytes 1835008 | tf_op jit(solution)/shard_map/all_to_all | solution.py:207
  35.4 10.9 %collective-permute-start = (bf16[3072,128]{1,0:T(8,128)(2,1)S(1)}, bf16[3072,128]{1,0:T(8,128)(2,1)S(1)}, u32[]{:S(2)}, u32[]{:S(2)}) collective-permute-start(bf16[3072,128]{1,0:T(8,128)(2,1)S(1)} %bitcast.28), channel_id=1, source_target_pairs={{0,1},{1,0},{2,3},{3,2},{4,5},{5,4},{6,7},{7,6},{8,9},{9,8},{10,11... | collective-permute-start | bytes 2359304 | tf_op jit(solution)/shard_map/ppermute | solution.py:217
  41.4 4.9 %copy-start.8 = (bf16[8,512,128]{2,1,0:T(8,128)(2,1)S(1)}, bf16[8,512,128]{2,1,0:T(8,128)(2,1)}, u32[]{:S(2)}) copy-start(bf16[8,512,128]{2,1,0:T(8,128)(2,1)} %pair_ref.1) | copy-start | bytes 3145732
  41.4 4.9 %copy-start.10 = (bf16[384,128]{1,0:T(8,128)(2,1)S(1)}, bf16[384,128]{1,0:T(8,128)(2,1)}, u32[]{:S(2)}) copy-start(bf16[384,128]{1,0:T(8,128)(2,1)} %wl_ref.1) | copy-start | bytes 294916
  41.4 4.9 %copy-start.11 = (bf16[384,128]{1,0:T(8,128)(2,1)S(1)}, bf16[384,128]{1,0:T(8,128)(2,1)}, u32[]{:S(2)}) copy-start(bf16[384,128]{1,0:T(8,128)(2,1)} %wr_ref.1) | copy-start | bytes 294916
  41.4 4.8 %collective-permute-start.1 = (s32[1,3072]{1,0:T(1,128)S(1)}, s32[1,3072]{1,0:T(1,128)S(1)}, u32[]{:S(2)}, u32[]{:S(2)}) collective-permute-start(s32[1,3072]{1,0:T(1,128)S(1)} %add.26.tok_ref), channel_id=1, source_target_pairs={{0,1},{1,0},{2,3},{3,2},{4,5},{5,4},{6,7},{7,6},{8,9},{9,8},{10,11... | collective-permute-start | bytes 36872 | tf_op jit(solution)/shard_map/ppermute | solution.py:218
  52.4 54.1 %copy-start = (bf16[8,128,512]{2,1,0:T(8,128)(2,1)}, bf16[8,128,512]{2,1,0:T(8,128)(2,1)S(1)}, u32[]{:S(2)}) copy-start(bf16[8,128,512]{2,1,0:T(8,128)(2,1)S(1)} %get-tuple-element.12.z_ref) | copy-start | bytes 3145732
  52.5 54.1 %copy-start.2 = (bf16[8,128,512]{2,1,0:T(8,128)(2,1)}, bf16[8,128,512]{2,1,0:T(8,128)(2,1)S(1)}, u32[]{:S(2)}) copy-start(bf16[8,128,512]{2,1,0:T(8,128)(2,1)S(1)} %get-tuple-element.11.n_ref) | copy-start | bytes 3145732
  106.6 8.8 %copy-start.13 = (bf16[2,128,128]{2,1,0:T(8,128)(2,1)S(1)}, bf16[2,128,128]{2,1,0:T(8,128)(2,1)}, u32[]{:S(2)}) copy-start(bf16[2,128,128]{2,1,0:T(8,128)(2,1)} %param.17) | copy-start | bytes 196612
  106.6 8.8 %copy-start.14 = (bf16[2,128,128]{2,1,0:T(8,128)(2,1)S(1)}, bf16[2,128,128]{2,1,0:T(8,128)(2,1)}, u32[]{:S(2)}) copy-start(bf16[2,128,128]{2,1,0:T(8,128)(2,1)} %param.18) | copy-start | bytes 196612
  108.3 35.0 %all-to-all-start.3 = ((bf16[64,16,512]{2,1,0:T(8,128)(2,1)}), bf16[64,16,512]{2,1,0:T(8,128)(2,1)S(1)}, u32[]{:S(2)}, u32[]{:S(2)}) async-start(bf16[64,16,512]{2,1,0:T(8,128)(2,1)} %product0.1), calls=%async_computation.3 | async-start | bytes 2097152 | tf_op jit(solution)/shard_map/all_to_all | solution.py:239
  115.4 1.2 copy-start.3
  143.3 1.2 copy-start.1
  149.0 1.0 copy-start.4
  150.0 1.0 copy-start.6
  208.6 35.0 %all-to-all-start.5 = ((bf16[64,16,512]{2,1,0:T(8,128)(2,1)}), bf16[64,16,512]{2,1,0:T(8,128)(2,1)S(1)}, u32[]{:S(2)}, u32[]{:S(2)}) async-start(bf16[64,16,512]{2,1,0:T(8,128)(2,1)} %product1.1), calls=%async_computation.5 | async-start | bytes 2097152 | tf_op jit(solution)/shard_map/all_to_all | solution.py:239
  215.6 1.2 copy-start.5
  243.6 1.2 copy-start.7

commit v2 on v1

v2 whole, which is shorter than its diff:
```python
import jax
import jax.numpy as jnp
from jax import lax
from jax.experimental import pallas as pl
from jax.experimental.pallas import tpu as pltpu
from jax.sharding import PartitionSpec as P

EPS = 1e-05
F32, BF16 = jnp.float32, jnp.bfloat16
NT = (((1,), (1,)), ((), ()))
TN = (((0,), (0,)), ((), ()))
VMEM_LIMIT = 16 * 2**20


def mm(a, b, dims=(((1,), (0,)), ((), ()))):
    return lax.dot_general(a, b, dims, preferred_element_type=F32)


def sigmoid(x):
    return 0.5 * jnp.tanh(0.5 * x) + 0.5


def column(row, width):
    n = row.shape[1]
    tile = jnp.broadcast_to(row, (128, n)).T
    return jnp.concatenate([tile] * (width // 128), axis=1)


def norm_rows(x, gain):
    n = x.shape[0]
    centred = x - jnp.sum(x, axis=0, keepdims=True) * (1.0 / n)
    variance = jnp.sum(centred * centred, axis=0, keepdims=True) * (1.0 / n)
    return centred * lax.rsqrt(variance + EPS) * gain


def pool(packed_ref, weight_ref, tokens):
    blocks, rows, _ = packed_ref.shape
    atoms = rows - 16
    some = 8
    total = None
    for at in range(0, blocks, some):
        feats = packed_ref[at : at + some, 0:atoms, :].reshape(some * atoms, -1)
        hidden = jnp.maximum(mm(feats, weight_ref[...]), 0.0).astype(BF16)
        hidden = jnp.concatenate([hidden, jnp.ones((some * atoms, 128), BF16)], axis=1)
        toks = []
        for k in range(at, at + some):
            codes = packed_ref[k, atoms:rows, :].astype(F32)
            toks.append((codes[0:1, :atoms] * 32.0 + codes[1:2, :atoms]).astype(jnp.int32))
        toks = jnp.concatenate(toks, axis=1)
        own = lax.broadcasted_iota(jnp.int32, (tokens, some * atoms), 0)
        part = mm(jnp.where(own == toks, 1.0, 0.0).astype(BF16), hidden)
        total = part if total is None else total + part
    return total


def pool_kernel(packed_ref, weight_ref, out_ref):
    out_ref[...] = pool(packed_ref, weight_ref, out_ref.shape[0])


def put_row(s_ref, r, value):
    for t in range(s_ref.shape[0]):
        s_ref[t, pl.ds(r, value.shape[0], stride=8), :] = value[:, t * 128 : t * 128 + 128]


def get_row(s_ref, r, c):
    return jnp.concatenate(
        [s_ref[t, pl.ds(r, c, stride=8), :] for t in range(s_ref.shape[0])], axis=1
    )


def fill(s_ref, x_ref):
    for t in range(s_ref.shape[0]):
        s_ref[t] = x_ref[:, :, t * 128 : t * 128 + 128].reshape(-1, 128).astype(F32)


def operands(normed, proj_t, r, sa_ref, sb_ref):
    c = normed.shape[0]
    p = mm(proj_t, normed)
    put_row(sa_ref, r, sigmoid(p[:c]) * p[c : 2 * c])
    put_row(sb_ref, r, sigmoid(p[2 * c : 3 * c]) * p[3 * c :])


def pack(sa_ref, sb_ref, u_ref):
    n = u_ref.shape[0]
    for s_ref, at in ((sa_ref, 0), (sb_ref, 16)):
        for t in range(s_ref.shape[0]):
            u_ref[:, at : at + 16, t * 128 : t * 128 + 128] = (
                s_ref[t].reshape(n, 16, 128).astype(BF16)
            )


def first_kernel(
    idx_ref, psum_ref, packed_ref, weight_ref, wl_ref, wr_ref, pair_ref, proj_ref, gain_ref,
    single_ref, z_out, u_ref, ts_ref, sa_ref, sb_ref, z_ref, sem,
):
    rows, tokens, c = pair_ref.shape
    cs = wl_ref.shape[0]
    total = psum_ref[...] + pool(packed_ref, weight_ref, tokens)
    counts = total[:, cs:]
    single = jnp.concatenate(
        [total[:, at : at + 128] / counts for at in range(0, cs, 128)], axis=1
    )
    ts_ref[...] = single
    right = mm(single.astype(BF16), wr_ref[...]).astype(BF16).astype(F32)
    start = pl.multiple_of(idx_ref[0] * 8, 8)
    own = ts_ref[pl.ds(start, 8), :].astype(BF16)
    single_ref[...] = own
    left = mm(own, wl_ref[...]).astype(BF16).astype(F32)
    gain = column(gain_ref[...], tokens)
    proj_t = proj_ref[...].T
    for r in range(rows):
        z = (pair_ref[r].astype(F32) + left[r : r + 1, :] + right).astype(BF16)
        z = z.T
        z_ref[r] = z
        normed = norm_rows(z.astype(F32), gain).astype(BF16)
        operands(normed, proj_t, r, sa_ref, sb_ref)
    copy = pltpu.make_async_copy(z_ref, z_out, sem)
    copy.start()
    pack(sa_ref, sb_ref, u_ref)
    copy.wait()


def gate_kernel(z_in, gate_ref, gain_ref, out_ref, z_ref, sem):
    rows, _, tokens = z_ref.shape
    copy = pltpu.make_async_copy(z_in, z_ref, sem)
    copy.start()
    gate_t = gate_ref[...].T
    gain = column(gain_ref[...], tokens)
    copy.wait()
    for r in range(rows):
        z = z_ref[r]
        normed = norm_rows(z.astype(F32), gain).astype(BF16)
        out_ref[r] = sigmoid(mm(gate_t, normed)).astype(BF16)
        out_ref[rows + r] = z


def product_kernel(dims, v_ref, r_ref):
    n, _, length = v_ref.shape
    a = v_ref[:, 0:16, :].astype(F32)
    b = v_ref[:, 16:32, :].astype(F32)
    out = []
    for ch in range(2):
        ac = a[:, ch * 8 : ch * 8 + 8, :].reshape(n * 8, length).astype(BF16)
        bc = b[:, ch * 8 : ch * 8 + 8, :].reshape(n * 8, length).astype(BF16)
        out.append(mm(ac, bc, dims).reshape(n, 8, length))
    r_ref[...] = jnp.concatenate(out, axis=1).astype(BF16)


def update_row(r, s_ref, out_t, gain, held_ref):
    c = out_t.shape[0]
    x = get_row(s_ref, r, c)
    normed = norm_rows(x, gain).astype(BF16)
    rows = held_ref.shape[0] // 2
    gating, z = held_ref[r].astype(F32), held_ref[rows + r].astype(F32)
    return (z + gating * mm(out_t, normed)).astype(BF16)


def middle_kernel(
    x_ref, held_ref, out_ref, gain_out_ref, proj_ref, gain_in_ref,
    z_out, u_ref, s_ref, sa_ref, sb_ref, z_ref, sem,
):
    rows, c, tokens = z_ref.shape
    fill(s_ref, x_ref)
    gain_out = column(gain_out_ref[...], tokens)
    gain_in = column(gain_in_ref[...], tokens)
    out_t = out_ref[...].T
    proj_t = proj_ref[...].T
    for r in range(rows):
        z = update_row(r, s_ref, out_t, gain_out, held_ref)
        z_ref[r] = z
        normed = norm_rows(z.astype(F32), gain_in).astype(BF16)
        operands(normed, proj_t, r, sa_ref, sb_ref)
    copy = pltpu.make_async_copy(z_ref, z_out, sem)
    copy.start()
    pack(sa_ref, sb_ref, u_ref)
    copy.wait()


def last_kernel(x_ref, held_ref, out_ref, gain_out_ref, pair_ref, s_ref):
    rows, tokens, c = pair_ref.shape
    fill(s_ref, x_ref)
    gain_out = column(gain_out_ref[...], tokens)
    out_t = out_ref[...].T
    for r in range(rows):
        z = update_row(r, s_ref, out_t, gain_out, held_ref)
        pair_ref[r] = z.T


def call(body, outs, args, scratch=(), name=None, flops=0, bytes_=0, far_in=(), far_out=()):
    specs = [
        pl.BlockSpec(
            memory_space=pltpu.HBM if k in far_in else pltpu.SMEM if a.ndim == 1 else pltpu.VMEM
        )
        for k, a in enumerate(args)
    ]
    places = [
        pl.BlockSpec(memory_space=pltpu.HBM if k in far_out else pltpu.VMEM)
        for k in range(len(outs))
    ]
    return pl.pallas_call(
        body,
        out_shape=outs,
        in_specs=specs,
        out_specs=places,
        scratch_shapes=list(scratch),
        compiler_params=pltpu.CompilerParams(vmem_limit_bytes=VMEM_LIMIT),
        cost_estimate=pl.CostEstimate(flops=flops, bytes_accessed=bytes_, transcendentals=0),
        name=name,
    )(*args)


def local(
    pair_map, atom_feats, atom_token, atom_weight, left_weight, right_weight,
    tri_proj, tri_gate, tri_out, tri_gains,
):
    rows, tokens, c = pair_map.shape
    atoms = atom_feats.shape[0]
    cs = atom_weight.shape[1]
    n = lax.axis_size("dap")
    shape = jax.ShapeDtypeStruct
    me = lax.axis_index("dap").astype(jnp.int32).reshape(1)

    ny, nx = 8, 4
    groups_y = [[(y * nx + x) * 2 + k for y in range(ny)] for x in range(nx) for k in range(2)]
    groups_x = [[(y * nx + x) * 2 + k for x in range(nx)] for y in range(ny) for k in range(2)]
    tok = atom_token.reshape(1, atoms)
    tok = jnp.concatenate([tok // 32, tok % 32], axis=0).astype(BF16)
    tok = jnp.pad(tok, ((0, 14), (0, c - atoms)))
    packed = jnp.concatenate([atom_feats, tok], axis=0)

    got = lax.all_to_all(
        jnp.broadcast_to(packed[None], (ny,) + packed.shape), "dap",
        split_axis=0, concat_axis=0, tiled=True, axis_index_groups=groups_y,
    )
    got = lax.all_gather(got, "dap", axis=0, tiled=True, axis_index_groups=groups_x)
    other = lax.ppermute(got, "dap", [(d, d ^ 1) for d in range(n)])
    (psum,) = call(
        pool_kernel, (shape((tokens, cs + 128), F32),), (got, atom_weight),
        name="pool_half", flops=3_000_000_000, bytes_=2_000_000,
    )
    big = pltpu.VMEM((tokens // 128, rows * c, 128), F32)
    held = [pltpu.VMEM((rows, c, tokens), BF16), pltpu.SemaphoreType.DMA]
    z_shape = shape((rows, c, tokens), BF16)
    sent_shape = shape((n, 32, tokens), BF16)
    token_single, z, sent = call(
        first_kernel,
        (shape((rows, cs), BF16), z_shape, sent_shape),
        (me, psum, other, atom_weight, left_weight, right_weight, pair_map,
         tri_proj[0], tri_gains[0, 0:1]),
        [pltpu.VMEM((tokens, cs), F32), big, big, *held],
        name="first", flops=4_000_000_000, bytes_=8_000_000, far_out=(1,),
    )

    def exchange(v):
        return lax.all_to_all(v, "dap", split_axis=0, concat_axis=0, tiled=True)

    for layer in range(2):
        got = exchange(sent)
        (kept,) = call(
            gate_kernel, (shape((2 * rows, c, tokens), BF16),),
            (z, tri_gate[layer], tri_gains[layer, 0:1]), held,
            name=f"gating{layer}", flops=200_000_000, bytes_=3_000_000, far_in=(0,),
        )
        dims = NT if layer == 0 else TN
        (prod,) = call(
            lambda v, r, dims=dims: product_kernel(dims, v, r),
            (shape((n, 16, tokens), BF16),), (got,),
            name=f"product{layer}", flops=1_000_000_000, bytes_=3_000_000,
        )
        prod = exchange(prod)
        if layer == 0:
            z, sent = call(
                middle_kernel, (z_shape, sent_shape),
                (prod, kept, tri_out[0], tri_gains[0, 1:2], tri_proj[1], tri_gains[1, 0:1]),
                [big, big, big, *held],
                name="middle", flops=1_000_000_000, bytes_=8_000_000, far_out=(0,),
            )
        else:
            (pair,) = call(
                last_kernel, (shape((rows, tokens, c), BF16),),
                (prod, kept, tri_out[1], tri_gains[1, 1:2]),
                [big],
                name="last", flops=200_000_000, bytes_=5_000_000,
            )
    return token_single, pair


def solution(mesh):
    placed = (
        P(("dp", "dap"), None, None),
        P(("dp", "dap"), None),
        P(("dp", "dap")),
        P(),
        P(),
        P(),
        P(),
        P(),
        P(),
        P(),
    )
    return jax.shard_map(
        local,
        mesh=mesh,
        in_specs=placed,
        out_specs=(P(("dp", "dap"), None), P(("dp", "dap"), None, None)),
        check_vma=False,
    )
```

time: 248 us -> 241 us (0.972)
  blocking collectives: 126 us -> 139 us
  waiting for transfers between devices: 63.2 us -> 50.8 us
  starting transfers between devices: 26.9 us -> 21.7 us
  local copies, waits for them, and re-layouts: 8.14 us -> 4.3 us
    all_gather x0 -> x1, blocking collectives: none -> 12.5 us  [local(): lax.all_gather(got, 'dap', axis=0, tiled=True, axis_index_groups=groups_x)]
    all_to_all x1 -> x0, waiting for transfers between devices: 10.7 us -> none  [spread(): lax.all_to_all(v, 'dap', split_axis=0, concat_axis=0, tiled=True, axis_in...]
    all_to_all x1 -> x0, starting transfers between devices: 5.01 us -> none  [spread(): lax.all_to_all(v, 'dap', split_axis=0, concat_axis=0, tiled=True, axis_in...]
    unnamed x32 -> x22, local copies, waits for them, and re-layouts: 6.89 us -> 3.47 us
    ppermute x2 -> x1, starting transfers between devices: 7.84 us -> 7.63 us  [local(): other = lax.ppermute(got, 'dap', [(d, d ^ 1) for d in range(n)])]
  transfers between devices with their start and end apart: 5 -> 3, of which waited for: 3 -> 2; matrix products, arithmetic and copies ran while one was open for 0% -> 0% of each run, Pallas kernels for 2% -> 2%
where the time goes in v2:
time: 241 us; the launch traced here: 240 us
  blocking collectives  139 us (58%)
  waiting for transfers between devices  50.8 us (21%)
  Pallas kernels  22.4 us (9%)
  starting transfers between devices  21.7 us (9%)
  local copies, waits for them, and re-layouts  4.3 us (2%)
    all_to_all x2, blocking collectives, exchange(): return lax.all_to_all(v, 'dap', split_axis=0, concat_axis=0, tiled=True)  110 us
    all_to_all x2, waiting for transfers between devices, exchange(): return lax.all_to_all(v, 'dap', split_axis=0, concat_axis=0, tiled=True)  50.8 us
    pallas_call x8, Pallas kernels, call(): pl.pallas_call(body, out_shape=outs, in_specs=specs, out_specs=places, sc...  22.4 us
    all_to_all x1, blocking collectives, local(): lax.all_to_all(jnp.broadcast_to(packed[None], (ny,) + packed.shape), 'dap...  16.3 us
    all_to_all x2, starting transfers between devices, exchange(): return lax.all_to_all(v, 'dap', split_axis=0, concat_axis=0, tiled=True)  14 us
    all_gather x1, blocking collectives, local(): lax.all_gather(got, 'dap', axis=0, tiled=True, axis_index_groups=groups_x)  12.5 us
    ppermute x1, starting transfers between devices, local(): other = lax.ppermute(got, 'dap', [(d, d ^ 1) for d in range(n)])  7.63 us
  transfers between devices with their start and end apart: 3, of which 2 were waited for; matrix products, arithmetic and copies ran while one was open for 0% of the time, Pallas kernels for 2%

profile of v2, /device:TPU:1, one launch (start us, length us, event | category | flops | bytes accessed | tf_op | source)
XLA Modules:
  0.0 240.1 jit_solution(4619573627708399949)
XLA Ops:
  0.7 0.7 convert_bitcast_fusion
  1.4 0.7 pad_maximum_fusion
  2.2 16.3 %all_to_all.25 = bf16[8,112,128]{2,1,0:T(8,128)(2,1)S(1)} all-to-all(bf16[8,112,128]{2,1,0:T(8,128)(2,1)S(1)} %broadcast_in_dim.2), channel_id=1, replica_groups={{0,8,16,24,32,40,48,56},{1,9,17,25,33,41,49,57},{2,10,18,26,34,42,50,58..., dimensions={0} | all-to-all | bytes 458752 | tf_op jit(solution)/shard_map/all_to_all | solution.py:231
  18.5 12.5 %all_gather.3.packed_ref = bf16[32,112,128]{2,1,0:T(8,128)(2,1)S(1)} all-gather(bf16[8,112,128]{2,1,0:T(8,128)(2,1)S(1)} %all_to_all.25), channel_id=1, replica_groups={{0,2,4,6},{1,3,5,7},{8,10,12,14},{9,11,13,15},{16,18,20,22},{17,19,21,2..., dimensions={0}, use_global_device_ids=true | all-gather | bytes 1146880 | tf_op jit(solution)/shard_map/all_gather | solution.py:235
  30.9 7.6 %collective-permute-start = (bf16[32,112,128]{2,1,0:T(8,128)(2,1)S(1)}, bf16[32,112,128]{2,1,0:T(8,128)(2,1)S(1)}, u32[]{:S(2)}, u32[]{:S(2)}) collective-permute-start(bf16[32,112,128]{2,1,0:T(8,128)(2,1)S(1)} %all_gather.3.packed_ref), channel_id=1, source_target_pairs={{0,1},{1,0},{2,3},{3,2},{4,5},{5,4},{6,7},{7,6},{8,9},{9,8},{10,11... | collective-permute-start | bytes 2752520 | tf_op jit(solution)/shard_map/ppermute | solution.py:236
  38.6 0.8 slice_bitcast_fusion.6
  39.4 0.0 copy-start.6
  39.4 2.5 %pool_half.1.psum_ref = f32[512,512]{1,0:T(8,128)S(1)} custom-call(bf16[32,112,128]{2,1,0:T(8,128)(2,1)S(1)} %all_gather.3.packed_ref, bf16[128,384]{1,0:T(8,128)(2,1)S(1)} %copy-done.5), custom_call_target="tpu_custom_call" | custom-call | flops 3000000000 | bytes 2000000 | tf_op jit(solution)/shard_map/pool_half/pallas_call | solution.py:200
  41.9 6.5 %first.1 = (bf16[8,384]{1,0:T(8,128)(2,1)}, bf16[8,128,512]{2,1,0:T(8,128)(2,1)S(1)}, bf16[64,32,512]{2,1,0:T(8,128)(2,1)S(1)}) custom-call(s32[1]{0:T(128)} %bitcast.idx_ref, f32[512,512]{1,0:T(8,128)S(1)} %pool_half.1.psum_ref, bf16[32,112,128]{2,1,0:T(8,128)(2,1)S(1)} %collective-permute-done.packed_ref, bf16[128,384]{1,0:T(8,128)(2,1)S(1)} %copy-done.5, ...), custom_call_target="tpu_custom_call" | custom-call | flops 4000000000 | bytes 8000000 | tf_op jit(solution)/shard_map/first/pallas_call | solution.py:200
  48.5 53.9 %all_to_all.26.v = bf16[64,32,512]{2,1,0:T(8,128)(2,1)S(1)} all-to-all(bf16[64,32,512]{2,1,0:T(8,128)(2,1)S(1)} %get-tuple-element.8), channel_id=1, replica_groups=mesh['dp'=8,'dap'=64] {'dap'}, dimensions={0} | all-to-all | bytes 4194304 | tf_op jit(solution)/shard_map/all_to_all | solution.py:255
  102.4 1.7 product0.1
  104.2 7.0 %all-to-all-start.2 = ((bf16[64,16,512]{2,1,0:T(8,128)(2,1)}), bf16[64,16,512]{2,1,0:T(8,128)(2,1)S(1)}, u32[]{:S(2)}, u32[]{:S(2)}) async-start(bf16[64,16,512]{2,1,0:T(8,128)(2,1)} %product0.1), calls=%async_computation.2 | async-start | bytes 2097152 | tf_op jit(solution)/shard_map/all_to_all | solution.py:255
  111.3 1.2 copy-done.1
  112.5 1.3 gating0.1.held_ref
  113.8 25.4 %all-to-all-done.2.x_ref = bf16[64,16,512]{2,1,0:T(8,128)(2,1)S(1)} async-done(((bf16[64,16,512]{2,1,0:T(8,128)(2,1)}), bf16[64,16,512]{2,1,0:T(8,128)(2,1)S(1)}, u32[]{:S(2)}, u32[]{:S(2)}) %all-to-all-start.2) | async-done | bytes 1048608 | tf_op jit(solution)/shard_map/all_to_all | solution.py:255
  139.2 4.7 %middle.1 = (bf16[8,128,512]{2,1,0:T(8,128)(2,1)S(1)}, bf16[64,32,512]{2,1,0:T(8,128)(2,1)S(1)}) custom-call(bf16[64,16,512]{2,1,0:T(8,128)(2,1)S(1)} %all-to-all-done.2.x_ref, bf16[16,128,512]{2,1,0:T(8,128)(2,1)S(1)} %gating0.1.held_ref, bf16[128,128]{1,0:T(8,128)(2,1)S(1)} %get-tuple-element.15.out_ref, f32[1,128]{1,0:T(1,128)S(1)} %get-tuple-element.19.gain_out_ref, ...), custom_call_target="tpu_custom_call" | custom-call | flops 1000000000 | bytes 8000000 | tf_op jit(solution)/shard_map/middle/pallas_call | solution.py:200
  143.9 1.0 copy-done.2
  144.9 55.9 %all_to_all.27.v = bf16[64,32,512]{2,1,0:T(8,128)(2,1)S(1)} all-to-all(bf16[64,32,512]{2,1,0:T(8,128)(2,1)S(1)} %get-tuple-element.10), channel_id=1, replica_groups=mesh['dp'=8,'dap'=64] {'dap'}, dimensions={0} | all-to-all | bytes 4194304 | tf_op jit(solution)/shard_map/all_to_all | solution.py:255
  200.8 1.7 product1.1
  202.5 7.0 %all-to-all-start.4 = ((bf16[64,16,512]{2,1,0:T(8,128)(2,1)}), bf16[64,16,512]{2,1,0:T(8,128)(2,1)S(1)}, u32[]{:S(2)}, u32[]{:S(2)}) async-start(bf16[64,16,512]{2,1,0:T(8,128)(2,1)} %product1.1), calls=%async_computation.4 | async-start | bytes 2097152 | tf_op jit(solution)/shard_map/all_to_all | solution.py:255
  209.5 1.2 copy-done.3
  210.8 1.3 gating1.1.held_ref
  212.1 25.4 %all-to-all-done.4.x_ref = bf16[64,16,512]{2,1,0:T(8,128)(2,1)S(1)} async-done(((bf16[64,16,512]{2,1,0:T(8,128)(2,1)}), bf16[64,16,512]{2,1,0:T(8,128)(2,1)S(1)}, u32[]{:S(2)}, u32[]{:S(2)}) %all-to-all-start.4) | async-done | bytes 1048608 | tf_op jit(solution)/shard_map/all_to_all | solution.py:255
  237.5 2.6 %last.1 = bf16[8,512,128]{2,1,0:T(8,128)(2,1)} custom-call(bf16[64,16,512]{2,1,0:T(8,128)(2,1)S(1)} %all-to-all-done.4.x_ref, bf16[16,128,512]{2,1,0:T(8,128)(2,1)S(1)} %gating1.1.held_ref, bf16[128,128]{1,0:T(8,128)(2,1)S(1)} %get-tuple-element.14.out_ref, f32[1,128]{1,0:T(1,128)S(1)} %get-tuple-element.18.gain_out_ref), custom_call_target="tpu_custom_call" | custom-call | flops 200000000 | bytes 5000000 | tf_op jit(solution)/shard_map/last/pallas_call | solution.py:200
  (24 shorter events, 0.1 us)
Async XLA Ops:
  0.6 38.7 %copy-start.8 = (bf16[2,128,512]{2,1,0:T(8,128)(2,1)S(1)}, bf16[2,128,512]{2,1,0:T(8,128)(2,1)}, u32[]{:S(2)}) copy-start(bf16[2,128,512]{2,1,0:T(8,128)(2,1)} %param.16) | copy-start | bytes 786436
  0.6 38.7 %copy-start.5 = (bf16[128,384]{1,0:T(8,128)(2,1)S(1)}, bf16[128,384]{1,0:T(8,128)(2,1)}, u32[]{:S(2)}) copy-start(bf16[128,384]{1,0:T(8,128)(2,1)} %weight_ref.3) | copy-start | bytes 294916
  30.9 11.0 %collective-permute-start = (bf16[32,112,128]{2,1,0:T(8,128)(2,1)S(1)}, bf16[32,112,128]{2,1,0:T(8,128)(2,1)S(1)}, u32[]{:S(2)}, u32[]{:S(2)}) collective-permute-start(bf16[32,112,128]{2,1,0:T(8,128)(2,1)S(1)} %all_gather.3.packed_ref), channel_id=1, source_target_pairs={{0,1},{1,0},{2,3},{3,2},{4,5},{5,4},{6,7},{7,6},{8,9},{9,8},{10,11... | collective-permute-start | bytes 2752520 | tf_op jit(solution)/shard_map/ppermute | solution.py:236
  39.4 2.5 %copy-start.4 = (bf16[8,512,128]{2,1,0:T(8,128)(2,1)S(1)}, bf16[8,512,128]{2,1,0:T(8,128)(2,1)}, u32[]{:S(2)}) copy-start(bf16[8,512,128]{2,1,0:T(8,128)(2,1)} %pair_ref.1) | copy-start | bytes 3145732
  39.4 2.5 %copy-start.6 = (bf16[384,128]{1,0:T(8,128)(2,1)S(1)}, bf16[384,128]{1,0:T(8,128)(2,1)}, u32[]{:S(2)}) copy-start(bf16[384,128]{1,0:T(8,128)(2,1)} %wl_ref.1) | copy-start | bytes 294916
  39.4 2.5 %copy-start.7 = (bf16[384,128]{1,0:T(8,128)(2,1)S(1)}, bf16[384,128]{1,0:T(8,128)(2,1)}, u32[]{:S(2)}) copy-start(bf16[384,128]{1,0:T(8,128)(2,1)} %wr_ref.1) | copy-start | bytes 294916
  48.5 53.9 %copy-start = (bf16[8,128,512]{2,1,0:T(8,128)(2,1)}, bf16[8,128,512]{2,1,0:T(8,128)(2,1)S(1)}, u32[]{:S(2)}) copy-start(bf16[8,128,512]{2,1,0:T(8,128)(2,1)S(1)} %get-tuple-element.9.z_in) | copy-start | bytes 3145732
  102.4 8.8 %copy-start.9 = (bf16[2,128,128]{2,1,0:T(8,128)(2,1)S(1)}, bf16[2,128,128]{2,1,0:T(8,128)(2,1)}, u32[]{:S(2)}) copy-start(bf16[2,128,128]{2,1,0:T(8,128)(2,1)} %param.17) | copy-start | bytes 196612
  102.4 8.8 %copy-start.10 = (bf16[2,128,128]{2,1,0:T(8,128)(2,1)S(1)}, bf16[2,128,128]{2,1,0:T(8,128)(2,1)}, u32[]{:S(2)}) copy-start(bf16[2,128,128]{2,1,0:T(8,128)(2,1)} %param.18) | copy-start | bytes 196612
  104.2 35.0 %all-to-all-start.2 = ((bf16[64,16,512]{2,1,0:T(8,128)(2,1)}), bf16[64,16,512]{2,1,0:T(8,128)(2,1)S(1)}, u32[]{:S(2)}, u32[]{:S(2)}) async-start(bf16[64,16,512]{2,1,0:T(8,128)(2,1)} %product0.1), calls=%async_computation.2 | async-start | bytes 2097152 | tf_op jit(solution)/shard_map/all_to_all | solution.py:255
  111.2 1.2 copy-start.1
  143.9 1.0 copy-start.2
  202.5 35.0 %all-to-all-start.4 = ((bf16[64,16,512]{2,1,0:T(8,128)(2,1)}), bf16[64,16,512]{2,1,0:T(8,128)(2,1)S(1)}, u32[]{:S(2)}, u32[]{:S(2)}) async-start(bf16[64,16,512]{2,1,0:T(8,128)(2,1)} %product1.1), calls=%async_computation.4 | async-start | bytes 2097152 | tf_op jit(solution)/shard_map/all_to_all | solution.py:255
  209.5 1.2 copy-start.3

commit v3 on v2

--- a/solution.py
+++ b/solution.py
@@ -9,7 +9,6 @@
 F32, BF16 = jnp.float32, jnp.bfloat16
 NT = (((1,), (1,)), ((), ()))
 TN = (((0,), (0,)), ((), ()))
-VMEM_LIMIT = 16 * 2**20
 
 
 def mm(a, b, dims=(((1,), (0,)), ((), ()))):
@@ -31,6 +30,24 @@
     centred = x - jnp.sum(x, axis=0, keepdims=True) * (1.0 / n)
     variance = jnp.sum(centred * centred, axis=0, keepdims=True) * (1.0 / n)
     return centred * lax.rsqrt(variance + EPS) * gain
+
+
+def pack_kernel(feats_in, tok_in, out_ref, feats_ref, tok_ref, sem_feats, sem_tok):
+    copies = [
+        pltpu.make_async_copy(feats_in, feats_ref, sem_feats),
+        pltpu.make_async_copy(tok_in, tok_ref, sem_tok),
+    ]
+    for copy in copies:
+        copy.start()
+    for copy in copies:
+        copy.wait()
+    atoms, c = feats_ref.shape
+    tok = jnp.concatenate([tok_ref[...], jnp.zeros((1, c - atoms), jnp.int32)], axis=1)
+    row = lax.broadcasted_iota(jnp.int32, (16, c), 0)
+    codes = jnp.where(row == 0, tok >> 5, jnp.where(row == 1, tok & 31, 0))
+    block = jnp.concatenate([feats_ref[...], codes.astype(F32).astype(BF16)], axis=0)
+    for k in range(out_ref.shape[0]):
+        out_ref[k] = block
 
 
 def pool(packed_ref, weight_ref, tokens):
@@ -53,10 +70,6 @@
     return total
 
 
-def pool_kernel(packed_ref, weight_ref, out_ref):
-    out_ref[...] = pool(packed_ref, weight_ref, out_ref.shape[0])
-
-
 def put_row(s_ref, r, value):
     for t in range(s_ref.shape[0]):
         s_ref[t, pl.ds(r, value.shape[0], stride=8), :] = value[:, t * 128 : t * 128 + 128]
@@ -73,11 +86,11 @@
         s_ref[t] = x_ref[:, :, t * 128 : t * 128 + 128].reshape(-1, 128).astype(F32)
 
 
-def operands(normed, proj_t, r, sa_ref, sb_ref):
+def operands(normed, half_proj_t, r, sa_ref, sb_ref):
     c = normed.shape[0]
-    p = mm(proj_t, normed)
-    put_row(sa_ref, r, sigmoid(p[:c]) * p[c : 2 * c])
-    put_row(sb_ref, r, sigmoid(p[2 * c : 3 * c]) * p[3 * c :])
+    p = mm(half_proj_t, normed)
+    put_row(sa_ref, r, jnp.tanh(p[:c]) * p[c : 2 * c] + p[c : 2 * c])
+    put_row(sb_ref, r, jnp.tanh(p[2 * c : 3 * c]) * p[3 * c :] + p[3 * c :])
 
 
 def pack(sa_ref, sb_ref, u_ref):
@@ -90,12 +103,12 @@
 
 
 def first_kernel(
-    idx_ref, psum_ref, packed_ref, weight_ref, wl_ref, wr_ref, pair_ref, proj_ref, gain_ref,
+    idx_ref, packed_ref, weight_ref, wl_ref, wr_ref, pair_ref, proj_ref, gain_ref,
     single_ref, z_out, u_ref, ts_ref, sa_ref, sb_ref, z_ref, sem,
 ):
     rows, tokens, c = pair_ref.shape
     cs = wl_ref.shape[0]
-    total = psum_ref[...] + pool(packed_ref, weight_ref, tokens)
+    total = pool(packed_ref, weight_ref, tokens)
     counts = total[:, cs:]
     single = jnp.concatenate(
         [total[:, at : at + 128] / counts for at in range(0, cs, 128)], axis=1
@@ -107,13 +120,13 @@
     single_ref[...] = own
     left = mm(own, wl_ref[...]).astype(BF16).astype(F32)
     gain = column(gain_ref[...], tokens)
-    proj_t = proj_ref[...].T
+    half_proj_t = (proj_ref[...].astype(F32) * 0.5).astype(BF16).T
     for r in range(rows):
         z = (pair_ref[r].astype(F32) + left[r : r + 1, :] + right).astype(BF16)
         z = z.T
         z_ref[r] = z
         normed = norm_rows(z.astype(F32), gain).astype(BF16)
-        operands(normed, proj_t, r, sa_ref, sb_ref)
+        operands(normed, half_proj_t, r, sa_ref, sb_ref)
     copy = pltpu.make_async_copy(z_ref, z_out, sem)
     copy.start()
     pack(sa_ref, sb_ref, u_ref)
@@ -164,12 +177,12 @@
     gain_out = column(gain_out_ref[...], tokens)
     gain_in = column(gain_in_ref[...], tokens)
     out_t = out_ref[...].T
-    proj_t = proj_ref[...].T
+    half_proj_t = (proj_ref[...].astype(F32) * 0.5).astype(BF16).T
     for r in range(rows):
         z = update_row(r, s_ref, out_t, gain_out, held_ref)
         z_ref[r] = z
         normed = norm_rows(z.astype(F32), gain_in).astype(BF16)
-        operands(normed, proj_t, r, sa_ref, sb_ref)
+        operands(normed, half_proj_t, r, sa_ref, sb_ref)
     copy = pltpu.make_async_copy(z_ref, z_out, sem)
     copy.start()
     pack(sa_ref, sb_ref, u_ref)
@@ -186,7 +199,9 @@
         pair_ref[r] = z.T
 
 
-def call(body, outs, args, scratch=(), name=None, flops=0, bytes_=0, far_in=(), far_out=()):
+def call(
+    body, outs, args, scratch=(), name=None, flops=0, bytes_=0, far_in=(), far_out=(), vmem=16
+):
     specs = [
         pl.BlockSpec(
             memory_space=pltpu.HBM if k in far_in else pltpu.SMEM if a.ndim == 1 else pltpu.VMEM
@@ -203,7 +218,7 @@
         in_specs=specs,
         out_specs=places,
         scratch_shapes=list(scratch),
-        compiler_params=pltpu.CompilerParams(vmem_limit_bytes=VMEM_LIMIT),
+        compiler_params=pltpu.CompilerParams(vmem_limit_bytes=vmem * 2**20),
         cost_estimate=pl.CostEstimate(flops=flops, bytes_accessed=bytes_, transcendentals=0),
         name=name,
     )(*args)
@@ -222,22 +237,17 @@
 
     ny, nx = 8, 4
     groups_y = [[(y * nx + x) * 2 + k for y in range(ny)] for x in range(nx) for k in range(2)]
-    groups_x = [[(y * nx + x) * 2 + k for x in range(nx)] for y in range(ny) for k in range(2)]
-    tok = atom_token.reshape(1, atoms)
-    tok = jnp.concatenate([tok // 32, tok % 32], axis=0).astype(BF16)
-    tok = jnp.pad(tok, ((0, 14), (0, c - atoms)))
-    packed = jnp.concatenate([atom_feats, tok], axis=0)
-
+    groups_xk = [[y * nx * 2 + k for k in range(nx * 2)] for y in range(ny)]
+    (packed,) = call(
+        pack_kernel, (shape((ny, atoms + 16, c), BF16),), (atom_feats, atom_token.reshape(1, atoms)),
+        [pltpu.VMEM((atoms, c), BF16), pltpu.VMEM((1, atoms), jnp.int32)]
+        + [pltpu.SemaphoreType.DMA] * 2,
+        name="packed_atoms", bytes_=300_000, far_in=(0, 1), vmem=60,
+    )
     got = lax.all_to_all(
-        jnp.broadcast_to(packed[None], (ny,) + packed.shape), "dap",
-        split_axis=0, concat_axis=0, tiled=True, axis_index_groups=groups_y,
-    )
-    got = lax.all_gather(got, "dap", axis=0, tiled=True, axis_index_groups=groups_x)
-    other = lax.ppermute(got, "dap", [(d, d ^ 1) for d in range(n)])
-    (psum,) = call(
-        pool_kernel, (shape((tokens, cs + 128), F32),), (got, atom_weight),
-        name="pool_half", flops=3_000_000_000, bytes_=2_000_000,
-    )
+        packed, "dap", split_axis=0, concat_axis=0, tiled=True, axis_index_groups=groups_y
+    )
+    got = lax.all_gather(got, "dap", axis=0, tiled=True, axis_index_groups=groups_xk)
     big = pltpu.VMEM((tokens // 128, rows * c, 128), F32)
     held = [pltpu.VMEM((rows, c, tokens), BF16), pltpu.SemaphoreType.DMA]
     z_shape = shape((rows, c, tokens), BF16)
@@ -245,10 +255,10 @@
     token_single, z, sent = call(
         first_kernel,
         (shape((rows, cs), BF16), z_shape, sent_shape),
-        (me, psum, other, atom_weight, left_weight, right_weight, pair_map,
+        (me, got, atom_weight, left_weight, right_weight, pair_map,
          tri_proj[0], tri_gains[0, 0:1]),
         [pltpu.VMEM((tokens, cs), F32), big, big, *held],
-        name="first", flops=4_000_000_000, bytes_=8_000_000, far_out=(1,),
+        name="first", flops=4_000_000_000, bytes_=8_000_000, far_out=(1,), vmem=32,
     )
 
     def exchange(v):
@@ -273,7 +283,7 @@
                 middle_kernel, (z_shape, sent_shape),
                 (prod, kept, tri_out[0], tri_gains[0, 1:2], tri_proj[1], tri_gains[1, 0:1]),
                 [big, big, big, *held],
-                name="middle", flops=1_000_000_000, bytes_=8_000_000, far_out=(0,),
+                name="middle", flops=1_000_000_000, bytes_=8_000_000, far_out=(0,), vmem=32,
             )
         else:
             (pair,) = call(

time: 241 us -> 275 us (1.14)
  waiting for transfers between devices: 50.8 us -> 81.7 us
  between operations: 0.85 us -> 14.2 us
  blocking collectives: 139 us -> 131 us
  starting transfers between devices: 21.7 us -> 14.1 us
  local copies, waits for them, and re-layouts: 4.3 us -> 9.61 us
    all_gather x0 -> x1, waiting for transfers between devices: none -> 30.9 us  [local(): lax.all_gather(got, 'dap', axis=0, tiled=True, axis_index_groups=groups_xk)]
    all_gather x1 -> x0, blocking collectives: 12.5 us -> none  [local(): lax.all_gather(got, 'dap', axis=0, tiled=True, axis_index_groups=groups_x)]
    ppermute x1 -> x0, starting transfers between devices: 7.63 us -> none  [local(): other = lax.ppermute(got, 'dap', [(d, d ^ 1) for d in range(n)])]
    unnamed x22, local copies, waits for them, and re-layouts: 3.47 us -> 7.85 us
    all_to_all x2, blocking collectives: 110 us -> 114 us  [exchange(): return lax.all_to_all(v, 'dap', split_axis=0, concat_axis=0, tiled=True)]
  transfers between devices with their start and end apart: 3 -> 3, of which waited for: 2 -> 3; matrix products, arithmetic and copies ran while one was open for 0% -> 1% of each run, Pallas kernels for 2% -> 1%
where the time goes in v3:
time: 275 us; the launch traced here: 274 us
  blocking collectives  131 us (48%)
  waiting for transfers between devices  81.7 us (30%)
  Pallas kernels  23.4 us (9%)
  between operations  14.2 us (5%)
  starting transfers between devices  14.1 us (5%)
  local copies, waits for them, and re-layouts  9.61 us (3%)
    all_to_all x2, blocking collectives, exchange(): return lax.all_to_all(v, 'dap', split_axis=0, concat_axis=0, tiled=True)  114 us
    all_to_all x2, waiting for transfers between devices, exchange(): return lax.all_to_all(v, 'dap', split_axis=0, concat_axis=0, tiled=True)  50.8 us
    all_gather x1, waiting for transfers between devices, local(): lax.all_gather(got, 'dap', axis=0, tiled=True, axis_index_groups=groups_xk)  30.9 us
    pallas_call x8, Pallas kernels, call(): pl.pallas_call(body, out_shape=outs, in_specs=specs, out_specs=places, sc...  23.4 us
    all_to_all x1, blocking collectives, local(): lax.all_to_all(packed, 'dap', split_axis=0, concat_axis=0, tiled=True, ax...  16.8 us
    all_to_all x2, starting transfers between devices, exchange(): return lax.all_to_all(v, 'dap', split_axis=0, concat_axis=0, tiled=True)  14 us
    unnamed x22, local copies, waits for them, and re-layouts  7.85 us
  transfers between devices with their start and end apart: 3, of which 3 were waited for; matrix products, arithmetic and copies ran while one was open for 1% of the time, Pallas kernels for 1%

profile of v3, /device:TPU:1, one launch (start us, length us, event | category | flops | bytes accessed | tf_op | source)
XLA Modules:
  0.0 274.0 jit_solution(13951520275972019670)
XLA Ops:
  7.2 1.5 packed_atoms.1
  8.7 16.8 %all_to_all.25 = bf16[8,112,128]{2,1,0:T(8,128)(2,1)} all-to-all(bf16[8,112,128]{2,1,0:T(8,128)(2,1)} %packed_atoms.1), channel_id=1, replica_groups={{0,8,16,24,32,40,48,56},{1,9,17,25,33,41,49,57},{2,10,18,26,34,42,50,58..., dimensions={0} | all-to-all | bytes 458752 | tf_op jit(solution)/shard_map/all_to_all | solution.py:247
  26.3 1.0 slice_bitcast_fusion
  27.2 30.9 %all-gather.2.cloned.1.call-done.packed_ref = bf16[64,112,128]{2,1,0:T(8,128)(2,1)} async-done(((bf16[8,112,128]{2,1,0:T(8,128)(2,1)}), bf16[64,112,128]{2,1,0:T(8,128)(2,1)}) %all-gather.2.cloned.1.call-update) | async-done | bytes 1835024 | tf_op jit(solution)/shard_map/all_gather | solution.py:250
  58.2 1.5 copy-done.4
  59.7 1.2 copy-done.5
  60.9 0.9 copy-done.6
  61.8 0.9 copy-done.7
  62.7 0.9 copy-done.8
  63.6 8.5 %first.1 = (bf16[8,384]{1,0:T(8,128)(2,1)}, bf16[8,128,512]{2,1,0:T(8,128)(2,1)S(1)}, bf16[64,32,512]{2,1,0:T(8,128)(2,1)S(1)}) custom-call(s32[1]{0:T(128)} %bitcast.idx_ref, bf16[64,112,128]{2,1,0:T(8,128)(2,1)S(1)} %copy-done.4, bf16[128,384]{1,0:T(8,128)(2,1)S(1)} %copy-done.6, bf16[384,128]{1,0:T(8,128)(2,1)S(1)} %copy-done.7, ...), custom_call_target="tpu_custom_call" | custom-call | flops 4000000000 | bytes 8000000 | tf_op jit(solution)/shard_map/first/pallas_call | solution.py:215
  72.1 58.3 %all_to_all.26.v = bf16[64,32,512]{2,1,0:T(8,128)(2,1)S(1)} all-to-all(bf16[64,32,512]{2,1,0:T(8,128)(2,1)S(1)} %get-tuple-element.8), channel_id=1, replica_groups=mesh['dp'=8,'dap'=64] {'dap'}, dimensions={0} | all-to-all | bytes 4194304 | tf_op jit(solution)/shard_map/all_to_all | solution.py:265
  130.4 1.7 product0.1
  132.1 7.0 %all-to-all-start.2 = ((bf16[64,16,512]{2,1,0:T(8,128)(2,1)}), bf16[64,16,512]{2,1,0:T(8,128)(2,1)S(1)}, u32[]{:S(2)}, u32[]{:S(2)}) async-start(bf16[64,16,512]{2,1,0:T(8,128)(2,1)} %product0.1), calls=%async_computation.2 | async-start | bytes 2097152 | tf_op jit(solution)/shard_map/all_to_all | solution.py:265
  139.2 1.2 copy-done.1
  140.4 1.3 gating0.1.held_ref
  141.8 25.4 %all-to-all-done.2.x_ref = bf16[64,16,512]{2,1,0:T(8,128)(2,1)S(1)} async-done(((bf16[64,16,512]{2,1,0:T(8,128)(2,1)}), bf16[64,16,512]{2,1,0:T(8,128)(2,1)S(1)}, u32[]{:S(2)}, u32[]{:S(2)}) %all-to-all-start.2) | async-done | bytes 1048608 | tf_op jit(solution)/shard_map/all_to_all | solution.py:265
  167.1 4.7 %middle.1 = (bf16[8,128,512]{2,1,0:T(8,128)(2,1)S(1)}, bf16[64,32,512]{2,1,0:T(8,128)(2,1)S(1)}) custom-call(bf16[64,16,512]{2,1,0:T(8,128)(2,1)S(1)} %all-to-all-done.2.x_ref, bf16[16,128,512]{2,1,0:T(8,128)(2,1)S(1)} %gating0.1.held_ref, bf16[128,128]{1,0:T(8,128)(2,1)S(1)} %get-tuple-element.15.out_ref, f32[1,128]{1,0:T(1,128)S(1)} %get-tuple-element.19.gain_out_ref, ...), custom_call_target="tpu_custom_call" | custom-call | flops 1000000000 | bytes 8000000 | tf_op jit(solution)/shard_map/middle/pallas_call | solution.py:215
  171.9 55.9 %all_to_all.27.v = bf16[64,32,512]{2,1,0:T(8,128)(2,1)S(1)} all-to-all(bf16[64,32,512]{2,1,0:T(8,128)(2,1)S(1)} %get-tuple-element.10), channel_id=1, replica_groups=mesh['dp'=8,'dap'=64] {'dap'}, dimensions={0} | all-to-all | bytes 4194304 | tf_op jit(solution)/shard_map/all_to_all | solution.py:265
  227.8 1.7 product1.1
  229.6 7.0 %all-to-all-start.4 = ((bf16[64,16,512]{2,1,0:T(8,128)(2,1)}), bf16[64,16,512]{2,1,0:T(8,128)(2,1)S(1)}, u32[]{:S(2)}, u32[]{:S(2)}) async-start(bf16[64,16,512]{2,1,0:T(8,128)(2,1)} %product1.1), calls=%async_computation.4 | async-start | bytes 2097152 | tf_op jit(solution)/shard_map/all_to_all | solution.py:265
  236.6 1.2 copy-done.3
  237.8 1.3 gating1.1.held_ref
  239.1 25.4 %all-to-all-done.4.x_ref = bf16[64,16,512]{2,1,0:T(8,128)(2,1)S(1)} async-done(((bf16[64,16,512]{2,1,0:T(8,128)(2,1)}), bf16[64,16,512]{2,1,0:T(8,128)(2,1)S(1)}, u32[]{:S(2)}, u32[]{:S(2)}) %all-to-all-start.4) | async-done | bytes 1048608 | tf_op jit(solution)/shard_map/all_to_all | solution.py:265
  264.6 2.6 last.1
  (20 shorter events, 0.9 us)
Async XLA Ops:
  7.2 51.0 %all-gather.2.cloned.1.call-start = ((), (), s32[]{:S(2)}) async-start(), calls=%async_computation.5 | async-start | bytes 2064384 | tf_op jit(solution)/shard_map/all_gather | solution.py:250
  58.2 1.5 copy-start.4
  59.7 1.2 copy-start.5
  60.9 0.9 copy-start.6
  61.8 0.9 copy-start.7
  62.7 0.9 copy-start.8
  72.1 58.3 %copy-start = (bf16[8,128,512]{2,1,0:T(8,128)(2,1)}, bf16[8,128,512]{2,1,0:T(8,128)(2,1)S(1)}, u32[]{:S(2)}) copy-start(bf16[8,128,512]{2,1,0:T(8,128)(2,1)S(1)} %get-tuple-element.9.z_in) | copy-start | bytes 3145732
  130.4 8.8 %copy-start.9 = (bf16[2,128,128]{2,1,0:T(8,128)(2,1)S(1)}, bf16[2,128,128]{2,1,0:T(8,128)(2,1)}, u32[]{:S(2)}) copy-start(bf16[2,128,128]{2,1,0:T(8,128)(2,1)} %param.17) | copy-start | bytes 196612
  130.4 8.8 %copy-start.10 = (bf16[2,128,128]{2,1,0:T(8,128)(2,1)S(1)}, bf16[2,128,128]{2,1,0:T(8,128)(2,1)}, u32[]{:S(2)}) copy-start(bf16[2,128,128]{2,1,0:T(8,128)(2,1)} %param.18) | copy-start | bytes 196612
  132.1 35.0 %all-to-all-start.2 = ((bf16[64,16,512]{2,1,0:T(8,128)(2,1)}), bf16[64,16,512]{2,1,0:T(8,128)(2,1)S(1)}, u32[]{:S(2)}, u32[]{:S(2)}) async-start(bf16[64,16,512]{2,1,0:T(8,128)(2,1)} %product0.1), calls=%async_computation.2 | async-start | bytes 2097152 | tf_op jit(solution)/shard_map/all_to_all | solution.py:265
  139.2 1.2 copy-start.1
  171.9 55.9 %copy-start.2 = (bf16[8,128,512]{2,1,0:T(8,128)(2,1)}, bf16[8,128,512]{2,1,0:T(8,128)(2,1)S(1)}, u32[]{:S(2)}) copy-start(bf16[8,128,512]{2,1,0:T(8,128)(2,1)S(1)} %get-tuple-element.11.z_in) | copy-start | bytes 3145732
  229.6 35.0 %all-to-all-start.4 = ((bf16[64,16,512]{2,1,0:T(8,128)(2,1)}), bf16[64,16,512]{2,1,0:T(8,128)(2,1)S(1)}, u32[]{:S(2)}, u32[]{:S(2)}) async-start(bf16[64,16,512]{2,1,0:T(8,128)(2,1)} %product1.1), calls=%async_computation.4 | async-start | bytes 2097152 | tf_op jit(solution)/shard_map/all_to_all | solution.py:265
  236.6 1.2 copy-start.3
Sparse Core Ops, SparseCore 0:
  25.6 32.4 all-gather.1

commit v4 on v3

--- a/solution.py
+++ b/solution.py
@@ -1,3 +1,5 @@
+import functools
+
 import jax
 import jax.numpy as jnp
 from jax import lax
@@ -6,6 +8,7 @@
 from jax.sharding import PartitionSpec as P
 
 EPS = 1e-05
+GROUP = 4
 F32, BF16 = jnp.float32, jnp.bfloat16
 NT = (((1,), (1,)), ((), ()))
 TN = (((0,), (0,)), ((), ()))
@@ -70,6 +73,10 @@
     return total
 
 
+def pool_kernel(packed_ref, weight_ref, out_ref):
+    out_ref[...] = pool(packed_ref, weight_ref, out_ref.shape[0])
+
+
 def put_row(s_ref, r, value):
     for t in range(s_ref.shape[0]):
         s_ref[t, pl.ds(r, value.shape[0], stride=8), :] = value[:, t * 128 : t * 128 + 128]
@@ -86,11 +93,14 @@
         s_ref[t] = x_ref[:, :, t * 128 : t * 128 + 128].reshape(-1, 128).astype(F32)
 
 
-def operands(normed, half_proj_t, r, sa_ref, sb_ref):
+def operands(normed, half_proj_t, at, sa_ref, sb_ref):
     c = normed.shape[0]
-    p = mm(half_proj_t, normed)
-    put_row(sa_ref, r, jnp.tanh(p[:c]) * p[c : 2 * c] + p[c : 2 * c])
-    put_row(sb_ref, r, jnp.tanh(p[2 * c : 3 * c]) * p[3 * c :] + p[3 * c :])
+    length = sa_ref.shape[0] * 128
+    for s_ref, block in ((sa_ref, 0), (sb_ref, 2)):
+        p = mm(half_proj_t[block * c : (block + 2) * c], normed)
+        p = jnp.tanh(p[:c]) * p[c:] + p[c:]
+        for k in range(normed.shape[1] // length):
+            put_row(s_ref, at + k, p[:, k * length : (k + 1) * length])
 
 
 def pack(sa_ref, sb_ref, u_ref):
@@ -103,12 +113,12 @@
 
 
 def first_kernel(
-    idx_ref, packed_ref, weight_ref, wl_ref, wr_ref, pair_ref, proj_ref, gain_ref,
+    idx_ref, psum_ref, packed_ref, weight_ref, wl_ref, wr_ref, pair_ref, proj_ref, gain_ref,
     single_ref, z_out, u_ref, ts_ref, sa_ref, sb_ref, z_ref, sem,
 ):
     rows, tokens, c = pair_ref.shape
     cs = wl_ref.shape[0]
-    total = pool(packed_ref, weight_ref, tokens)
+    total = psum_ref[...] + pool(packed_ref, weight_ref, tokens)
     counts = total[:, cs:]
     single = jnp.concatenate(
         [total[:, at : at + 128] / counts for at in range(0, cs, 128)], axis=1
@@ -119,26 +129,30 @@
     own = ts_ref[pl.ds(start, 8), :].astype(BF16)
     single_ref[...] = own
     left = mm(own, wl_ref[...]).astype(BF16).astype(F32)
-    gain = column(gain_ref[...], tokens)
-    half_proj_t = (proj_ref[...].astype(F32) * 0.5).astype(BF16).T
-    for r in range(rows):
-        z = (pair_ref[r].astype(F32) + left[r : r + 1, :] + right).astype(BF16)
-        z = z.T
-        z_ref[r] = z
+    gain = column(gain_ref[0, 0:1, :], GROUP * tokens)
+    half_proj_t = (proj_ref[0].astype(F32) * 0.5).astype(BF16).T
+    for at in range(0, rows, GROUP):
+        some = range(at, at + GROUP)
+        z = [
+            (pair_ref[r].astype(F32) + left[r : r + 1, :] + right).astype(BF16).T for r in some
+        ]
+        for r, row in zip(some, z):
+            z_ref[r] = row
+        z = jnp.concatenate(z, axis=1)
         normed = norm_rows(z.astype(F32), gain).astype(BF16)
-        operands(normed, half_proj_t, r, sa_ref, sb_ref)
+        operands(normed, half_proj_t, at, sa_ref, sb_ref)
     copy = pltpu.make_async_copy(z_ref, z_out, sem)
     copy.start()
     pack(sa_ref, sb_ref, u_ref)
     copy.wait()
 
 
-def gate_kernel(z_in, gate_ref, gain_ref, out_ref, z_ref, sem):
+def gate_kernel(layer, z_in, gate_ref, gain_ref, out_ref, z_ref, sem):
     rows, _, tokens = z_ref.shape
     copy = pltpu.make_async_copy(z_in, z_ref, sem)
     copy.start()
-    gate_t = gate_ref[...].T
-    gain = column(gain_ref[...], tokens)
+    gate_t = gate_ref[layer].T
+    gain = column(gain_ref[layer, 0:1, :], tokens)
     copy.wait()
     for r in range(rows):
         z = z_ref[r]
@@ -159,44 +173,48 @@
     r_ref[...] = jnp.concatenate(out, axis=1).astype(BF16)
 
 
-def update_row(r, s_ref, out_t, gain, held_ref):
-    c = out_t.shape[0]
-    x = get_row(s_ref, r, c)
+def update_rows(some, s_ref, out_t, gain, held_ref):
+    c, rows = out_t.shape[0], held_ref.shape[0] // 2
+    x = jnp.concatenate([get_row(s_ref, r, c) for r in some], axis=1)
     normed = norm_rows(x, gain).astype(BF16)
-    rows = held_ref.shape[0] // 2
-    gating, z = held_ref[r].astype(F32), held_ref[rows + r].astype(F32)
+    gating = jnp.concatenate([held_ref[r].astype(F32) for r in some], axis=1)
+    z = jnp.concatenate([held_ref[rows + r].astype(F32) for r in some], axis=1)
     return (z + gating * mm(out_t, normed)).astype(BF16)
 
 
 def middle_kernel(
-    x_ref, held_ref, out_ref, gain_out_ref, proj_ref, gain_in_ref,
+    x_ref, held_ref, out_ref, proj_ref, gain_ref,
     z_out, u_ref, s_ref, sa_ref, sb_ref, z_ref, sem,
 ):
     rows, c, tokens = z_ref.shape
     fill(s_ref, x_ref)
-    gain_out = column(gain_out_ref[...], tokens)
-    gain_in = column(gain_in_ref[...], tokens)
-    out_t = out_ref[...].T
-    half_proj_t = (proj_ref[...].astype(F32) * 0.5).astype(BF16).T
-    for r in range(rows):
-        z = update_row(r, s_ref, out_t, gain_out, held_ref)
-        z_ref[r] = z
+    gain_out = column(gain_ref[0, 1:2, :], GROUP * tokens)
+    gain_in = column(gain_ref[1, 0:1, :], GROUP * tokens)
+    out_t = out_ref[0].T
+    half_proj_t = (proj_ref[1].astype(F32) * 0.5).astype(BF16).T
+    for at in range(0, rows, GROUP):
+        some = range(at, at + GROUP)
+        z = update_rows(some, s_ref, out_t, gain_out, held_ref)
+        for k, r in enumerate(some):
+            z_ref[r] = z[:, k * tokens : (k + 1) * tokens]
         normed = norm_rows(z.astype(F32), gain_in).astype(BF16)
-        operands(normed, half_proj_t, r, sa_ref, sb_ref)
+        operands(normed, half_proj_t, at, sa_ref, sb_ref)
     copy = pltpu.make_async_copy(z_ref, z_out, sem)
     copy.start()
     pack(sa_ref, sb_ref, u_ref)
     copy.wait()
 
 
-def last_kernel(x_ref, held_ref, out_ref, gain_out_ref, pair_ref, s_ref):
+def last_kernel(x_ref, held_ref, out_ref, gain_ref, pair_ref, s_ref):
     rows, tokens, c = pair_ref.shape
     fill(s_ref, x_ref)
-    gain_out = column(gain_out_ref[...], tokens)
-    out_t = out_ref[...].T
-    for r in range(rows):
-        z = update_row(r, s_ref, out_t, gain_out, held_ref)
-        pair_ref[r] = z.T
+    gain_out = column(gain_ref[1, 1:2, :], GROUP * tokens)
+    out_t = out_ref[1].T
+    for at in range(0, rows, GROUP):
+        some = range(at, at + GROUP)
+        z = update_rows(some, s_ref, out_t, gain_out, held_ref)
+        for k, r in enumerate(some):
+            pair_ref[r] = z[:, k * tokens : (k + 1) * tokens].T
 
 
 def call(
@@ -237,7 +255,7 @@
 
     ny, nx = 8, 4
     groups_y = [[(y * nx + x) * 2 + k for y in range(ny)] for x in range(nx) for k in range(2)]
-    groups_xk = [[y * nx * 2 + k for k in range(nx * 2)] for y in range(ny)]
+    groups_x = [[(y * nx + x) * 2 + k for x in range(nx)] for y in range(ny) for k in range(2)]
     (packed,) = call(
         pack_kernel, (shape((ny, atoms + 16, c), BF16),), (atom_feats, atom_token.reshape(1, atoms)),
         [pltpu.VMEM((atoms, c), BF16), pltpu.VMEM((1, atoms), jnp.int32)]
@@ -247,7 +265,12 @@
     got = lax.all_to_all(
         packed, "dap", split_axis=0, concat_axis=0, tiled=True, axis_index_groups=groups_y
     )
-    got = lax.all_gather(got, "dap", axis=0, tiled=True, axis_index_groups=groups_xk)
+    got = lax.all_gather(got, "dap", axis=0, tiled=True, axis_index_groups=groups_x)
+    other = lax.ppermute(got, "dap", [(d, d ^ 1) for d in range(n)])
+    (psum,) = call(
+        pool_kernel, (shape((tokens, cs + 128), F32),), (got, atom_weight),
+        name="pool_half", flops=3_000_000_000, bytes_=2_000_000,
+    )
     big = pltpu.VMEM((tokens // 128, rows * c, 128), F32)
     held = [pltpu.VMEM((rows, c, tokens), BF16), pltpu.SemaphoreType.DMA]
     z_shape = shape((rows, c, tokens), BF16)
@@ -255,8 +278,8 @@
     token_single, z, sent = call(
         first_kernel,
         (shape((rows, cs), BF16), z_shape, sent_shape),
-        (me, got, atom_weight, left_weight, right_weight, pair_map,
-         tri_proj[0], tri_gains[0, 0:1]),
+        (me, psum, other, atom_weight, left_weight, right_weight, pair_map,
+         tri_proj, tri_gains),
         [pltpu.VMEM((tokens, cs), F32), big, big, *held],
         name="first", flops=4_000_000_000, bytes_=8_000_000, far_out=(1,), vmem=32,
     )
@@ -267,13 +290,12 @@
     for layer in range(2):
         got = exchange(sent)
         (kept,) = call(
-            gate_kernel, (shape((2 * rows, c, tokens), BF16),),
-            (z, tri_gate[layer], tri_gains[layer, 0:1]), held,
+            functools.partial(gate_kernel, layer), (shape((2 * rows, c, tokens), BF16),),
+            (z, tri_gate, tri_gains), held,
             name=f"gating{layer}", flops=200_000_000, bytes_=3_000_000, far_in=(0,),
         )
-        dims = NT if layer == 0 else TN
         (prod,) = call(
-            lambda v, r, dims=dims: product_kernel(dims, v, r),
+            functools.partial(product_kernel, TN if layer else NT),
             (shape((n, 16, tokens), BF16),), (got,),
             name=f"product{layer}", flops=1_000_000_000, bytes_=3_000_000,
         )
@@ -281,14 +303,14 @@
         if layer == 0:
             z, sent = call(
                 middle_kernel, (z_shape, sent_shape),
-                (prod, kept, tri_out[0], tri_gains[0, 1:2], tri_proj[1], tri_gains[1, 0:1]),
+                (prod, kept, tri_out, tri_proj, tri_gains),
                 [big, big, big, *held],
                 name="middle", flops=1_000_000_000, bytes_=8_000_000, far_out=(0,), vmem=32,
             )
         else:
             (pair,) = call(
                 last_kernel, (shape((rows, tokens, c), BF16),),
-                (prod, kept, tri_out[1], tri_gains[1, 1:2]),
+                (prod, kept, tri_out, tri_gains),
                 [big],
                 name="last", flops=200_000_000, bytes_=5_000_000,
             )

time: 275 us -> 239 us (0.87)
  waiting for transfers between devices: 81.7 us -> 50.8 us
  between operations: 14.2 us -> 0.83 us
  blocking collectives: 131 us -> 139 us
  starting transfers between devices: 14.1 us -> 21.9 us
  local copies, waits for them, and re-layouts: 9.61 us -> 3.37 us
    all_gather x1 -> x0, waiting for transfers between devices: 30.9 us -> none  [local(): lax.all_gather(got, 'dap', axis=0, tiled=True, axis_index_groups=groups_xk)]
    all_gather x0 -> x1, blocking collectives: none -> 12.5 us  [local(): lax.all_gather(got, 'dap', axis=0, tiled=True, axis_index_groups=groups_x)]
    ppermute x0 -> x1, starting transfers between devices: none -> 7.81 us  [local(): other = lax.ppermute(got, 'dap', [(d, d ^ 1) for d in range(n)])]
    all_to_all x2, blocking collectives: 114 us -> 109 us  [exchange(): return lax.all_to_all(v, 'dap', split_axis=0, concat_axis=0, tiled=True)]
    unnamed x22 -> x26, local copies, waits for them, and re-layouts: 7.85 us -> 3.37 us
    pallas_call x8 -> x9, Pallas kernels: 23.4 us -> 23 us  [call(): pl.pallas_call(body, out_shape=outs, in_specs=specs, out_specs=places, sc...]
  transfers between devices with their start and end apart: 3 -> 3, of which waited for: 3 -> 2; matrix products, arithmetic and copies ran while one was open for 1% -> 0% of each run, Pallas kernels for 1% -> 2%
where the time goes in v4:
time: 239 us
  blocking collectives  139 us (58%)
  waiting for transfers between devices  50.8 us (21%)
  Pallas kernels  23 us (10%)
  starting transfers between devices  21.9 us (9%)
  local copies, waits for them, and re-layouts  3.37 us (1%)
    all_to_all x2, blocking collectives, exchange(): return lax.all_to_all(v, 'dap', split_axis=0, concat_axis=0, tiled=True)  109 us
    all_to_all x2, waiting for transfers between devices, exchange(): return lax.all_to_all(v, 'dap', split_axis=0, concat_axis=0, tiled=True)  50.8 us
    pallas_call x9, Pallas kernels, call(): pl.pallas_call(body, out_shape=outs, in_specs=specs, out_specs=places, sc...  23 us
    all_to_all x1, blocking collectives, local(): lax.all_to_all(packed, 'dap', split_axis=0, concat_axis=0, tiled=True, ax...  16.7 us
    all_to_all x2, starting transfers between devices, exchange(): return lax.all_to_all(v, 'dap', split_axis=0, concat_axis=0, tiled=True)  14 us
    all_gather x1, blocking collectives, local(): lax.all_gather(got, 'dap', axis=0, tiled=True, axis_index_groups=groups_x)  12.5 us
    ppermute x1, starting transfers between devices, local(): other = lax.ppermute(got, 'dap', [(d, d ^ 1) for d in range(n)])  7.81 us
  transfers between devices with their start and end apart: 3, of which 2 were waited for; matrix products, arithmetic and copies ran while one was open for 0% of the time, Pallas kernels for 2%

profile of v4, /device:TPU:1, one launch (start us, length us, event | category | flops | bytes accessed | tf_op | source)
XLA Modules:
  0.0 238.6 jit_solution(11615971719082920)
XLA Ops:
  0.6 1.5 packed_atoms.1
  2.1 16.7 %all_to_all.25 = bf16[8,112,128]{2,1,0:T(8,128)(2,1)S(1)} all-to-all(bf16[8,112,128]{2,1,0:T(8,128)(2,1)} %packed_atoms.1), channel_id=1, replica_groups={{0,8,16,24,32,40,48,56},{1,9,17,25,33,41,49,57},{2,10,18,26,34,42,50,58..., dimensions={0} | all-to-all | bytes 458752 | tf_op jit(solution)/shard_map/all_to_all | solution.py:265
  18.8 12.5 %all_gather.3.packed_ref = bf16[32,112,128]{2,1,0:T(8,128)(2,1)S(1)} all-gather(bf16[8,112,128]{2,1,0:T(8,128)(2,1)S(1)} %all_to_all.25), channel_id=1, replica_groups={{0,2,4,6},{1,3,5,7},{8,10,12,14},{9,11,13,15},{16,18,20,22},{17,19,21,2..., dimensions={0}, use_global_device_ids=true | all-gather | bytes 1146880 | tf_op jit(solution)/shard_map/all_gather | solution.py:268
  31.3 7.8 %collective-permute-start = (bf16[32,112,128]{2,1,0:T(8,128)(2,1)S(1)}, bf16[32,112,128]{2,1,0:T(8,128)(2,1)S(1)}, u32[]{:S(2)}, u32[]{:S(2)}) collective-permute-start(bf16[32,112,128]{2,1,0:T(8,128)(2,1)S(1)} %all_gather.3.packed_ref), channel_id=1, source_target_pairs={{0,1},{1,0},{2,3},{3,2},{4,5},{5,4},{6,7},{7,6},{8,9},{9,8},{10,11... | collective-permute-start | bytes 2752520 | tf_op jit(solution)/shard_map/ppermute | solution.py:269
  39.1 0.0 copy-start.9
  39.1 0.9 copy-done.9
  40.0 0.0 copy-start.11
  40.0 0.0 copy-start.12
  40.0 2.5 %pool_half.1.psum_ref = f32[512,512]{1,0:T(8,128)S(1)} custom-call(bf16[32,112,128]{2,1,0:T(8,128)(2,1)S(1)} %all_gather.3.packed_ref, bf16[128,384]{1,0:T(8,128)(2,1)S(1)} %copy-done.9), custom_call_target="tpu_custom_call" | custom-call | flops 3000000000 | bytes 2000000 | tf_op jit(solution)/shard_map/pool_half/pallas_call | solution.py:233
  42.6 6.3 %first.1 = (bf16[8,384]{1,0:T(8,128)(2,1)}, bf16[8,128,512]{2,1,0:T(8,128)(2,1)S(1)}, bf16[64,32,512]{2,1,0:T(8,128)(2,1)S(1)}) custom-call(s32[1]{0:T(128)} %bitcast.idx_ref, f32[512,512]{1,0:T(8,128)S(1)} %pool_half.1.psum_ref, bf16[32,112,128]{2,1,0:T(8,128)(2,1)S(1)} %collective-permute-done.packed_ref, bf16[128,384]{1,0:T(8,128)(2,1)S(1)} %copy-done.10, ...), custom_call_target="tpu_custom_call" | custom-call | flops 4000000000 | bytes 8000000 | tf_op jit(solution)/shard_map/first/pallas_call | solution.py:233
  48.9 53.6 %all_to_all.26.v_ref = bf16[64,32,512]{2,1,0:T(8,128)(2,1)S(1)} all-to-all(bf16[64,32,512]{2,1,0:T(8,128)(2,1)S(1)} %get-tuple-element.8), channel_id=1, replica_groups=mesh['dp'=8,'dap'=64] {'dap'}, dimensions={0} | all-to-all | bytes 4194304 | tf_op jit(solution)/shard_map/all_to_all | solution.py:288
  102.5 1.7 product0.1
  104.2 7.0 %all-to-all-start.2 = ((bf16[64,16,512]{2,1,0:T(8,128)(2,1)}), bf16[64,16,512]{2,1,0:T(8,128)(2,1)S(1)}, u32[]{:S(2)}, u32[]{:S(2)}) async-start(bf16[64,16,512]{2,1,0:T(8,128)(2,1)} %product0.1), calls=%async_computation.2 | async-start | bytes 2097152 | tf_op jit(solution)/shard_map/all_to_all | solution.py:288
  111.2 1.2 copy-done.1
  112.4 1.3 gating0.1.held_ref
  113.8 25.4 %all-to-all-done.2.x_ref = bf16[64,16,512]{2,1,0:T(8,128)(2,1)S(1)} async-done(((bf16[64,16,512]{2,1,0:T(8,128)(2,1)}), bf16[64,16,512]{2,1,0:T(8,128)(2,1)S(1)}, u32[]{:S(2)}, u32[]{:S(2)}) %all-to-all-start.2) | async-done | bytes 1048608 | tf_op jit(solution)/shard_map/all_to_all | solution.py:288
  139.2 4.1 %middle.1 = (bf16[8,128,512]{2,1,0:T(8,128)(2,1)S(1)}, bf16[64,32,512]{2,1,0:T(8,128)(2,1)S(1)}) custom-call(bf16[64,16,512]{2,1,0:T(8,128)(2,1)S(1)} %all-to-all-done.2.x_ref, bf16[16,128,512]{2,1,0:T(8,128)(2,1)S(1)} %gating0.1.held_ref, bf16[2,128,128]{2,1,0:T(8,128)(2,1)S(1)} %copy-done.5, bf16[2,128,512]{2,1,0:T(8,128)(2,1)S(1)} %copy-done.8, ...), custom_call_target="tpu_custom_call" | custom-call | flops 1000000000 | bytes 8000000 | tf_op jit(solution)/shard_map/middle/pallas_call | solution.py:233
  143.3 55.9 %all_to_all.27.v_ref = bf16[64,32,512]{2,1,0:T(8,128)(2,1)S(1)} all-to-all(bf16[64,32,512]{2,1,0:T(8,128)(2,1)S(1)} %get-tuple-element.10), channel_id=1, replica_groups=mesh['dp'=8,'dap'=64] {'dap'}, dimensions={0} | all-to-all | bytes 4194304 | tf_op jit(solution)/shard_map/all_to_all | solution.py:288
  199.2 1.7 product1.1
  201.0 7.0 %all-to-all-start.4 = ((bf16[64,16,512]{2,1,0:T(8,128)(2,1)}), bf16[64,16,512]{2,1,0:T(8,128)(2,1)S(1)}, u32[]{:S(2)}, u32[]{:S(2)}) async-start(bf16[64,16,512]{2,1,0:T(8,128)(2,1)} %product1.1), calls=%async_computation.4 | async-start | bytes 2097152 | tf_op jit(solution)/shard_map/all_to_all | solution.py:288
  208.0 1.2 copy-done.3
  209.2 1.3 gating1.1.held_ref
  210.5 25.4 %all-to-all-done.4.x_ref = bf16[64,16,512]{2,1,0:T(8,128)(2,1)S(1)} async-done(((bf16[64,16,512]{2,1,0:T(8,128)(2,1)}), bf16[64,16,512]{2,1,0:T(8,128)(2,1)S(1)}, u32[]{:S(2)}, u32[]{:S(2)}) %all-to-all-start.4) | async-done | bytes 1048608 | tf_op jit(solution)/shard_map/all_to_all | solution.py:288
  236.0 2.6 %last.1 = bf16[8,512,128]{2,1,0:T(8,128)(2,1)} custom-call(bf16[64,16,512]{2,1,0:T(8,128)(2,1)S(1)} %all-to-all-done.4.x_ref, bf16[16,128,512]{2,1,0:T(8,128)(2,1)S(1)} %gating1.1.held_ref, bf16[2,128,128]{2,1,0:T(8,128)(2,1)S(1)} %copy-done.5, f32[2,2,128]{2,1,0:T(2,128)S(1)} %copy-done.6), custom_call_target="tpu_custom_call" | custom-call | flops 200000000 | bytes 5000000 | tf_op jit(solution)/shard_map/last/pallas_call | solution.py:233
  (21 shorter events, 0.0 us)
Async XLA Ops:
  31.3 11.2 %collective-permute-start = (bf16[32,112,128]{2,1,0:T(8,128)(2,1)S(1)}, bf16[32,112,128]{2,1,0:T(8,128)(2,1)S(1)}, u32[]{:S(2)}, u32[]{:S(2)}) collective-permute-start(bf16[32,112,128]{2,1,0:T(8,128)(2,1)S(1)} %all_gather.3.packed_ref), channel_id=1, source_target_pairs={{0,1},{1,0},{2,3},{3,2},{4,5},{5,4},{6,7},{7,6},{8,9},{9,8},{10,11... | collective-permute-start | bytes 2752520 | tf_op jit(solution)/shard_map/ppermute | solution.py:269
  39.1 0.9 copy-start.9
  40.0 2.5 %copy-start.6 = (f32[2,2,128]{2,1,0:T(2,128)S(1)}, f32[2,2,128]{2,1,0:T(2,128)}, u32[]{:S(2)}) copy-start(f32[2,2,128]{2,1,0:T(2,128)} %gain_ref.9) | copy-start | bytes 6148
  40.0 2.5 %copy-start.7 = (bf16[8,512,128]{2,1,0:T(8,128)(2,1)S(1)}, bf16[8,512,128]{2,1,0:T(8,128)(2,1)}, u32[]{:S(2)}) copy-start(bf16[8,512,128]{2,1,0:T(8,128)(2,1)} %pair_ref.1) | copy-start | bytes 3145732
  40.0 2.5 %copy-start.8 = (bf16[2,128,512]{2,1,0:T(8,128)(2,1)S(1)}, bf16[2,128,512]{2,1,0:T(8,128)(2,1)}, u32[]{:S(2)}) copy-start(bf16[2,128,512]{2,1,0:T(8,128)(2,1)} %proj_ref.3) | copy-start | bytes 786436
  40.0 2.6 %copy-start.10 = (bf16[128,384]{1,0:T(8,128)(2,1)S(1)}, bf16[128,384]{1,0:T(8,128)(2,1)}, u32[]{:S(2)}) copy-start(bf16[128,384]{1,0:T(8,128)(2,1)} %weight_ref.3) | copy-start | bytes 294916
  40.0 2.6 %copy-start.11 = (bf16[384,128]{1,0:T(8,128)(2,1)S(1)}, bf16[384,128]{1,0:T(8,128)(2,1)}, u32[]{:S(2)}) copy-start(bf16[384,128]{1,0:T(8,128)(2,1)} %wl_ref.1) | copy-start | bytes 294916
  40.0 2.6 %copy-start.12 = (bf16[384,128]{1,0:T(8,128)(2,1)S(1)}, bf16[384,128]{1,0:T(8,128)(2,1)}, u32[]{:S(2)}) copy-start(bf16[384,128]{1,0:T(8,128)(2,1)} %wr_ref.1) | copy-start | bytes 294916
  48.9 53.6 %copy-start = (bf16[8,128,512]{2,1,0:T(8,128)(2,1)}, bf16[8,128,512]{2,1,0:T(8,128)(2,1)S(1)}, u32[]{:S(2)}) copy-start(bf16[8,128,512]{2,1,0:T(8,128)(2,1)S(1)} %get-tuple-element.9.z_in) | copy-start | bytes 3145732
  102.5 8.8 %copy-start.4 = (bf16[2,128,128]{2,1,0:T(8,128)(2,1)S(1)}, bf16[2,128,128]{2,1,0:T(8,128)(2,1)}, u32[]{:S(2)}) copy-start(bf16[2,128,128]{2,1,0:T(8,128)(2,1)} %gate_ref.3) | copy-start | bytes 196612
  104.2 35.0 %all-to-all-start.2 = ((bf16[64,16,512]{2,1,0:T(8,128)(2,1)}), bf16[64,16,512]{2,1,0:T(8,128)(2,1)S(1)}, u32[]{:S(2)}, u32[]{:S(2)}) async-start(bf16[64,16,512]{2,1,0:T(8,128)(2,1)} %product0.1), calls=%async_computation.2 | async-start | bytes 2097152 | tf_op jit(solution)/shard_map/all_to_all | solution.py:288
  111.2 1.2 copy-start.1
  112.4 26.7 %copy-start.5 = (bf16[2,128,128]{2,1,0:T(8,128)(2,1)S(1)}, bf16[2,128,128]{2,1,0:T(8,128)(2,1)}, u32[]{:S(2)}) copy-start(bf16[2,128,128]{2,1,0:T(8,128)(2,1)} %out_ref.3) | copy-start | bytes 196612
  143.3 55.9 %copy-start.2 = (bf16[8,128,512]{2,1,0:T(8,128)(2,1)}, bf16[8,128,512]{2,1,0:T(8,128)(2,1)S(1)}, u32[]{:S(2)}) copy-start(bf16[8,128,512]{2,1,0:T(8,128)(2,1)S(1)} %get-tuple-element.11.z_in) | copy-start | bytes 3145732
  201.0 35.0 %all-to-all-start.4 = ((bf16[64,16,512]{2,1,0:T(8,128)(2,1)}), bf16[64,16,512]{2,1,0:T(8,128)(2,1)S(1)}, u32[]{:S(2)}, u32[]{:S(2)}) async-start(bf16[64,16,512]{2,1,0:T(8,128)(2,1)} %product1.1), calls=%async_computation.4 | async-start | bytes 2097152 | tf_op jit(solution)/shard_map/all_to_all | solution.py:288
  208.0 1.2 copy-start.3

commit v5 on v4

--- a/solution.py
+++ b/solution.py
@@ -9,12 +9,14 @@
 
 EPS = 1e-05
 GROUP = 4
+PARTS = 2
 F32, BF16 = jnp.float32, jnp.bfloat16
 NT = (((1,), (1,)), ((), ()))
 TN = (((0,), (0,)), ((), ()))
-
-
-def mm(a, b, dims=(((1,), (0,)), ((), ()))):
+NN = (((1,), (0,)), ((), ()))
+
+
+def mm(a, b, dims=NN):
     return lax.dot_general(a, b, dims, preferred_element_type=F32)
 
 
@@ -56,7 +58,7 @@
 def pool(packed_ref, weight_ref, tokens):
     blocks, rows, _ = packed_ref.shape
     atoms = rows - 16
-    some = 8
+    some = 32
     total = None
     for at in range(0, blocks, some):
         feats = packed_ref[at : at + some, 0:atoms, :].reshape(some * atoms, -1)
@@ -161,16 +163,27 @@
         out_ref[rows + r] = z
 
 
-def product_kernel(dims, v_ref, r_ref):
+def product_kernel(dims, v_ref, r_out, r_ref, sem):
     n, _, length = v_ref.shape
     a = v_ref[:, 0:16, :].astype(F32)
     b = v_ref[:, 16:32, :].astype(F32)
-    out = []
-    for ch in range(2):
-        ac = a[:, ch * 8 : ch * 8 + 8, :].reshape(n * 8, length).astype(BF16)
-        bc = b[:, ch * 8 : ch * 8 + 8, :].reshape(n * 8, length).astype(BF16)
-        out.append(mm(ac, bc, dims).reshape(n, 8, length))
-    r_ref[...] = jnp.concatenate(out, axis=1).astype(BF16)
+    a = [a[:, k : k + 8, :].reshape(n * 8, length).astype(BF16) for k in (0, 8)]
+    b = [b[:, k : k + 8, :].reshape(n * 8, length).astype(BF16) for k in (0, 8)]
+    if dims == TN:
+        a, dims = [x.T for x in a], NN
+    part = n // PARTS
+    copies = []
+    for k in range(PARTS):
+        out = [
+            mm(x[k * part * 8 : (k + 1) * part * 8], y, dims).reshape(part, 8, length)
+            for x, y in zip(a, b)
+        ]
+        here = pl.ds(k * part, part)
+        r_ref[here] = jnp.concatenate(out, axis=1).astype(BF16)
+        copies.append(pltpu.make_async_copy(r_ref.at[here], r_out.at[here], sem.at[k]))
+        copies[-1].start()
+    for copy in copies:
+        copy.wait()
 
 
 def update_rows(some, s_ref, out_t, gain, held_ref):
@@ -205,16 +218,23 @@
     copy.wait()
 
 
-def last_kernel(x_ref, held_ref, out_ref, gain_ref, pair_ref, s_ref):
+def last_kernel(x_ref, held_ref, out_ref, gain_ref, pair_out, s_ref, pair_ref, sem):
     rows, tokens, c = pair_ref.shape
     fill(s_ref, x_ref)
     gain_out = column(gain_ref[1, 1:2, :], GROUP * tokens)
     out_t = out_ref[1].T
+    copies = []
     for at in range(0, rows, GROUP):
         some = range(at, at + GROUP)
         z = update_rows(some, s_ref, out_t, gain_out, held_ref)
         for k, r in enumerate(some):
             pair_ref[r] = z[:, k * tokens : (k + 1) * tokens].T
+        here = pl.ds(at, GROUP)
+        k = at // GROUP
+        copies.append(pltpu.make_async_copy(pair_ref.at[here], pair_out.at[here], sem.at[k]))
+        copies[-1].start()
+    for copy in copies:
+        copy.wait()
 
 
 def call(
@@ -297,7 +317,8 @@
         (prod,) = call(
             functools.partial(product_kernel, TN if layer else NT),
             (shape((n, 16, tokens), BF16),), (got,),
-            name=f"product{layer}", flops=1_000_000_000, bytes_=3_000_000,
+            [pltpu.VMEM((n, 16, tokens), BF16), pltpu.SemaphoreType.DMA((PARTS,))],
+            far_out=(0,), vmem=32, name=f"product{layer}", flops=1_000_000_000, bytes_=3_000_000,
         )
         prod = exchange(prod)
         if layer == 0:
@@ -305,14 +326,14 @@
                 middle_kernel, (z_shape, sent_shape),
                 (prod, kept, tri_out, tri_proj, tri_gains),
                 [big, big, big, *held],
-                name="middle", flops=1_000_000_000, bytes_=8_000_000, far_out=(0,), vmem=32,
+                name="middle", flops=1_000_000_000, bytes_=8_000_000, far_out=(0,), vmem=40,
             )
         else:
             (pair,) = call(
                 last_kernel, (shape((rows, tokens, c), BF16),),
                 (prod, kept, tri_out, tri_gains),
-                [big],
-                name="last", flops=200_000_000, bytes_=5_000_000,
+                [big, pltpu.VMEM((rows, tokens, c), BF16), pltpu.SemaphoreType.DMA((rows // GROUP,))],
+                far_out=(0,), vmem=32, name="last", flops=200_000_000, bytes_=5_000_000,
             )
     return token_single, pair
 

time: 239 us -> 239 us (level)
  no operation moved by 1% of the time
where the time goes in v5:
time: 239 us; the launch traced here: 238 us
  blocking collectives  139 us (58%)
  waiting for transfers between devices  50.8 us (21%)
  Pallas kernels  22.2 us (9%)
  starting transfers between devices  21.9 us (9%)
  local copies, waits for them, and re-layouts  3.37 us (1%)
    all_to_all x2, blocking collectives, exchange(): return lax.all_to_all(v, 'dap', split_axis=0, concat_axis=0, tiled=True)  109 us
    all_to_all x2, waiting for transfers between devices, exchange(): return lax.all_to_all(v, 'dap', split_axis=0, concat_axis=0, tiled=True)  50.8 us
    pallas_call x9, Pallas kernels, call(): pl.pallas_call(body, out_shape=outs, in_specs=specs, out_specs=places, sc...  22.2 us
    all_to_all x1, blocking collectives, local(): lax.all_to_all(packed, 'dap', split_axis=0, concat_axis=0, tiled=True, ax...  16.7 us
    all_to_all x2, starting transfers between devices, exchange(): return lax.all_to_all(v, 'dap', split_axis=0, concat_axis=0, tiled=True)  14.1 us
    all_gather x1, blocking collectives, local(): lax.all_gather(got, 'dap', axis=0, tiled=True, axis_index_groups=groups_x)  12.5 us
    ppermute x1, starting transfers between devices, local(): other = lax.ppermute(got, 'dap', [(d, d ^ 1) for d in range(n)])  7.81 us
  transfers between devices with their start and end apart: 3, of which 2 were waited for; matrix products, arithmetic and copies ran while one was open for 0% of the time, Pallas kernels for 2%

profile of v5, /device:TPU:1, one launch (start us, length us, event | category | flops | bytes accessed | tf_op | source)
XLA Modules:
  0.0 237.9 jit_solution(1749515577458754205)
XLA Ops:
  0.6 1.5 packed_atoms.1
  2.1 16.7 %all_to_all.25 = bf16[8,112,128]{2,1,0:T(8,128)(2,1)S(1)} all-to-all(bf16[8,112,128]{2,1,0:T(8,128)(2,1)} %packed_atoms.1), channel_id=1, replica_groups={{0,8,16,24,32,40,48,56},{1,9,17,25,33,41,49,57},{2,10,18,26,34,42,50,58..., dimensions={0} | all-to-all | bytes 458752 | tf_op jit(solution)/shard_map/all_to_all | solution.py:285
  18.8 12.5 %all_gather.3.packed_ref = bf16[32,112,128]{2,1,0:T(8,128)(2,1)S(1)} all-gather(bf16[8,112,128]{2,1,0:T(8,128)(2,1)S(1)} %all_to_all.25), channel_id=1, replica_groups={{0,2,4,6},{1,3,5,7},{8,10,12,14},{9,11,13,15},{16,18,20,22},{17,19,21,2..., dimensions={0}, use_global_device_ids=true | all-gather | bytes 1146880 | tf_op jit(solution)/shard_map/all_gather | solution.py:288
  31.3 7.8 %collective-permute-start = (bf16[32,112,128]{2,1,0:T(8,128)(2,1)S(1)}, bf16[32,112,128]{2,1,0:T(8,128)(2,1)S(1)}, u32[]{:S(2)}, u32[]{:S(2)}) collective-permute-start(bf16[32,112,128]{2,1,0:T(8,128)(2,1)S(1)} %all_gather.3.packed_ref), channel_id=1, source_target_pairs={{0,1},{1,0},{2,3},{3,2},{4,5},{5,4},{6,7},{7,6},{8,9},{9,8},{10,11... | collective-permute-start | bytes 2752520 | tf_op jit(solution)/shard_map/ppermute | solution.py:289
  39.1 0.0 copy-start.9
  39.1 0.9 copy-done.9
  40.0 0.0 copy-start.11
  40.0 0.0 copy-start.12
  40.0 2.4 %pool_half.1.psum_ref = f32[512,512]{1,0:T(8,128)S(1)} custom-call(bf16[32,112,128]{2,1,0:T(8,128)(2,1)S(1)} %all_gather.3.packed_ref, bf16[128,384]{1,0:T(8,128)(2,1)S(1)} %copy-done.9), custom_call_target="tpu_custom_call" | custom-call | flops 3000000000 | bytes 2000000 | tf_op jit(solution)/shard_map/pool_half/pallas_call | solution.py:253
  42.5 6.0 %first.1 = (bf16[8,384]{1,0:T(8,128)(2,1)}, bf16[8,128,512]{2,1,0:T(8,128)(2,1)S(1)}, bf16[64,32,512]{2,1,0:T(8,128)(2,1)S(1)}) custom-call(s32[1]{0:T(128)} %bitcast.idx_ref, f32[512,512]{1,0:T(8,128)S(1)} %pool_half.1.psum_ref, bf16[32,112,128]{2,1,0:T(8,128)(2,1)S(1)} %collective-permute-done.packed_ref, bf16[128,384]{1,0:T(8,128)(2,1)S(1)} %copy-done.10, ...), custom_call_target="tpu_custom_call" | custom-call | flops 4000000000 | bytes 8000000 | tf_op jit(solution)/shard_map/first/pallas_call | solution.py:253
  48.5 53.5 %all_to_all.26.v_ref = bf16[64,32,512]{2,1,0:T(8,128)(2,1)S(1)} all-to-all(bf16[64,32,512]{2,1,0:T(8,128)(2,1)S(1)} %get-tuple-element.8), channel_id=1, replica_groups=mesh['dp'=8,'dap'=64] {'dap'}, dimensions={0} | all-to-all | bytes 4194304 | tf_op jit(solution)/shard_map/all_to_all | solution.py:308
  102.1 1.6 product0.1
  103.6 7.0 %all-to-all-start.2 = ((bf16[64,16,512]{2,1,0:T(8,128)(2,1)}), bf16[64,16,512]{2,1,0:T(8,128)(2,1)S(1)}, u32[]{:S(2)}, u32[]{:S(2)}) async-start(bf16[64,16,512]{2,1,0:T(8,128)(2,1)} %product0.1), calls=%async_computation.2 | async-start | bytes 2097152 | tf_op jit(solution)/shard_map/all_to_all | solution.py:308
  110.7 1.2 copy-done.1
  111.9 1.3 gating0.1.held_ref
  113.3 25.4 %all-to-all-done.2.x_ref = bf16[64,16,512]{2,1,0:T(8,128)(2,1)S(1)} async-done(((bf16[64,16,512]{2,1,0:T(8,128)(2,1)}), bf16[64,16,512]{2,1,0:T(8,128)(2,1)S(1)}, u32[]{:S(2)}, u32[]{:S(2)}) %all-to-all-start.2) | async-done | bytes 1048608 | tf_op jit(solution)/shard_map/all_to_all | solution.py:308
  138.7 4.1 %middle.1 = (bf16[8,128,512]{2,1,0:T(8,128)(2,1)S(1)}, bf16[64,32,512]{2,1,0:T(8,128)(2,1)S(1)}) custom-call(bf16[64,16,512]{2,1,0:T(8,128)(2,1)S(1)} %all-to-all-done.2.x_ref, bf16[16,128,512]{2,1,0:T(8,128)(2,1)S(1)} %gating0.1.held_ref, bf16[2,128,128]{2,1,0:T(8,128)(2,1)S(1)} %copy-done.5, bf16[2,128,512]{2,1,0:T(8,128)(2,1)S(1)} %copy-done.8, ...), custom_call_target="tpu_custom_call" | custom-call | flops 1000000000 | bytes 8000000 | tf_op jit(solution)/shard_map/middle/pallas_call | solution.py:253
  142.8 55.9 %all_to_all.27.v_ref = bf16[64,32,512]{2,1,0:T(8,128)(2,1)S(1)} all-to-all(bf16[64,32,512]{2,1,0:T(8,128)(2,1)S(1)} %get-tuple-element.10), channel_id=1, replica_groups=mesh['dp'=8,'dap'=64] {'dap'}, dimensions={0} | all-to-all | bytes 4194304 | tf_op jit(solution)/shard_map/all_to_all | solution.py:308
  198.7 1.6 product1.1
  200.3 7.0 %all-to-all-start.4 = ((bf16[64,16,512]{2,1,0:T(8,128)(2,1)}), bf16[64,16,512]{2,1,0:T(8,128)(2,1)S(1)}, u32[]{:S(2)}, u32[]{:S(2)}) async-start(bf16[64,16,512]{2,1,0:T(8,128)(2,1)} %product1.1), calls=%async_computation.4 | async-start | bytes 2097152 | tf_op jit(solution)/shard_map/all_to_all | solution.py:308
  207.3 1.2 copy-done.3
  208.5 1.3 gating1.1.held_ref
  209.9 25.4 %all-to-all-done.4.x_ref = bf16[64,16,512]{2,1,0:T(8,128)(2,1)S(1)} async-done(((bf16[64,16,512]{2,1,0:T(8,128)(2,1)}), bf16[64,16,512]{2,1,0:T(8,128)(2,1)S(1)}, u32[]{:S(2)}, u32[]{:S(2)}) %all-to-all-start.4) | async-done | bytes 1048608 | tf_op jit(solution)/shard_map/all_to_all | solution.py:308
  235.3 2.5 %last.1 = bf16[8,512,128]{2,1,0:T(8,128)(2,1)} custom-call(bf16[64,16,512]{2,1,0:T(8,128)(2,1)S(1)} %all-to-all-done.4.x_ref, bf16[16,128,512]{2,1,0:T(8,128)(2,1)S(1)} %gating1.1.held_ref, bf16[2,128,128]{2,1,0:T(8,128)(2,1)S(1)} %copy-done.5, f32[2,2,128]{2,1,0:T(2,128)S(1)} %copy-done.6), custom_call_target="tpu_custom_call" | custom-call | flops 200000000 | bytes 5000000 | tf_op jit(solution)/shard_map/last/pallas_call | solution.py:253
  (21 shorter events, 0.0 us)
Async XLA Ops:
  31.3 11.1 %collective-permute-start = (bf16[32,112,128]{2,1,0:T(8,128)(2,1)S(1)}, bf16[32,112,128]{2,1,0:T(8,128)(2,1)S(1)}, u32[]{:S(2)}, u32[]{:S(2)}) collective-permute-start(bf16[32,112,128]{2,1,0:T(8,128)(2,1)S(1)} %all_gather.3.packed_ref), channel_id=1, source_target_pairs={{0,1},{1,0},{2,3},{3,2},{4,5},{5,4},{6,7},{7,6},{8,9},{9,8},{10,11... | collective-permute-start | bytes 2752520 | tf_op jit(solution)/shard_map/ppermute | solution.py:289
  39.1 0.9 copy-start.9
  40.0 2.4 %copy-start.6 = (f32[2,2,128]{2,1,0:T(2,128)S(1)}, f32[2,2,128]{2,1,0:T(2,128)}, u32[]{:S(2)}) copy-start(f32[2,2,128]{2,1,0:T(2,128)} %gain_ref.9) | copy-start | bytes 6148
  40.0 2.4 %copy-start.7 = (bf16[8,512,128]{2,1,0:T(8,128)(2,1)S(1)}, bf16[8,512,128]{2,1,0:T(8,128)(2,1)}, u32[]{:S(2)}) copy-start(bf16[8,512,128]{2,1,0:T(8,128)(2,1)} %pair_ref.1) | copy-start | bytes 3145732
  40.0 2.4 %copy-start.8 = (bf16[2,128,512]{2,1,0:T(8,128)(2,1)S(1)}, bf16[2,128,512]{2,1,0:T(8,128)(2,1)}, u32[]{:S(2)}) copy-start(bf16[2,128,512]{2,1,0:T(8,128)(2,1)} %proj_ref.3) | copy-start | bytes 786436
  40.0 2.5 %copy-start.10 = (bf16[128,384]{1,0:T(8,128)(2,1)S(1)}, bf16[128,384]{1,0:T(8,128)(2,1)}, u32[]{:S(2)}) copy-start(bf16[128,384]{1,0:T(8,128)(2,1)} %weight_ref.3) | copy-start | bytes 294916
  40.0 2.5 %copy-start.11 = (bf16[384,128]{1,0:T(8,128)(2,1)S(1)}, bf16[384,128]{1,0:T(8,128)(2,1)}, u32[]{:S(2)}) copy-start(bf16[384,128]{1,0:T(8,128)(2,1)} %wl_ref.1) | copy-start | bytes 294916
  40.0 2.5 %copy-start.12 = (bf16[384,128]{1,0:T(8,128)(2,1)S(1)}, bf16[384,128]{1,0:T(8,128)(2,1)}, u32[]{:S(2)}) copy-start(bf16[384,128]{1,0:T(8,128)(2,1)} %wr_ref.1) | copy-start | bytes 294916
  48.5 53.6 %copy-start = (bf16[8,128,512]{2,1,0:T(8,128)(2,1)}, bf16[8,128,512]{2,1,0:T(8,128)(2,1)S(1)}, u32[]{:S(2)}) copy-start(bf16[8,128,512]{2,1,0:T(8,128)(2,1)S(1)} %get-tuple-element.9.z_in) | copy-start | bytes 3145732
  102.1 8.6 %copy-start.4 = (bf16[2,128,128]{2,1,0:T(8,128)(2,1)S(1)}, bf16[2,128,128]{2,1,0:T(8,128)(2,1)}, u32[]{:S(2)}) copy-start(bf16[2,128,128]{2,1,0:T(8,128)(2,1)} %gate_ref.3) | copy-start | bytes 196612
  103.6 35.0 %all-to-all-start.2 = ((bf16[64,16,512]{2,1,0:T(8,128)(2,1)}), bf16[64,16,512]{2,1,0:T(8,128)(2,1)S(1)}, u32[]{:S(2)}, u32[]{:S(2)}) async-start(bf16[64,16,512]{2,1,0:T(8,128)(2,1)} %product0.1), calls=%async_computation.2 | async-start | bytes 2097152 | tf_op jit(solution)/shard_map/all_to_all | solution.py:308
  110.7 1.2 copy-start.1
  111.9 26.7 %copy-start.5 = (bf16[2,128,128]{2,1,0:T(8,128)(2,1)S(1)}, bf16[2,128,128]{2,1,0:T(8,128)(2,1)}, u32[]{:S(2)}) copy-start(bf16[2,128,128]{2,1,0:T(8,128)(2,1)} %out_ref.3) | copy-start | bytes 196612
  142.8 56.0 %copy-start.2 = (bf16[8,128,512]{2,1,0:T(8,128)(2,1)}, bf16[8,128,512]{2,1,0:T(8,128)(2,1)S(1)}, u32[]{:S(2)}) copy-start(bf16[8,128,512]{2,1,0:T(8,128)(2,1)S(1)} %get-tuple-element.11.z_in) | copy-start | bytes 3145732
  200.3 35.0 %all-to-all-start.4 = ((bf16[64,16,512]{2,1,0:T(8,128)(2,1)}), bf16[64,16,512]{2,1,0:T(8,128)(2,1)S(1)}, u32[]{:S(2)}, u32[]{:S(2)}) async-start(bf16[64,16,512]{2,1,0:T(8,128)(2,1)} %product1.1), calls=%async_computation.4 | async-start | bytes 2097152 | tf_op jit(solution)/shard_map/all_to_all | solution.py:308
  207.3 1.2 copy-start.3

commit v6 on v5

--- a/solution.py
+++ b/solution.py
@@ -8,7 +8,8 @@
 from jax.sharding import PartitionSpec as P
 
 EPS = 1e-05
-GROUP = 4
+WIDTH = 128
+CODES = 8
 PARTS = 2
 F32, BF16 = jnp.float32, jnp.bfloat16
 NT = (((1,), (1,)), ((), ()))
@@ -37,27 +38,9 @@
     return centred * lax.rsqrt(variance + EPS) * gain
 
 
-def pack_kernel(feats_in, tok_in, out_ref, feats_ref, tok_ref, sem_feats, sem_tok):
-    copies = [
-        pltpu.make_async_copy(feats_in, feats_ref, sem_feats),
-        pltpu.make_async_copy(tok_in, tok_ref, sem_tok),
-    ]
-    for copy in copies:
-        copy.start()
-    for copy in copies:
-        copy.wait()
-    atoms, c = feats_ref.shape
-    tok = jnp.concatenate([tok_ref[...], jnp.zeros((1, c - atoms), jnp.int32)], axis=1)
-    row = lax.broadcasted_iota(jnp.int32, (16, c), 0)
-    codes = jnp.where(row == 0, tok >> 5, jnp.where(row == 1, tok & 31, 0))
-    block = jnp.concatenate([feats_ref[...], codes.astype(F32).astype(BF16)], axis=0)
-    for k in range(out_ref.shape[0]):
-        out_ref[k] = block
-
-
 def pool(packed_ref, weight_ref, tokens):
     blocks, rows, _ = packed_ref.shape
-    atoms = rows - 16
+    atoms = rows - CODES
     some = 32
     total = None
     for at in range(0, blocks, some):
@@ -79,14 +62,15 @@
     out_ref[...] = pool(packed_ref, weight_ref, out_ref.shape[0])
 
 
-def put_row(s_ref, r, value):
-    for t in range(s_ref.shape[0]):
-        s_ref[t, pl.ds(r, value.shape[0], stride=8), :] = value[:, t * 128 : t * 128 + 128]
-
-
-def get_row(s_ref, r, c):
+def put_row(s_ref, r, at, value):
+    for k in range(value.shape[1] // 128):
+        tile = value[:, k * 128 : k * 128 + 128]
+        s_ref[at // 128 + k, pl.ds(r, value.shape[0], stride=8), :] = tile
+
+
+def get_row(s_ref, r, at, c):
     return jnp.concatenate(
-        [s_ref[t, pl.ds(r, c, stride=8), :] for t in range(s_ref.shape[0])], axis=1
+        [s_ref[t, pl.ds(r, c, stride=8), :] for t in range(at // 128, (at + WIDTH) // 128)], axis=1
     )
 
 
@@ -97,12 +81,11 @@
 
 def operands(normed, half_proj_t, at, sa_ref, sb_ref):
     c = normed.shape[0]
-    length = sa_ref.shape[0] * 128
     for s_ref, block in ((sa_ref, 0), (sb_ref, 2)):
         p = mm(half_proj_t[block * c : (block + 2) * c], normed)
         p = jnp.tanh(p[:c]) * p[c:] + p[c:]
-        for k in range(normed.shape[1] // length):
-            put_row(s_ref, at + k, p[:, k * length : (k + 1) * length])
+        for r in range(normed.shape[1] // WIDTH):
+            put_row(s_ref, r, at, p[:, r * WIDTH : (r + 1) * WIDTH])
 
 
 def pack(sa_ref, sb_ref, u_ref):
@@ -131,15 +114,16 @@
     own = ts_ref[pl.ds(start, 8), :].astype(BF16)
     single_ref[...] = own
     left = mm(own, wl_ref[...]).astype(BF16).astype(F32)
-    gain = column(gain_ref[0, 0:1, :], GROUP * tokens)
+    gain = column(gain_ref[0, 0:1, :], rows * WIDTH)
     half_proj_t = (proj_ref[0].astype(F32) * 0.5).astype(BF16).T
-    for at in range(0, rows, GROUP):
-        some = range(at, at + GROUP)
+    for at in range(0, tokens, WIDTH):
+        here = slice(at, at + WIDTH)
         z = [
-            (pair_ref[r].astype(F32) + left[r : r + 1, :] + right).astype(BF16).T for r in some
+            (pair_ref[r, here, :].astype(F32) + left[r : r + 1, :] + right[here]).astype(BF16).T
+            for r in range(rows)
         ]
-        for r, row in zip(some, z):
-            z_ref[r] = row
+        for r, row in enumerate(z):
+            z_ref[r, :, here] = row
         z = jnp.concatenate(z, axis=1)
         normed = norm_rows(z.astype(F32), gain).astype(BF16)
         operands(normed, half_proj_t, at, sa_ref, sb_ref)
@@ -186,12 +170,13 @@
         copy.wait()
 
 
-def update_rows(some, s_ref, out_t, gain, held_ref):
+def update_rows(at, s_ref, out_t, gain, held_ref):
     c, rows = out_t.shape[0], held_ref.shape[0] // 2
-    x = jnp.concatenate([get_row(s_ref, r, c) for r in some], axis=1)
+    here = slice(at, at + WIDTH)
+    x = jnp.concatenate([get_row(s_ref, r, at, c) for r in range(rows)], axis=1)
     normed = norm_rows(x, gain).astype(BF16)
-    gating = jnp.concatenate([held_ref[r].astype(F32) for r in some], axis=1)
-    z = jnp.concatenate([held_ref[rows + r].astype(F32) for r in some], axis=1)
+    gating = jnp.concatenate([held_ref[r, :, here].astype(F32) for r in range(rows)], axis=1)
+    z = jnp.concatenate([held_ref[rows + r, :, here].astype(F32) for r in range(rows)], axis=1)
     return (z + gating * mm(out_t, normed)).astype(BF16)
 
 
@@ -201,15 +186,14 @@
 ):
     rows, c, tokens = z_ref.shape
     fill(s_ref, x_ref)
-    gain_out = column(gain_ref[0, 1:2, :], GROUP * tokens)
-    gain_in = column(gain_ref[1, 0:1, :], GROUP * tokens)
+    gain_out = column(gain_ref[0, 1:2, :], rows * WIDTH)
+    gain_in = column(gain_ref[1, 0:1, :], rows * WIDTH)
     out_t = out_ref[0].T
     half_proj_t = (proj_ref[1].astype(F32) * 0.5).astype(BF16).T
-    for at in range(0, rows, GROUP):
-        some = range(at, at + GROUP)
-        z = update_rows(some, s_ref, out_t, gain_out, held_ref)
-        for k, r in enumerate(some):
-            z_ref[r] = z[:, k * tokens : (k + 1) * tokens]
+    for at in range(0, tokens, WIDTH):
+        z = update_rows(at, s_ref, out_t, gain_out, held_ref)
+        for r in range(rows):
+            z_ref[r, :, at : at + WIDTH] = z[:, r * WIDTH : (r + 1) * WIDTH]
         normed = norm_rows(z.astype(F32), gain_in).astype(BF16)
         operands(normed, half_proj_t, at, sa_ref, sb_ref)
     copy = pltpu.make_async_copy(z_ref, z_out, sem)
@@ -221,17 +205,17 @@
 def last_kernel(x_ref, held_ref, out_ref, gain_ref, pair_out, s_ref, pair_ref, sem):
     rows, tokens, c = pair_ref.shape
     fill(s_ref, x_ref)
-    gain_out = column(gain_ref[1, 1:2, :], GROUP * tokens)
+    gain_out = column(gain_ref[1, 1:2, :], rows * WIDTH)
     out_t = out_ref[1].T
     copies = []
-    for at in range(0, rows, GROUP):
-        some = range(at, at + GROUP)
-        z = update_rows(some, s_ref, out_t, gain_out, held_ref)
-        for k, r in enumerate(some):
-            pair_ref[r] = z[:, k * tokens : (k + 1) * tokens].T
-        here = pl.ds(at, GROUP)
-        k = at // GROUP
-        copies.append(pltpu.make_async_copy(pair_ref.at[here], pair_out.at[here], sem.at[k]))
+    for at in range(0, tokens, WIDTH):
+        z = update_rows(at, s_ref, out_t, gain_out, held_ref)
+        for r in range(rows):
+            pair_ref[r, at : at + WIDTH, :] = z[:, r * WIDTH : (r + 1) * WIDTH].T
+        here = (slice(None), pl.ds(at, WIDTH))
+        copies.append(
+            pltpu.make_async_copy(pair_ref.at[here], pair_out.at[here], sem.at[at // WIDTH])
+        )
         copies[-1].start()
     for copy in copies:
         copy.wait()
@@ -276,14 +260,13 @@
     ny, nx = 8, 4
     groups_y = [[(y * nx + x) * 2 + k for y in range(ny)] for x in range(nx) for k in range(2)]
     groups_x = [[(y * nx + x) * 2 + k for x in range(nx)] for y in range(ny) for k in range(2)]
-    (packed,) = call(
-        pack_kernel, (shape((ny, atoms + 16, c), BF16),), (atom_feats, atom_token.reshape(1, atoms)),
-        [pltpu.VMEM((atoms, c), BF16), pltpu.VMEM((1, atoms), jnp.int32)]
-        + [pltpu.SemaphoreType.DMA] * 2,
-        name="packed_atoms", bytes_=300_000, far_in=(0, 1), vmem=60,
-    )
+    tok = atom_token.reshape(1, atoms)
+    tok = jnp.concatenate([tok >> 5, tok & 31], axis=0).astype(BF16)
+    tok = jnp.pad(tok, ((0, CODES - 2), (0, c - atoms)))
+    packed = jnp.concatenate([atom_feats, tok], axis=0)
     got = lax.all_to_all(
-        packed, "dap", split_axis=0, concat_axis=0, tiled=True, axis_index_groups=groups_y
+        jnp.broadcast_to(packed[None], (ny,) + packed.shape), "dap", split_axis=0,
+        concat_axis=0, tiled=True, axis_index_groups=groups_y,
     )
     got = lax.all_gather(got, "dap", axis=0, tiled=True, axis_index_groups=groups_x)
     other = lax.ppermute(got, "dap", [(d, d ^ 1) for d in range(n)])
@@ -332,7 +315,7 @@
             (pair,) = call(
                 last_kernel, (shape((rows, tokens, c), BF16),),
                 (prod, kept, tri_out, tri_gains),
-                [big, pltpu.VMEM((rows, tokens, c), BF16), pltpu.SemaphoreType.DMA((rows // GROUP,))],
+                [big, pltpu.VMEM((rows, tokens, c), BF16), pltpu.SemaphoreType.DMA((tokens // WIDTH,))],
                 far_out=(0,), vmem=32, name="last", flops=200_000_000, bytes_=5_000_000,
             )
     return token_single, pair

time: 239 us -> 237 us (level)
  Pallas kernels: 22.2 us -> 19.7 us
    pallas_call x9 -> x8, Pallas kernels: 22.2 us -> 19.7 us  [call(): pl.pallas_call(body, out_shape=outs, in_specs=specs, out_specs=places, sc...]
where the time goes in v6:
time: 237 us; the launch traced here: 236 us
  blocking collectives  138 us (58%)
  waiting for transfers between devices  50.9 us (21%)
  starting transfers between devices  22.2 us (9%)
  Pallas kernels  19.7 us (8%)
  local copies, waits for them, and re-layouts  3.4 us (1%)
    all_to_all x2, blocking collectives, exchange(): return lax.all_to_all(v, 'dap', split_axis=0, concat_axis=0, tiled=True)  110 us
    all_to_all x2, waiting for transfers between devices, exchange(): return lax.all_to_all(v, 'dap', split_axis=0, concat_axis=0, tiled=True)  50.9 us
    pallas_call x8, Pallas kernels, call(): pl.pallas_call(body, out_shape=outs, in_specs=specs, out_specs=places, sc...  19.7 us
    all_to_all x1, blocking collectives, local(): lax.all_to_all(jnp.broadcast_to(packed[None], (ny,) + packed.shape), 'dap...  16.2 us
    all_to_all x2, starting transfers between devices, exchange(): return lax.all_to_all(v, 'dap', split_axis=0, concat_axis=0, tiled=True)  14.1 us
    all_gather x1, blocking collectives, local(): lax.all_gather(got, 'dap', axis=0, tiled=True, axis_index_groups=groups_x)  11.6 us
    ppermute x1, starting transfers between devices, local(): other = lax.ppermute(got, 'dap', [(d, d ^ 1) for d in range(n)])  8.09 us
  transfers between devices with their start and end apart: 3, of which 2 were waited for; matrix products, arithmetic and copies ran while one was open for 0% of the time, Pallas kernels for 2%

profile of v6, /device:TPU:1, one launch (start us, length us, event | category | flops | bytes accessed | tf_op | source)
XLA Modules:
  0.0 236.2 jit_solution(12552637964590490816)
XLA Ops:
  0.6 0.7 convert_bitcast_fusion.1
  1.3 0.7 pad_maximum_fusion
  2.1 16.2 %all_to_all.25 = bf16[8,104,128]{2,1,0:T(8,128)(2,1)S(1)} all-to-all(bf16[8,104,128]{2,1,0:T(8,128)(2,1)S(1)} %broadcast_in_dim.2), channel_id=1, replica_groups={{0,8,16,24,32,40,48,56},{1,9,17,25,33,41,49,57},{2,10,18,26,34,42,50,58..., dimensions={0} | all-to-all | bytes 425984 | tf_op jit(solution)/shard_map/all_to_all | solution.py:267
  18.3 11.6 %all_gather.3.packed_ref = bf16[32,104,128]{2,1,0:T(8,128)(2,1)S(1)} all-gather(bf16[8,104,128]{2,1,0:T(8,128)(2,1)S(1)} %all_to_all.25), channel_id=1, replica_groups={{0,2,4,6},{1,3,5,7},{8,10,12,14},{9,11,13,15},{16,18,20,22},{17,19,21,2..., dimensions={0}, use_global_device_ids=true | all-gather | bytes 1064960 | tf_op jit(solution)/shard_map/all_gather | solution.py:271
  29.9 8.1 %collective-permute-start = (bf16[32,104,128]{2,1,0:T(8,128)(2,1)S(1)}, bf16[32,104,128]{2,1,0:T(8,128)(2,1)S(1)}, u32[]{:S(2)}, u32[]{:S(2)}) collective-permute-start(bf16[32,104,128]{2,1,0:T(8,128)(2,1)S(1)} %all_gather.3.packed_ref), channel_id=1, source_target_pairs={{0,1},{1,0},{2,3},{3,2},{4,5},{5,4},{6,7},{7,6},{8,9},{9,8},{10,11... | collective-permute-start | bytes 2555912 | tf_op jit(solution)/shard_map/ppermute | solution.py:272
  38.0 0.9 copy-done.9
  38.9 0.0 copy-start.11
  38.9 0.0 copy-start.12
  38.9 2.4 %pool_half.1.psum_ref = f32[512,512]{1,0:T(8,128)S(1)} custom-call(bf16[32,104,128]{2,1,0:T(8,128)(2,1)S(1)} %all_gather.3.packed_ref, bf16[128,384]{1,0:T(8,128)(2,1)S(1)} %copy-done.9), custom_call_target="tpu_custom_call" | custom-call | flops 3000000000 | bytes 2000000 | tf_op jit(solution)/shard_map/pool_half/pallas_call | solution.py:237
  41.4 5.8 %first.1 = (bf16[8,384]{1,0:T(8,128)(2,1)}, bf16[8,128,512]{2,1,0:T(8,128)(2,1)S(1)}, bf16[64,32,512]{2,1,0:T(8,128)(2,1)S(1)}) custom-call(s32[1]{0:T(128)} %bitcast.idx_ref, f32[512,512]{1,0:T(8,128)S(1)} %pool_half.1.psum_ref, bf16[32,104,128]{2,1,0:T(8,128)(2,1)S(1)} %collective-permute-done.packed_ref, bf16[128,384]{1,0:T(8,128)(2,1)S(1)} %copy-done.10, ...), custom_call_target="tpu_custom_call" | custom-call | flops 4000000000 | bytes 8000000 | tf_op jit(solution)/shard_map/first/pallas_call | solution.py:237
  47.2 53.9 %all_to_all.26.v_ref = bf16[64,32,512]{2,1,0:T(8,128)(2,1)S(1)} all-to-all(bf16[64,32,512]{2,1,0:T(8,128)(2,1)S(1)} %get-tuple-element.8), channel_id=1, replica_groups=mesh['dp'=8,'dap'=64] {'dap'}, dimensions={0} | all-to-all | bytes 4194304 | tf_op jit(solution)/shard_map/all_to_all | solution.py:291
  101.1 1.6 product0.1
  102.6 7.0 %all-to-all-start.2 = ((bf16[64,16,512]{2,1,0:T(8,128)(2,1)}), bf16[64,16,512]{2,1,0:T(8,128)(2,1)S(1)}, u32[]{:S(2)}, u32[]{:S(2)}) async-start(bf16[64,16,512]{2,1,0:T(8,128)(2,1)} %product0.1), calls=%async_computation.2 | async-start | bytes 2097152 | tf_op jit(solution)/shard_map/all_to_all | solution.py:291
  109.7 1.2 copy-done.1
  110.9 1.3 gating0.1.held_ref
  112.2 25.4 %all-to-all-done.2.x_ref = bf16[64,16,512]{2,1,0:T(8,128)(2,1)S(1)} async-done(((bf16[64,16,512]{2,1,0:T(8,128)(2,1)}), bf16[64,16,512]{2,1,0:T(8,128)(2,1)S(1)}, u32[]{:S(2)}, u32[]{:S(2)}) %all-to-all-start.2) | async-done | bytes 1048608 | tf_op jit(solution)/shard_map/all_to_all | solution.py:291
  137.7 3.6 %middle.1 = (bf16[8,128,512]{2,1,0:T(8,128)(2,1)S(1)}, bf16[64,32,512]{2,1,0:T(8,128)(2,1)S(1)}) custom-call(bf16[64,16,512]{2,1,0:T(8,128)(2,1)S(1)} %all-to-all-done.2.x_ref, bf16[16,128,512]{2,1,0:T(8,128)(2,1)S(1)} %gating0.1.held_ref, bf16[2,128,128]{2,1,0:T(8,128)(2,1)S(1)} %copy-done.5, bf16[2,128,512]{2,1,0:T(8,128)(2,1)S(1)} %copy-done.8, ...), custom_call_target="tpu_custom_call" | custom-call | flops 1000000000 | bytes 8000000 | tf_op jit(solution)/shard_map/middle/pallas_call | solution.py:237
  141.2 55.9 %all_to_all.27.v_ref = bf16[64,32,512]{2,1,0:T(8,128)(2,1)S(1)} all-to-all(bf16[64,32,512]{2,1,0:T(8,128)(2,1)S(1)} %get-tuple-element.10), channel_id=1, replica_groups=mesh['dp'=8,'dap'=64] {'dap'}, dimensions={0} | all-to-all | bytes 4194304 | tf_op jit(solution)/shard_map/all_to_all | solution.py:291
  197.2 1.6 product1.1
  198.8 7.0 %all-to-all-start.4 = ((bf16[64,16,512]{2,1,0:T(8,128)(2,1)}), bf16[64,16,512]{2,1,0:T(8,128)(2,1)S(1)}, u32[]{:S(2)}, u32[]{:S(2)}) async-start(bf16[64,16,512]{2,1,0:T(8,128)(2,1)} %product1.1), calls=%async_computation.4 | async-start | bytes 2097152 | tf_op jit(solution)/shard_map/all_to_all | solution.py:291
  205.8 1.2 copy-done.3
  207.0 1.3 gating1.1.held_ref
  208.3 25.4 %all-to-all-done.4.x_ref = bf16[64,16,512]{2,1,0:T(8,128)(2,1)S(1)} async-done(((bf16[64,16,512]{2,1,0:T(8,128)(2,1)}), bf16[64,16,512]{2,1,0:T(8,128)(2,1)S(1)}, u32[]{:S(2)}, u32[]{:S(2)}) %all-to-all-start.4) | async-done | bytes 1048608 | tf_op jit(solution)/shard_map/all_to_all | solution.py:291
  233.8 2.3 last.1
  (24 shorter events, 0.1 us)
Async XLA Ops:
  29.9 11.4 %collective-permute-start = (bf16[32,104,128]{2,1,0:T(8,128)(2,1)S(1)}, bf16[32,104,128]{2,1,0:T(8,128)(2,1)S(1)}, u32[]{:S(2)}, u32[]{:S(2)}) collective-permute-start(bf16[32,104,128]{2,1,0:T(8,128)(2,1)S(1)} %all_gather.3.packed_ref), channel_id=1, source_target_pairs={{0,1},{1,0},{2,3},{3,2},{4,5},{5,4},{6,7},{7,6},{8,9},{9,8},{10,11... | collective-permute-start | bytes 2555912 | tf_op jit(solution)/shard_map/ppermute | solution.py:272
  38.0 0.9 copy-start.9
  38.9 2.4 %copy-start.6 = (f32[2,2,128]{2,1,0:T(2,128)S(1)}, f32[2,2,128]{2,1,0:T(2,128)}, u32[]{:S(2)}) copy-start(f32[2,2,128]{2,1,0:T(2,128)} %gain_ref.9) | copy-start | bytes 6148
  38.9 2.4 %copy-start.7 = (bf16[8,512,128]{2,1,0:T(8,128)(2,1)S(1)}, bf16[8,512,128]{2,1,0:T(8,128)(2,1)}, u32[]{:S(2)}) copy-start(bf16[8,512,128]{2,1,0:T(8,128)(2,1)} %pair_ref.1) | copy-start | bytes 3145732
  38.9 2.4 %copy-start.8 = (bf16[2,128,512]{2,1,0:T(8,128)(2,1)S(1)}, bf16[2,128,512]{2,1,0:T(8,128)(2,1)}, u32[]{:S(2)}) copy-start(bf16[2,128,512]{2,1,0:T(8,128)(2,1)} %proj_ref.3) | copy-start | bytes 786436
  38.9 2.5 %copy-start.10 = (bf16[128,384]{1,0:T(8,128)(2,1)S(1)}, bf16[128,384]{1,0:T(8,128)(2,1)}, u32[]{:S(2)}) copy-start(bf16[128,384]{1,0:T(8,128)(2,1)} %weight_ref.3) | copy-start | bytes 294916
  38.9 2.5 %copy-start.11 = (bf16[384,128]{1,0:T(8,128)(2,1)S(1)}, bf16[384,128]{1,0:T(8,128)(2,1)}, u32[]{:S(2)}) copy-start(bf16[384,128]{1,0:T(8,128)(2,1)} %wl_ref.1) | copy-start | bytes 294916
  38.9 2.5 %copy-start.12 = (bf16[384,128]{1,0:T(8,128)(2,1)S(1)}, bf16[384,128]{1,0:T(8,128)(2,1)}, u32[]{:S(2)}) copy-start(bf16[384,128]{1,0:T(8,128)(2,1)} %wr_ref.1) | copy-start | bytes 294916
  47.1 53.9 %copy-start = (bf16[8,128,512]{2,1,0:T(8,128)(2,1)}, bf16[8,128,512]{2,1,0:T(8,128)(2,1)S(1)}, u32[]{:S(2)}) copy-start(bf16[8,128,512]{2,1,0:T(8,128)(2,1)S(1)} %get-tuple-element.9.z_in) | copy-start | bytes 3145732
  101.1 8.6 %copy-start.4 = (bf16[2,128,128]{2,1,0:T(8,128)(2,1)S(1)}, bf16[2,128,128]{2,1,0:T(8,128)(2,1)}, u32[]{:S(2)}) copy-start(bf16[2,128,128]{2,1,0:T(8,128)(2,1)} %gate_ref.3) | copy-start | bytes 196612
  102.6 35.0 %all-to-all-start.2 = ((bf16[64,16,512]{2,1,0:T(8,128)(2,1)}), bf16[64,16,512]{2,1,0:T(8,128)(2,1)S(1)}, u32[]{:S(2)}, u32[]{:S(2)}) async-start(bf16[64,16,512]{2,1,0:T(8,128)(2,1)} %product0.1), calls=%async_computation.2 | async-start | bytes 2097152 | tf_op jit(solution)/shard_map/all_to_all | solution.py:291
  109.7 1.2 copy-start.1
  110.9 26.7 %copy-start.5 = (bf16[2,128,128]{2,1,0:T(8,128)(2,1)S(1)}, bf16[2,128,128]{2,1,0:T(8,128)(2,1)}, u32[]{:S(2)}) copy-start(bf16[2,128,128]{2,1,0:T(8,128)(2,1)} %out_ref.3) | copy-start | bytes 196612
  141.2 56.0 %copy-start.2 = (bf16[8,128,512]{2,1,0:T(8,128)(2,1)}, bf16[8,128,512]{2,1,0:T(8,128)(2,1)S(1)}, u32[]{:S(2)}) copy-start(bf16[8,128,512]{2,1,0:T(8,128)(2,1)S(1)} %get-tuple-element.11.z_in) | copy-start | bytes 3145732
  198.8 35.0 %all-to-all-start.4 = ((bf16[64,16,512]{2,1,0:T(8,128)(2,1)}), bf16[64,16,512]{2,1,0:T(8,128)(2,1)S(1)}, u32[]{:S(2)}, u32[]{:S(2)}) async-start(bf16[64,16,512]{2,1,0:T(8,128)(2,1)} %product1.1), calls=%async_computation.4 | async-start | bytes 2097152 | tf_op jit(solution)/shard_map/all_to_all | solution.py:291
  205.8 1.2 copy-start.3

commit v7 on v6

--- a/solution.py
+++ b/solution.py
@@ -38,6 +38,24 @@
     return centred * lax.rsqrt(variance + EPS) * gain
 
 
+def pack_kernel(feats_in, tok_in, out_ref, feats_ref, tok_ref, sem_feats, sem_tok):
+    copies = [
+        pltpu.make_async_copy(feats_in, feats_ref, sem_feats),
+        pltpu.make_async_copy(tok_in, tok_ref, sem_tok),
+    ]
+    for copy in copies:
+        copy.start()
+    for copy in copies:
+        copy.wait()
+    atoms, c = feats_ref.shape
+    tok = jnp.concatenate([tok_ref[...], jnp.zeros((1, c - atoms), jnp.int32)], axis=1)
+    row = lax.broadcasted_iota(jnp.int32, (CODES, c), 0)
+    codes = jnp.where(row == 0, tok >> 5, jnp.where(row == 1, tok & 31, 0))
+    block = jnp.concatenate([feats_ref[...], codes.astype(F32).astype(BF16)], axis=0)
+    for k in range(out_ref.shape[0]):
+        out_ref[k] = block
+
+
 def pool(packed_ref, weight_ref, tokens):
     blocks, rows, _ = packed_ref.shape
     atoms = rows - CODES
@@ -45,7 +63,7 @@
     total = None
     for at in range(0, blocks, some):
         feats = packed_ref[at : at + some, 0:atoms, :].reshape(some * atoms, -1)
-        hidden = jnp.maximum(mm(feats, weight_ref[...]), 0.0).astype(BF16)
+        hidden = jnp.maximum(mm(feats, weight_ref[...].astype(BF16)), 0.0).astype(BF16)
         hidden = jnp.concatenate([hidden, jnp.ones((some * atoms, 128), BF16)], axis=1)
         toks = []
         for k in range(at, at + some):
@@ -260,18 +278,21 @@
     ny, nx = 8, 4
     groups_y = [[(y * nx + x) * 2 + k for y in range(ny)] for x in range(nx) for k in range(2)]
     groups_x = [[(y * nx + x) * 2 + k for x in range(nx)] for y in range(ny) for k in range(2)]
-    tok = atom_token.reshape(1, atoms)
-    tok = jnp.concatenate([tok >> 5, tok & 31], axis=0).astype(BF16)
-    tok = jnp.pad(tok, ((0, CODES - 2), (0, c - atoms)))
-    packed = jnp.concatenate([atom_feats, tok], axis=0)
+    (packed,) = call(
+        pack_kernel, (shape((ny, atoms + CODES, c), BF16),), (atom_feats, atom_token.reshape(1, atoms)),
+        [pltpu.VMEM((atoms, c), BF16), pltpu.VMEM((1, atoms), jnp.int32)]
+        + [pltpu.SemaphoreType.DMA] * 2,
+        name="packed_atoms", bytes_=300_000, far_in=(0, 1), vmem=60,
+    )
     got = lax.all_to_all(
-        jnp.broadcast_to(packed[None], (ny,) + packed.shape), "dap", split_axis=0,
+        packed, "dap", split_axis=0,
         concat_axis=0, tiled=True, axis_index_groups=groups_y,
     )
+    got, weight = lax.optimization_barrier((got, atom_weight.astype(F32)))
     got = lax.all_gather(got, "dap", axis=0, tiled=True, axis_index_groups=groups_x)
     other = lax.ppermute(got, "dap", [(d, d ^ 1) for d in range(n)])
     (psum,) = call(
-        pool_kernel, (shape((tokens, cs + 128), F32),), (got, atom_weight),
+        pool_kernel, (shape((tokens, cs + 128), F32),), (got, weight),
         name="pool_half", flops=3_000_000_000, bytes_=2_000_000,
     )
     big = pltpu.VMEM((tokens // 128, rows * c, 128), F32)
@@ -281,7 +302,7 @@
     token_single, z, sent = call(
         first_kernel,
         (shape((rows, cs), BF16), z_shape, sent_shape),
-        (me, psum, other, atom_weight, left_weight, right_weight, pair_map,
+        (me, psum, other, weight, left_weight, right_weight, pair_map,
          tri_proj, tri_gains),
         [pltpu.VMEM((tokens, cs), F32), big, big, *held],
         name="first", flops=4_000_000_000, bytes_=8_000_000, far_out=(1,), vmem=32,

time: 237 us -> 236 us (level)
  blocking collectives: 138 us -> 121 us
  starting transfers between devices: 22.2 us -> 30.3 us
  waiting for transfers between devices: 50.9 us -> 58.8 us
    all_to_all x1 -> x0, blocking collectives: 16.2 us -> none  [local(): lax.all_to_all(jnp.broadcast_to(packed[None], (ny,) + packed.shape), 'dap...]
    all_to_all x0 -> x1, waiting for transfers between devices: none -> 7.95 us  [local(): lax.all_to_all(packed, 'dap', split_axis=0, concat_axis=0, tiled=True, ax...]
    all_to_all x0 -> x1, starting transfers between devices: none -> 7.66 us  [local(): lax.all_to_all(packed, 'dap', split_axis=0, concat_axis=0, tiled=True, ax...]
    pallas_call x8 -> x9, Pallas kernels: 19.7 us -> 21.4 us  [call(): pl.pallas_call(body, out_shape=outs, in_specs=specs, out_specs=places, sc...]
  transfers between devices with their start and end apart: 3 -> 4, of which waited for: 2 -> 3; matrix products, arithmetic and copies ran while one was open for 0% -> 0% of each run, Pallas kernels for 2% -> 2%
where the time goes in v7:
time: 236 us
  blocking collectives  121 us (51%)
  waiting for transfers between devices  58.8 us (25%)
  starting transfers between devices  30.3 us (13%)
  Pallas kernels  21.4 us (9%)
  local copies, waits for them, and re-layouts  2.48 us (1%)
    all_to_all x2, blocking collectives, exchange(): return lax.all_to_all(v, 'dap', split_axis=0, concat_axis=0, tiled=True)  109 us
    all_to_all x2, waiting for transfers between devices, exchange(): return lax.all_to_all(v, 'dap', split_axis=0, concat_axis=0, tiled=True)  50.8 us
    pallas_call x9, Pallas kernels, call(): pl.pallas_call(body, out_shape=outs, in_specs=specs, out_specs=places, sc...  21.4 us
    all_to_all x2, starting transfers between devices, exchange(): return lax.all_to_all(v, 'dap', split_axis=0, concat_axis=0, tiled=True)  14.1 us
    all_gather x1, blocking collectives, local(): lax.all_gather(got, 'dap', axis=0, tiled=True, axis_index_groups=groups_x)  11.6 us
    ppermute x1, starting transfers between devices, local(): other = lax.ppermute(got, 'dap', [(d, d ^ 1) for d in range(n)])  8.55 us
    all_to_all x1, waiting for transfers between devices, local(): lax.all_to_all(packed, 'dap', split_axis=0, concat_axis=0, tiled=True, ax...  7.95 us
    all_to_all x1, starting transfers between devices, local(): lax.all_to_all(packed, 'dap', split_axis=0, concat_axis=0, tiled=True, ax...  7.66 us
  transfers between devices with their start and end apart: 4, of which 3 were waited for; matrix products, arithmetic and copies ran while one was open for 0% of the time, Pallas kernels for 2%

profile of v7, /device:TPU:1, one launch (start us, length us, event | category | flops | bytes accessed | tf_op | source)
XLA Modules:
  0.0 235.7 jit_solution(12985411156092525404)
XLA Ops:
  0.6 1.5 packed_atoms.1
  2.1 7.7 %all-to-all-start = ((bf16[8,104,128]{2,1,0:T(8,128)(2,1)}), bf16[8,104,128]{2,1,0:T(8,128)(2,1)S(1)}, u32[]{:S(2)}, u32[]{:S(2)}) async-start(bf16[8,104,128]{2,1,0:T(8,128)(2,1)} %packed_atoms.1), calls=%async_computation | async-start | bytes 425984 | tf_op jit(solution)/shard_map/all_to_all | solution.py:287
  9.8 0.9 convert_element_type.3.weight_ref
  10.7 7.9 %all-to-all-done = bf16[8,104,128]{2,1,0:T(8,128)(2,1)S(1)} async-done(((bf16[8,104,128]{2,1,0:T(8,128)(2,1)}), bf16[8,104,128]{2,1,0:T(8,128)(2,1)S(1)}, u32[]{:S(2)}, u32[]{:S(2)}) %all-to-all-start) | async-done | bytes 213024 | tf_op jit(solution)/shard_map/all_to_all | solution.py:287
  18.6 11.6 %all_gather.3.packed_ref = bf16[32,104,128]{2,1,0:T(8,128)(2,1)S(1)} all-gather(bf16[8,104,128]{2,1,0:T(8,128)(2,1)S(1)} %all-to-all-done), channel_id=1, replica_groups={{0,2,4,6},{1,3,5,7},{8,10,12,14},{9,11,13,15},{16,18,20,22},{17,19,21,2..., dimensions={0}, use_global_device_ids=true | all-gather | bytes 1064960 | tf_op jit(solution)/shard_map/all_gather | solution.py:292
  30.2 8.5 %collective-permute-start = (bf16[32,104,128]{2,1,0:T(8,128)(2,1)S(1)}, bf16[32,104,128]{2,1,0:T(8,128)(2,1)S(1)}, u32[]{:S(2)}, u32[]{:S(2)}) collective-permute-start(bf16[32,104,128]{2,1,0:T(8,128)(2,1)S(1)} %all_gather.3.packed_ref), channel_id=1, source_target_pairs={{0,1},{1,0},{2,3},{3,2},{4,5},{5,4},{6,7},{7,6},{8,9},{9,8},{10,11... | collective-permute-start | bytes 2555912 | tf_op jit(solution)/shard_map/ppermute | solution.py:293
  38.7 0.0 copy-start.6
  38.8 0.0 copy-start.7
  38.8 2.4 %pool_half.1.psum_ref = f32[512,512]{1,0:T(8,128)S(1)} custom-call(bf16[32,104,128]{2,1,0:T(8,128)(2,1)S(1)} %all_gather.3.packed_ref, f32[128,384]{1,0:T(8,128)S(1)} %convert_element_type.3.weight_ref), custom_call_target="tpu_custom_call" | custom-call | flops 3000000000 | bytes 2000000 | tf_op jit(solution)/shard_map/pool_half/pallas_call | solution.py:255
  41.2 5.8 %first.1 = (bf16[8,384]{1,0:T(8,128)(2,1)}, bf16[8,128,512]{2,1,0:T(8,128)(2,1)S(1)}, bf16[64,32,512]{2,1,0:T(8,128)(2,1)S(1)}) custom-call(s32[1]{0:T(128)} %bitcast.idx_ref, f32[512,512]{1,0:T(8,128)S(1)} %pool_half.1.psum_ref, bf16[32,104,128]{2,1,0:T(8,128)(2,1)S(1)} %collective-permute-done.packed_ref, f32[128,384]{1,0:T(8,128)S(1)} %convert_element_type.3.weight_ref, ...), custom_call_target="tpu_custom_call" | custom-call | flops 4000000000 | bytes 8000000 | tf_op jit(solution)/shard_map/first/pallas_call | solution.py:255
  47.0 53.4 %all_to_all.25.v_ref = bf16[64,32,512]{2,1,0:T(8,128)(2,1)S(1)} all-to-all(bf16[64,32,512]{2,1,0:T(8,128)(2,1)S(1)} %get-tuple-element.12), channel_id=1, replica_groups=mesh['dp'=8,'dap'=64] {'dap'}, dimensions={0} | all-to-all | bytes 4194304 | tf_op jit(solution)/shard_map/all_to_all | solution.py:312
  100.4 1.6 product0.1
  102.0 7.0 %all-to-all-start.2 = ((bf16[64,16,512]{2,1,0:T(8,128)(2,1)}), bf16[64,16,512]{2,1,0:T(8,128)(2,1)S(1)}, u32[]{:S(2)}, u32[]{:S(2)}) async-start(bf16[64,16,512]{2,1,0:T(8,128)(2,1)} %product0.1), calls=%async_computation.2 | async-start | bytes 2097152 | tf_op jit(solution)/shard_map/all_to_all | solution.py:312
  109.1 1.2 copy-done.1
  110.3 1.3 gating0.1.held_ref
  111.6 25.4 %all-to-all-done.2.x_ref = bf16[64,16,512]{2,1,0:T(8,128)(2,1)S(1)} async-done(((bf16[64,16,512]{2,1,0:T(8,128)(2,1)}), bf16[64,16,512]{2,1,0:T(8,128)(2,1)S(1)}, u32[]{:S(2)}, u32[]{:S(2)}) %all-to-all-start.2) | async-done | bytes 1048608 | tf_op jit(solution)/shard_map/all_to_all | solution.py:312
  137.0 3.6 %middle.1 = (bf16[8,128,512]{2,1,0:T(8,128)(2,1)S(1)}, bf16[64,32,512]{2,1,0:T(8,128)(2,1)S(1)}) custom-call(bf16[64,16,512]{2,1,0:T(8,128)(2,1)S(1)} %all-to-all-done.2.x_ref, bf16[16,128,512]{2,1,0:T(8,128)(2,1)S(1)} %gating0.1.held_ref, bf16[2,128,128]{2,1,0:T(8,128)(2,1)S(1)} %copy-done.5, bf16[2,128,512]{2,1,0:T(8,128)(2,1)S(1)} %copy-done.8, ...), custom_call_target="tpu_custom_call" | custom-call | flops 1000000000 | bytes 8000000 | tf_op jit(solution)/shard_map/middle/pallas_call | solution.py:255
  140.7 55.9 %all_to_all.26.v_ref = bf16[64,32,512]{2,1,0:T(8,128)(2,1)S(1)} all-to-all(bf16[64,32,512]{2,1,0:T(8,128)(2,1)S(1)} %get-tuple-element.14), channel_id=1, replica_groups=mesh['dp'=8,'dap'=64] {'dap'}, dimensions={0} | all-to-all | bytes 4194304 | tf_op jit(solution)/shard_map/all_to_all | solution.py:312
  196.6 1.6 product1.1
  198.2 7.0 %all-to-all-start.4 = ((bf16[64,16,512]{2,1,0:T(8,128)(2,1)}), bf16[64,16,512]{2,1,0:T(8,128)(2,1)S(1)}, u32[]{:S(2)}, u32[]{:S(2)}) async-start(bf16[64,16,512]{2,1,0:T(8,128)(2,1)} %product1.1), calls=%async_computation.4 | async-start | bytes 2097152 | tf_op jit(solution)/shard_map/all_to_all | solution.py:312
  205.2 1.2 copy-done.3
  206.4 1.3 gating1.1.held_ref
  207.8 25.4 %all-to-all-done.4.x_ref = bf16[64,16,512]{2,1,0:T(8,128)(2,1)S(1)} async-done(((bf16[64,16,512]{2,1,0:T(8,128)(2,1)}), bf16[64,16,512]{2,1,0:T(8,128)(2,1)S(1)}, u32[]{:S(2)}, u32[]{:S(2)}) %all-to-all-start.4) | async-done | bytes 1048608 | tf_op jit(solution)/shard_map/all_to_all | solution.py:312
  233.2 2.4 %last.1 = bf16[8,512,128]{2,1,0:T(8,128)(2,1)} custom-call(bf16[64,16,512]{2,1,0:T(8,128)(2,1)S(1)} %all-to-all-done.4.x_ref, bf16[16,128,512]{2,1,0:T(8,128)(2,1)S(1)} %gating1.1.held_ref, bf16[2,128,128]{2,1,0:T(8,128)(2,1)S(1)} %copy-done.5, f32[2,2,128]{2,1,0:T(2,128)S(1)} %copy-done.6), custom_call_target="tpu_custom_call" | custom-call | flops 200000000 | bytes 5000000 | tf_op jit(solution)/shard_map/last/pallas_call | solution.py:255
  (19 shorter events, 0.0 us)
Async XLA Ops:
  2.1 16.5 %all-to-all-start = ((bf16[8,104,128]{2,1,0:T(8,128)(2,1)}), bf16[8,104,128]{2,1,0:T(8,128)(2,1)S(1)}, u32[]{:S(2)}, u32[]{:S(2)}) async-start(bf16[8,104,128]{2,1,0:T(8,128)(2,1)} %packed_atoms.1), calls=%async_computation | async-start | bytes 425984 | tf_op jit(solution)/shard_map/all_to_all | solution.py:287
  30.2 11.0 %collective-permute-start = (bf16[32,104,128]{2,1,0:T(8,128)(2,1)S(1)}, bf16[32,104,128]{2,1,0:T(8,128)(2,1)S(1)}, u32[]{:S(2)}, u32[]{:S(2)}) collective-permute-start(bf16[32,104,128]{2,1,0:T(8,128)(2,1)S(1)} %all_gather.3.packed_ref), channel_id=1, source_target_pairs={{0,1},{1,0},{2,3},{3,2},{4,5},{5,4},{6,7},{7,6},{8,9},{9,8},{10,11... | collective-permute-start | bytes 2555912 | tf_op jit(solution)/shard_map/ppermute | solution.py:293
  38.7 2.5 %copy-start.6 = (f32[2,2,128]{2,1,0:T(2,128)S(1)}, f32[2,2,128]{2,1,0:T(2,128)}, u32[]{:S(2)}) copy-start(f32[2,2,128]{2,1,0:T(2,128)} %gain_ref.9) | copy-start | bytes 6148
  38.8 2.5 %copy-start.7 = (bf16[8,512,128]{2,1,0:T(8,128)(2,1)S(1)}, bf16[8,512,128]{2,1,0:T(8,128)(2,1)}, u32[]{:S(2)}) copy-start(bf16[8,512,128]{2,1,0:T(8,128)(2,1)} %pair_ref.1) | copy-start | bytes 3145732
  38.8 2.4 %copy-start.8 = (bf16[2,128,512]{2,1,0:T(8,128)(2,1)S(1)}, bf16[2,128,512]{2,1,0:T(8,128)(2,1)}, u32[]{:S(2)}) copy-start(bf16[2,128,512]{2,1,0:T(8,128)(2,1)} %proj_ref.3) | copy-start | bytes 786436
  38.8 2.4 %copy-start.9 = (bf16[384,128]{1,0:T(8,128)(2,1)S(1)}, bf16[384,128]{1,0:T(8,128)(2,1)}, u32[]{:S(2)}) copy-start(bf16[384,128]{1,0:T(8,128)(2,1)} %wl_ref.1) | copy-start | bytes 294916
  38.8 2.4 %copy-start.10 = (bf16[384,128]{1,0:T(8,128)(2,1)S(1)}, bf16[384,128]{1,0:T(8,128)(2,1)}, u32[]{:S(2)}) copy-start(bf16[384,128]{1,0:T(8,128)(2,1)} %wr_ref.1) | copy-start | bytes 294916
  47.0 53.4 %copy-start = (bf16[8,128,512]{2,1,0:T(8,128)(2,1)}, bf16[8,128,512]{2,1,0:T(8,128)(2,1)S(1)}, u32[]{:S(2)}) copy-start(bf16[8,128,512]{2,1,0:T(8,128)(2,1)S(1)} %get-tuple-element.13.z_in) | copy-start | bytes 3145732
  100.4 8.6 %copy-start.4 = (bf16[2,128,128]{2,1,0:T(8,128)(2,1)S(1)}, bf16[2,128,128]{2,1,0:T(8,128)(2,1)}, u32[]{:S(2)}) copy-start(bf16[2,128,128]{2,1,0:T(8,128)(2,1)} %gate_ref.3) | copy-start | bytes 196612
  102.0 35.0 %all-to-all-start.2 = ((bf16[64,16,512]{2,1,0:T(8,128)(2,1)}), bf16[64,16,512]{2,1,0:T(8,128)(2,1)S(1)}, u32[]{:S(2)}, u32[]{:S(2)}) async-start(bf16[64,16,512]{2,1,0:T(8,128)(2,1)} %product0.1), calls=%async_computation.2 | async-start | bytes 2097152 | tf_op jit(solution)/shard_map/all_to_all | solution.py:312
  109.1 1.2 copy-start.1
  110.3 26.7 %copy-start.5 = (bf16[2,128,128]{2,1,0:T(8,128)(2,1)S(1)}, bf16[2,128,128]{2,1,0:T(8,128)(2,1)}, u32[]{:S(2)}) copy-start(bf16[2,128,128]{2,1,0:T(8,128)(2,1)} %out_ref.3) | copy-start | bytes 196612
  140.7 56.0 %copy-start.2 = (bf16[8,128,512]{2,1,0:T(8,128)(2,1)}, bf16[8,128,512]{2,1,0:T(8,128)(2,1)S(1)}, u32[]{:S(2)}) copy-start(bf16[8,128,512]{2,1,0:T(8,128)(2,1)S(1)} %get-tuple-element.15.z_in) | copy-start | bytes 3145732
  198.2 35.0 %all-to-all-start.4 = ((bf16[64,16,512]{2,1,0:T(8,128)(2,1)}), bf16[64,16,512]{2,1,0:T(8,128)(2,1)S(1)}, u32[]{:S(2)}, u32[]{:S(2)}) async-start(bf16[64,16,512]{2,1,0:T(8,128)(2,1)} %product1.1), calls=%async_computation.4 | async-start | bytes 2097152 | tf_op jit(solution)/shard_map/all_to_all | solution.py:312
  205.2 1.2 copy-start.3

commit v8 on v7

--- a/solution.py
+++ b/solution.py
@@ -122,9 +122,9 @@
     rows, tokens, c = pair_ref.shape
     cs = wl_ref.shape[0]
     total = psum_ref[...] + pool(packed_ref, weight_ref, tokens)
-    counts = total[:, cs:]
+    share = 1.0 / total[:, cs:]
     single = jnp.concatenate(
-        [total[:, at : at + 128] / counts for at in range(0, cs, 128)], axis=1
+        [total[:, at : at + 128] * share for at in range(0, cs, 128)], axis=1
     )
     ts_ref[...] = single
     right = mm(single.astype(BF16), wr_ref[...]).astype(BF16).astype(F32)

time: 236 us -> 236 us (level)
  no operation moved by 1% of the time
where the time goes in v8:
time: 236 us
  blocking collectives  121 us (51%)
  waiting for transfers between devices  58.8 us (25%)
  starting transfers between devices  30.3 us (13%)
  Pallas kernels  21.4 us (9%)
  local copies, waits for them, and re-layouts  2.48 us (1%)
    all_to_all x2, blocking collectives, exchange(): return lax.all_to_all(v, 'dap', split_axis=0, concat_axis=0, tiled=True)  109 us
    all_to_all x2, waiting for transfers between devices, exchange(): return lax.all_to_all(v, 'dap', split_axis=0, concat_axis=0, tiled=True)  50.8 us
    pallas_call x9, Pallas kernels, call(): pl.pallas_call(body, out_shape=outs, in_specs=specs, out_specs=places, sc...  21.4 us
    all_to_all x2, starting transfers between devices, exchange(): return lax.all_to_all(v, 'dap', split_axis=0, concat_axis=0, tiled=True)  14.1 us
    all_gather x1, blocking collectives, local(): lax.all_gather(got, 'dap', axis=0, tiled=True, axis_index_groups=groups_x)  11.6 us
    ppermute x1, starting transfers between devices, local(): other = lax.ppermute(got, 'dap', [(d, d ^ 1) for d in range(n)])  8.55 us
    all_to_all x1, waiting for transfers between devices, local(): lax.all_to_all(packed, 'dap', split_axis=0, concat_axis=0, tiled=True, ax...  7.95 us
    all_to_all x1, starting transfers between devices, local(): lax.all_to_all(packed, 'dap', split_axis=0, concat_axis=0, tiled=True, ax...  7.66 us
  transfers between devices with their start and end apart: 4, of which 3 were waited for; matrix products, arithmetic and copies ran while one was open for 0% of the time, Pallas kernels for 2%

profile of v8, /device:TPU:1, one launch (start us, length us, event | category | flops | bytes accessed | tf_op | source)
XLA Modules:
  0.0 235.7 jit_solution(12985411156092525404)
XLA Ops:
  0.6 1.5 packed_atoms.1
  2.1 7.7 %all-to-all-start = ((bf16[8,104,128]{2,1,0:T(8,128)(2,1)}), bf16[8,104,128]{2,1,0:T(8,128)(2,1)S(1)}, u32[]{:S(2)}, u32[]{:S(2)}) async-start(bf16[8,104,128]{2,1,0:T(8,128)(2,1)} %packed_atoms.1), calls=%async_computation | async-start | bytes 425984 | tf_op jit(solution)/shard_map/all_to_all | solution.py:287
  9.8 0.9 convert_element_type.3.weight_ref
  10.7 7.9 %all-to-all-done = bf16[8,104,128]{2,1,0:T(8,128)(2,1)S(1)} async-done(((bf16[8,104,128]{2,1,0:T(8,128)(2,1)}), bf16[8,104,128]{2,1,0:T(8,128)(2,1)S(1)}, u32[]{:S(2)}, u32[]{:S(2)}) %all-to-all-start) | async-done | bytes 213024 | tf_op jit(solution)/shard_map/all_to_all | solution.py:287
  18.6 11.6 %all_gather.3.packed_ref = bf16[32,104,128]{2,1,0:T(8,128)(2,1)S(1)} all-gather(bf16[8,104,128]{2,1,0:T(8,128)(2,1)S(1)} %all-to-all-done), channel_id=1, replica_groups={{0,2,4,6},{1,3,5,7},{8,10,12,14},{9,11,13,15},{16,18,20,22},{17,19,21,2..., dimensions={0}, use_global_device_ids=true | all-gather | bytes 1064960 | tf_op jit(solution)/shard_map/all_gather | solution.py:292
  30.2 8.5 %collective-permute-start = (bf16[32,104,128]{2,1,0:T(8,128)(2,1)S(1)}, bf16[32,104,128]{2,1,0:T(8,128)(2,1)S(1)}, u32[]{:S(2)}, u32[]{:S(2)}) collective-permute-start(bf16[32,104,128]{2,1,0:T(8,128)(2,1)S(1)} %all_gather.3.packed_ref), channel_id=1, source_target_pairs={{0,1},{1,0},{2,3},{3,2},{4,5},{5,4},{6,7},{7,6},{8,9},{9,8},{10,11... | collective-permute-start | bytes 2555912 | tf_op jit(solution)/shard_map/ppermute | solution.py:293
  38.7 0.0 copy-start.6
  38.8 0.0 copy-start.7
  38.8 2.4 %pool_half.1.psum_ref = f32[512,512]{1,0:T(8,128)S(1)} custom-call(bf16[32,104,128]{2,1,0:T(8,128)(2,1)S(1)} %all_gather.3.packed_ref, f32[128,384]{1,0:T(8,128)S(1)} %convert_element_type.3.weight_ref), custom_call_target="tpu_custom_call" | custom-call | flops 3000000000 | bytes 2000000 | tf_op jit(solution)/shard_map/pool_half/pallas_call | solution.py:255
  41.2 5.8 %first.1 = (bf16[8,384]{1,0:T(8,128)(2,1)}, bf16[8,128,512]{2,1,0:T(8,128)(2,1)S(1)}, bf16[64,32,512]{2,1,0:T(8,128)(2,1)S(1)}) custom-call(s32[1]{0:T(128)} %bitcast.idx_ref, f32[512,512]{1,0:T(8,128)S(1)} %pool_half.1.psum_ref, bf16[32,104,128]{2,1,0:T(8,128)(2,1)S(1)} %collective-permute-done.packed_ref, f32[128,384]{1,0:T(8,128)S(1)} %convert_element_type.3.weight_ref, ...), custom_call_target="tpu_custom_call" | custom-call | flops 4000000000 | bytes 8000000 | tf_op jit(solution)/shard_map/first/pallas_call | solution.py:255
  47.0 53.4 %all_to_all.25.v_ref = bf16[64,32,512]{2,1,0:T(8,128)(2,1)S(1)} all-to-all(bf16[64,32,512]{2,1,0:T(8,128)(2,1)S(1)} %get-tuple-element.12), channel_id=1, replica_groups=mesh['dp'=8,'dap'=64] {'dap'}, dimensions={0} | all-to-all | bytes 4194304 | tf_op jit(solution)/shard_map/all_to_all | solution.py:312
  100.4 1.6 product0.1
  102.0 7.0 %all-to-all-start.2 = ((bf16[64,16,512]{2,1,0:T(8,128)(2,1)}), bf16[64,16,512]{2,1,0:T(8,128)(2,1)S(1)}, u32[]{:S(2)}, u32[]{:S(2)}) async-start(bf16[64,16,512]{2,1,0:T(8,128)(2,1)} %product0.1), calls=%async_computation.2 | async-start | bytes 2097152 | tf_op jit(solution)/shard_map/all_to_all | solution.py:312
  109.1 1.2 copy-done.1
  110.3 1.3 gating0.1.held_ref
  111.6 25.4 %all-to-all-done.2.x_ref = bf16[64,16,512]{2,1,0:T(8,128)(2,1)S(1)} async-done(((bf16[64,16,512]{2,1,0:T(8,128)(2,1)}), bf16[64,16,512]{2,1,0:T(8,128)(2,1)S(1)}, u32[]{:S(2)}, u32[]{:S(2)}) %all-to-all-start.2) | async-done | bytes 1048608 | tf_op jit(solution)/shard_map/all_to_all | solution.py:312
  137.0 3.6 %middle.1 = (bf16[8,128,512]{2,1,0:T(8,128)(2,1)S(1)}, bf16[64,32,512]{2,1,0:T(8,128)(2,1)S(1)}) custom-call(bf16[64,16,512]{2,1,0:T(8,128)(2,1)S(1)} %all-to-all-done.2.x_ref, bf16[16,128,512]{2,1,0:T(8,128)(2,1)S(1)} %gating0.1.held_ref, bf16[2,128,128]{2,1,0:T(8,128)(2,1)S(1)} %copy-done.5, bf16[2,128,512]{2,1,0:T(8,128)(2,1)S(1)} %copy-done.8, ...), custom_call_target="tpu_custom_call" | custom-call | flops 1000000000 | bytes 8000000 | tf_op jit(solution)/shard_map/middle/pallas_call | solution.py:255
  140.7 55.9 %all_to_all.26.v_ref = bf16[64,32,512]{2,1,0:T(8,128)(2,1)S(1)} all-to-all(bf16[64,32,512]{2,1,0:T(8,128)(2,1)S(1)} %get-tuple-element.14), channel_id=1, replica_groups=mesh['dp'=8,'dap'=64] {'dap'}, dimensions={0} | all-to-all | bytes 4194304 | tf_op jit(solution)/shard_map/all_to_all | solution.py:312
  196.6 1.6 product1.1
  198.2 7.0 %all-to-all-start.4 = ((bf16[64,16,512]{2,1,0:T(8,128)(2,1)}), bf16[64,16,512]{2,1,0:T(8,128)(2,1)S(1)}, u32[]{:S(2)}, u32[]{:S(2)}) async-start(bf16[64,16,512]{2,1,0:T(8,128)(2,1)} %product1.1), calls=%async_computation.4 | async-start | bytes 2097152 | tf_op jit(solution)/shard_map/all_to_all | solution.py:312
  205.2 1.2 copy-done.3
  206.4 1.3 gating1.1.held_ref
  207.8 25.4 %all-to-all-done.4.x_ref = bf16[64,16,512]{2,1,0:T(8,128)(2,1)S(1)} async-done(((bf16[64,16,512]{2,1,0:T(8,128)(2,1)}), bf16[64,16,512]{2,1,0:T(8,128)(2,1)S(1)}, u32[]{:S(2)}, u32[]{:S(2)}) %all-to-all-start.4) | async-done | bytes 1048608 | tf_op jit(solution)/shard_map/all_to_all | solution.py:312
  233.2 2.4 %last.1 = bf16[8,512,128]{2,1,0:T(8,128)(2,1)} custom-call(bf16[64,16,512]{2,1,0:T(8,128)(2,1)S(1)} %all-to-all-done.4.x_ref, bf16[16,128,512]{2,1,0:T(8,128)(2,1)S(1)} %gating1.1.held_ref, bf16[2,128,128]{2,1,0:T(8,128)(2,1)S(1)} %copy-done.5, f32[2,2,128]{2,1,0:T(2,128)S(1)} %copy-done.6), custom_call_target="tpu_custom_call" | custom-call | flops 200000000 | bytes 5000000 | tf_op jit(solution)/shard_map/last/pallas_call | solution.py:255
  (19 shorter events, 0.0 us)
Async XLA Ops:
  2.1 16.5 %all-to-all-start = ((bf16[8,104,128]{2,1,0:T(8,128)(2,1)}), bf16[8,104,128]{2,1,0:T(8,128)(2,1)S(1)}, u32[]{:S(2)}, u32[]{:S(2)}) async-start(bf16[8,104,128]{2,1,0:T(8,128)(2,1)} %packed_atoms.1), calls=%async_computation | async-start | bytes 425984 | tf_op jit(solution)/shard_map/all_to_all | solution.py:287
  30.2 11.0 %collective-permute-start = (bf16[32,104,128]{2,1,0:T(8,128)(2,1)S(1)}, bf16[32,104,128]{2,1,0:T(8,128)(2,1)S(1)}, u32[]{:S(2)}, u32[]{:S(2)}) collective-permute-start(bf16[32,104,128]{2,1,0:T(8,128)(2,1)S(1)} %all_gather.3.packed_ref), channel_id=1, source_target_pairs={{0,1},{1,0},{2,3},{3,2},{4,5},{5,4},{6,7},{7,6},{8,9},{9,8},{10,11... | collective-permute-start | bytes 2555912 | tf_op jit(solution)/shard_map/ppermute | solution.py:293
  38.7 2.5 %copy-start.6 = (f32[2,2,128]{2,1,0:T(2,128)S(1)}, f32[2,2,128]{2,1,0:T(2,128)}, u32[]{:S(2)}) copy-start(f32[2,2,128]{2,1,0:T(2,128)} %gain_ref.9) | copy-start | bytes 6148
  38.8 2.5 %copy-start.7 = (bf16[8,512,128]{2,1,0:T(8,128)(2,1)S(1)}, bf16[8,512,128]{2,1,0:T(8,128)(2,1)}, u32[]{:S(2)}) copy-start(bf16[8,512,128]{2,1,0:T(8,128)(2,1)} %pair_ref.1) | copy-start | bytes 3145732
  38.8 2.4 %copy-start.8 = (bf16[2,128,512]{2,1,0:T(8,128)(2,1)S(1)}, bf16[2,128,512]{2,1,0:T(8,128)(2,1)}, u32[]{:S(2)}) copy-start(bf16[2,128,512]{2,1,0:T(8,128)(2,1)} %proj_ref.3) | copy-start | bytes 786436
  38.8 2.4 %copy-start.9 = (bf16[384,128]{1,0:T(8,128)(2,1)S(1)}, bf16[384,128]{1,0:T(8,128)(2,1)}, u32[]{:S(2)}) copy-start(bf16[384,128]{1,0:T(8,128)(2,1)} %wl_ref.1) | copy-start | bytes 294916
  38.8 2.4 %copy-start.10 = (bf16[384,128]{1,0:T(8,128)(2,1)S(1)}, bf16[384,128]{1,0:T(8,128)(2,1)}, u32[]{:S(2)}) copy-start(bf16[384,128]{1,0:T(8,128)(2,1)} %wr_ref.1) | copy-start | bytes 294916
  47.0 53.4 %copy-start = (bf16[8,128,512]{2,1,0:T(8,128)(2,1)}, bf16[8,128,512]{2,1,0:T(8,128)(2,1)S(1)}, u32[]{:S(2)}) copy-start(bf16[8,128,512]{2,1,0:T(8,128)(2,1)S(1)} %get-tuple-element.13.z_in) | copy-start | bytes 3145732
  100.4 8.6 %copy-start.4 = (bf16[2,128,128]{2,1,0:T(8,128)(2,1)S(1)}, bf16[2,128,128]{2,1,0:T(8,128)(2,1)}, u32[]{:S(2)}) copy-start(bf16[2,128,128]{2,1,0:T(8,128)(2,1)} %gate_ref.3) | copy-start | bytes 196612
  102.0 35.0 %all-to-all-start.2 = ((bf16[64,16,512]{2,1,0:T(8,128)(2,1)}), bf16[64,16,512]{2,1,0:T(8,128)(2,1)S(1)}, u32[]{:S(2)}, u32[]{:S(2)}) async-start(bf16[64,16,512]{2,1,0:T(8,128)(2,1)} %product0.1), calls=%async_computation.2 | async-start | bytes 2097152 | tf_op jit(solution)/shard_map/all_to_all | solution.py:312
  109.1 1.2 copy-start.1
  110.3 26.7 %copy-start.5 = (bf16[2,128,128]{2,1,0:T(8,128)(2,1)S(1)}, bf16[2,128,128]{2,1,0:T(8,128)(2,1)}, u32[]{:S(2)}) copy-start(bf16[2,128,128]{2,1,0:T(8,128)(2,1)} %out_ref.3) | copy-start | bytes 196612
  140.7 56.0 %copy-start.2 = (bf16[8,128,512]{2,1,0:T(8,128)(2,1)}, bf16[8,128,512]{2,1,0:T(8,128)(2,1)S(1)}, u32[]{:S(2)}) copy-start(bf16[8,128,512]{2,1,0:T(8,128)(2,1)S(1)} %get-tuple-element.15.z_in) | copy-start | bytes 3145732
  198.2 35.0 %all-to-all-start.4 = ((bf16[64,16,512]{2,1,0:T(8,128)(2,1)}), bf16[64,16,512]{2,1,0:T(8,128)(2,1)S(1)}, u32[]{:S(2)}, u32[]{:S(2)}) async-start(bf16[64,16,512]{2,1,0:T(8,128)(2,1)} %product1.1), calls=%async_computation.4 | async-start | bytes 2097152 | tf_op jit(solution)/shard_map/all_to_all | solution.py:312
  205.2 1.2 copy-start.3
